TPU v7x, 1024 devices: a whole 8x8x8 slice. The times are simulated.
1024 devices in a mesh: rep: 16 (over x, core), fsdp: 64 (over y, z).
Axes of the slice: x: 8, y: 8, z: 8, core: 2. Of those that a mesh axis runs over, the one named last changes fastest.
Arguments:
- partial_grads: bfloat16 [16, 192, 512, 512], P('rep', None, 'fsdp'), may hold values from -150 to 150
- block_owner: int32 [192], replicated, may hold values from 0 to 63, as said below
- block_slot: int32 [192], replicated, may hold values from 0 to 5, as said below
- left_roots: bfloat16 [384, 512, 512], P('fsdp'), may hold values from -1 to 2.5
- right_roots: bfloat16 [384, 512, 512], P('fsdp'), may hold values from -1 to 2.5
- momentum: float32 [192, 512, 512], P(None, 'fsdp', 'rep'), may hold values from -6 to 6
Outputs:
- new_momentum: float32 [192, 512, 512], P(None, 'fsdp', 'rep')
Inputs may be any that keep to these rules, and one draw needn't show every extreme that they name: `block_owner`: every owner index names at least one block and at most 6 blocks; some index names exactly 6. `block_slot`: blocks with the same owner have different slots.
All inputs are finite; a program needn't handle non-finite values.
Results may differ from a plain program's by a relative error of at most 0.017.
Values may be sent and summed in bfloat16 or wider, within the bound.
No kernel may reach another device: no remote copies, remote signals or barrier semaphores. Data moves between devices by JAX's collectives and lax.ppermute only.
A program may use at most 64 MiB of HBM per device.

v0:
```python
import jax
import jax.numpy as jnp
from jax import lax
from jax.sharding import PartitionSpec as P


def on_device(partial_grads, block_owner, block_slot, left_roots, right_roots, momentum):
    owner_count = lax.axis_size("fsdp")
    replicas = lax.axis_size("rep")
    blocks = partial_grads.shape[1]
    sliver_rows = partial_grads.shape[2]
    block_width = partial_grads.shape[3]
    slot_count = left_roots.shape[0]
    slice_cols = block_width // replicas
    block_area = float(block_width * block_width)
    entries = block_slot * owner_count + block_owner
    select = (
        entries[None, :] == lax.broadcasted_iota(jnp.int32, (slot_count * owner_count, blocks), 0)
    ).astype(jnp.bfloat16)
    summed = lax.psum_scatter(
        partial_grads[0].astype(jnp.float32).astype(jnp.bfloat16),
        "rep",
        scatter_dimension=2,
        tiled=True,
    )
    outgoing = jnp.dot(
        select, summed.reshape(blocks, sliver_rows * slice_cols), preferred_element_type=jnp.float32
    )
    outgoing = outgoing.astype(jnp.bfloat16).reshape(
        slot_count, owner_count, sliver_rows, slice_cols
    )
    arrived = lax.all_to_all(outgoing, "fsdp", split_axis=1, concat_axis=2, tiled=True)
    owned_cols = arrived.reshape(slot_count, owner_count * sliver_rows, slice_cols)
    start_col = lax.axis_index("rep") * slice_cols
    gathered = lax.all_gather(owned_cols, "rep", axis=2, tiled=True)
    right_prod = jnp.einsum(
        "srk,skc->src", gathered, right_roots, preferred_element_type=jnp.float32
    ).astype(jnp.bfloat16)
    precond = jnp.einsum("sik,skc->sic", left_roots, right_prod, preferred_element_type=jnp.float32)
    grad_squares = jnp.sum(jnp.square(gathered.astype(jnp.float32)), axis=(1, 2))
    precond_squares = jnp.sum(precond * precond, axis=(1, 2))
    own_precond = lax.dynamic_slice_in_dim(precond, start_col, slice_cols, 2)
    graft_scale = jnp.sqrt(grad_squares / block_area) / jnp.sqrt(
        precond_squares / block_area + 1e-06
    )
    grafted = (own_precond * graft_scale[:, None, None]).astype(jnp.bfloat16)
    outgoing_back = grafted.reshape(slot_count, owner_count, sliver_rows, slice_cols)
    returned_parts = lax.all_to_all(outgoing_back, "fsdp", split_axis=1, concat_axis=1, tiled=True)
    returned = jnp.dot(
        select.T,
        returned_parts.reshape(slot_count * owner_count, sliver_rows * slice_cols),
        preferred_element_type=jnp.float32,
    )
    returned = returned.reshape(blocks, sliver_rows, slice_cols)
    return 0.9 * momentum + 0.1 * returned


def solution(mesh):
    in_specs = (
        P("rep", None, "fsdp", None),
        P(),
        P(),
        P("fsdp", None, None),
        P("fsdp", None, None),
        P(None, "fsdp", "rep"),
    )
    out_specs = P(None, "fsdp", "rep")
    return jax.shard_map(
        on_device, mesh=mesh, in_specs=in_specs, out_specs=out_specs, check_vma=False
    )
```

profile of v0, /device:TPU:1, one launch (start us, length us, event | category | flops | bytes accessed | tf_op | source)
XLA Modules:
  0.0 220.6 jit_solution(3037853417874203859)
XLA Ops:
  6.5 0.0 copy-start
  6.5 0.0 copy-start.2
  6.5 0.0 copy-start.1
  6.5 0.0 reduce-scatter.2.cloned.1.call-start
  6.5 4.8 %copy.28 = bf16[1,192,8,512]{1,2,3,0:T(8,128)(2,1)} copy(bf16[1,192,8,512]{3,2,1,0:T(8,128)(2,1)} %param.6) | data formatting | bytes 3145728 | tf_op args[0]
  11.3 0.0 reduce-scatter.2.cloned.1.call-update
  11.4 0.0 all-gather.2.cloned.1.call-start
  11.4 0.0 copy-done.2
  11.4 0.0 copy-done.1
  11.4 76.1 %reduce-scatter.2.cloned.1.call-done = bf16[192,8,32]{0,1,2:T(8,128)(2,1)} async-done(((bf16[192,8,512]{0,1,2:T(8,128)(2,1)}), bf16[192,8,32]{0,1,2:T(8,128)(2,1)}) %reduce-scatter.2.cloned.1.call-update) | async-done | bytes 98320 | tf_op jit(solution)/shard_map/reduce_scatter | solution.py:20
  87.6 0.9 copy.29
  88.5 0.3 convolution_convert_fusion
  88.8 1.2 reshape.38
  90.0 2.2 copy.44
  92.2 1.7 reshape.39
  93.9 23.1 %all_to_all.14 = bf16[64,2,768]{2,1,0:T(2,128)(2,1)S(1)} all-to-all(bf16[64,2,768]{2,1,0:T(2,128)(2,1)S(1)} %reshape.39), channel_id=1, replica_groups=mesh['rep'=16,'fsdp'=64] {'fsdp'}, dimensions={0} | all-to-all | bytes 393216 | tf_op jit(solution)/shard_map/all_to_all | solution.py:32
  117.0 1.2 reshape.40
  118.2 2.2 copy_bitcast_fusion
  120.4 2.1 copy.33
  122.4 0.0 all-gather.2.cloned.1.call-update
  122.5 40.4 %all-gather.2.cloned.1.call-done = bf16[6,512,512]{1,2,0:T(8,128)(2,1)} async-done(((bf16[6,512,32]{1,2,0:T(8,128)(2,1)}), bf16[6,512,512]{1,2,0:T(8,128)(2,1)}) %all-gather.2.cloned.1.call-update) | async-done | bytes 3145744 | tf_op jit(solution)/shard_map/all_gather | solution.py:35
  162.8 2.7 %multiply_reduce_fusion.1 = f32[6]{0:T(128)S(1)} fusion(bf16[6,512,512]{1,2,0:T(8,128)(2,1)} %all-gather.2.cloned.1.call-done), kind=kLoop, calls=%fused_computation.1 | loop fusion | flops 4718586 | bytes 3145752 | tf_op jit(solution)/shard_map/reduce_sum | solution.py:40
  165.5 0.0 copy-done
  165.5 9.1 %multiply_reduce_fusion = (f32[6]{0:T(128)S(1)}, f32[6,512,512]{2,1,0:T(8,128)}) fusion(bf16[6,512,512]{2,1,0:T(8,128)(2,1)S(1)} %copy-done, bf16[6,512,512]{1,2,0:T(8,128)(2,1)} %all-gather.2.cloned.1.call-done, bf16[6,512,512]{2,1,0:T(8,128)(2,1)} %param.10), kind=kOutput, calls=%fused_computation | convolution fusion | flops 3225944064 | bytes 15728664 | tf_op jit(solution)/shard_map/sik,skc->sic/dot_general | solution.py:39
  174.7 1.1 fusion.8
  175.8 1.2 copy.35
  176.9 2.2 copy_bitcast_fusion.2
  179.1 1.7 reshape.41
  180.8 25.6 %all_to_all.15 = bf16[64,2,768]{2,1,0:T(2,128)(2,1)S(1)} all-to-all(bf16[64,2,768]{2,1,0:T(2,128)(2,1)S(1)} %reshape.41), channel_id=1, replica_groups=mesh['rep'=16,'fsdp'=64] {'fsdp'}, dimensions={0} | all-to-all | bytes 393216 | tf_op jit(solution)/shard_map/all_to_all | solution.py:48
  206.5 1.2 reshape.42
  207.7 2.7 %copy.37 = bf16[6,64,8,32]{1,0,3,2:T(8,128)(2,1)} copy(bf16[6,64,8,32]{3,2,0,1:T(8,128)(2,1)} %bitcast.33) | data formatting | bytes 393216 | tf_op jit(solution)/shard_map/all_to_all | solution.py:48
  210.4 1.4 reshape.36
  211.8 2.0 fusion.4
  (2 shorter events, 0.0 us)
Async XLA Ops:
  6.5 159.0 %copy-start = (bf16[6,512,512]{2,1,0:T(8,128)(2,1)S(1)}, bf16[6,512,512]{2,1,0:T(8,128)(2,1)}, u32[]{:S(2)}) copy-start(bf16[6,512,512]{2,1,0:T(8,128)(2,1)} %param.9) | copy-start | bytes 9437188
  6.5 4.9 %copy-start.2 = (s32[192]{0:T(256)S(1)}, s32[192]{0:T(256)}, u32[]{:S(2)}) copy-start(s32[192]{0:T(256)} %param.8) | copy-start | bytes 2308
  6.5 4.9 %copy-start.1 = (s32[192]{0:T(256)S(1)}, s32[192]{0:T(256)}, u32[]{:S(2)}) copy-start(s32[192]{0:T(256)} %param.7) | copy-start | bytes 2308
  6.5 81.0 %reduce-scatter.2.cloned.1.call-start = ((), (), s32[]{:S(2)}) async-start(), calls=%async_computation.3 | async-start | bytes 2228224 | tf_op jit(solution)/shard_map/reduce_scatter | solution.py:20
  11.4 151.5 %all-gather.2.cloned.1.call-start = ((), (), s32[]{:S(2)}) async-start(), calls=%async_computation.4 | async-start | bytes 3342336 | tf_op jit(solution)/shard_map/all_gather | solution.py:35
Sparse Core Ops, SparseCore 0:
  11.5 76.0 reduce-scatter.1
  122.6 40.2 all-gather.1
where the time goes:
time: 222 us; the launch traced here: 221 us
  waiting for transfers between devices  117 us (53%)
  blocking collectives  48.7 us (22%)
  local copies, waits for them, and re-layouts  26.6 us (12%)
  between operations  13.5 us (6%)
  matrix products  11.4 us (5%)
  other arithmetic  3.82 us (2%)
    reduce_scatter x1, waiting for transfers between devices, on_device(): lax.psum_scatter(partial_grads[0].astype(jnp.float32).astype(jnp.bfloat16...  76.1 us
    all_gather x1, waiting for transfers between devices, on_device(): gathered = lax.all_gather(owned_cols, 'rep', axis=2, tiled=True)  40.4 us
    all_to_all x1, blocking collectives, on_device(): lax.all_to_all(outgoing_back, 'fsdp', split_axis=1, concat_axis=1, tiled=...  25.6 us
    all_to_all x1, blocking collectives, on_device(): lax.all_to_all(outgoing, 'fsdp', split_axis=1, concat_axis=2, tiled=True)  23.1 us
    unnamed x12, local copies, waits for them, and re-layouts  12.9 us
    dot_general x1, matrix products, on_device(): jnp.einsum('sik,skc->sic', left_roots, right_prod, preferred_element_type...  9.12 us
  transfers between devices with their start and end apart: 2, of which 2 were waited for; matrix products, arithmetic and copies ran while one was open for 0% of the time, Pallas kernels for 0%

commit v1 on v0

v1 whole, which is shorter than its diff:
```python
import functools

import jax
import jax.numpy as jnp
from jax import lax
from jax.experimental import pallas as pl
from jax.experimental.pallas import tpu as pltpu
from jax.sharding import Mesh, PartitionSpec as P

LANES = 128
VMEM = pl.BlockSpec(memory_space=pltpu.VMEM)
SMEM = pl.BlockSpec(memory_space=pltpu.SMEM)


def pair_sum_kernel(core_ref, place_ref, own_ref, other_ref, out_ref):
    del core_ref
    blocks = other_ref.shape[0]

    def body(b, carry):
        total = own_ref[b].astype(jnp.float32) + other_ref[b].astype(jnp.float32)
        out_ref[place_ref[b]] = total.astype(out_ref.dtype)
        return carry

    lax.fori_loop(0, blocks, body, 0, unroll=8)


def pair_sum(core, place, grads, other):
    blocks, rows, width = other.shape
    return pl.pallas_call(
        pair_sum_kernel,
        out_shape=jax.ShapeDtypeStruct(other.shape, other.dtype),
        grid_spec=pltpu.PrefetchScalarGridSpec(
            num_scalar_prefetch=2,
            grid=(1,),
            in_specs=[
                pl.BlockSpec((blocks, rows, width), lambda i, core, place: (core[0], 0, 0)),
                pl.BlockSpec((blocks, rows, width), lambda i, core, place: (0, 0, 0)),
            ],
            out_specs=pl.BlockSpec((blocks, rows, width), lambda i, core, place: (0, 0, 0)),
        ),
        compiler_params=pltpu.CompilerParams(vmem_limit_bytes=32 * 2**20),
        name="pair_sum",
    )(core, place, grads, other)


def sum_to_owner_kernel(owner_ref, parts_ref, out_ref):
    out_ref[...] = jnp.zeros_like(out_ref)
    for j in range(parts_ref.shape[1]):
        total = parts_ref[0, j].astype(jnp.float32)
        for i in range(1, parts_ref.shape[0]):
            total = total + parts_ref[i, j].astype(jnp.float32)
        out_ref[owner_ref[j]] = total.astype(out_ref.dtype)


def sum_to_owner(owner, parts, owner_count):
    return pl.pallas_call(
        sum_to_owner_kernel,
        out_shape=jax.ShapeDtypeStruct((owner_count,) + parts.shape[2:], parts.dtype),
        in_specs=[SMEM, VMEM],
        out_specs=VMEM,
        compiler_params=pltpu.CompilerParams(vmem_limit_bytes=32 * 2**20),
        name="sum_to_owner",
    )(owner, parts)


def precondition_kernel(slot_ref, grad_ref, left_ref, right_ref, out_ref):
    del slot_ref
    size = left_ref.shape[-1]
    grad = grad_ref[...].reshape(size, size)
    right_prod = jnp.dot(grad, right_ref[0], preferred_element_type=jnp.float32)
    precond = jnp.dot(
        left_ref[0], right_prod.astype(jnp.bfloat16), preferred_element_type=jnp.float32
    )
    grad_float = grad.astype(jnp.float32)
    area = float(size * size)
    grad_mean = jnp.sum(grad_float * grad_float, keepdims=True) / area
    precond_mean = jnp.sum(precond * precond, keepdims=True) / area
    scale = jnp.sqrt(grad_mean) / jnp.sqrt(precond_mean + 1e-06)
    out_ref[...] = (precond * scale).astype(out_ref.dtype).reshape(out_ref.shape)


def precondition(slot, grad, left_roots, right_roots):
    size = left_roots.shape[-1]
    whole = pl.BlockSpec(grad.shape, lambda i, slot: (0, 0, 0))
    factor = pl.BlockSpec((1, size, size), lambda i, slot: (slot[0], 0, 0))
    return pl.pallas_call(
        precondition_kernel,
        out_shape=jax.ShapeDtypeStruct(grad.shape, grad.dtype),
        grid_spec=pltpu.PrefetchScalarGridSpec(
            num_scalar_prefetch=1,
            grid=(1,),
            in_specs=[whole, factor, factor],
            out_specs=whole,
        ),
        compiler_params=pltpu.CompilerParams(vmem_limit_bytes=32 * 2**20),
        name="precondition",
    )(slot, grad, left_roots, right_roots)


def split_columns_kernel(owner_ref, rows_ref, out_ref):
    replicas, groups, rows, lanes = out_ref.shape
    width = rows_ref.shape[-1] // replicas
    per = lanes // width
    lane = lax.broadcasted_iota(jnp.int32, (rows, lanes), 1) // width
    for g in range(groups):
        blocks = [rows_ref[owner_ref[g * per + i]].astype(jnp.float32) for i in range(per)]
        for t in range(replicas // per):
            tiles = [block[:, t * lanes : (t + 1) * lanes] for block in blocks]
            for k in range(per):
                mixed = tiles[k]
                for i in range(per):
                    if i != k:
                        moved = pltpu.roll(tiles[i], ((i - k) % per) * width, 1)
                        mixed = jnp.where(lane == i, moved, mixed)
                out_ref[t * per + k, g] = mixed.astype(out_ref.dtype)


def split_columns(owner, rows, replicas):
    count = owner.shape[0]
    width = rows.shape[-1] // replicas
    per = LANES // width
    shape = (replicas, count // per, rows.shape[1], LANES)
    return pl.pallas_call(
        split_columns_kernel,
        out_shape=jax.ShapeDtypeStruct(shape, rows.dtype),
        in_specs=[SMEM, VMEM],
        out_specs=VMEM,
        compiler_params=pltpu.CompilerParams(vmem_limit_bytes=32 * 2**20),
        name="split_columns",
    )(owner, rows)


def update_kernel(place_ref, momentum_ref, pieces_ref, out_ref, block_ref):
    replicas, groups, _, lanes = pieces_ref.shape
    width = momentum_ref.shape[-1]
    per = lanes // width
    count = place_ref.shape[0]
    half = count // 2

    def invert(b, carry):
        block_ref[place_ref[b]] = b
        return carry

    lax.fori_loop(0, count, invert, 0, unroll=8)
    del half

    def body(r, carry):
        for g in range(groups):
            tile = pieces_ref[r, g].astype(jnp.float32)
            for i in range(per):
                piece = tile if i == 0 else pltpu.roll(tile, lanes - i * width, 1)
                b = block_ref[r * (groups * per) + g * per + i]
                out_ref[b] = 0.9 * momentum_ref[b] + 0.1 * piece[:, :width]
        return carry

    lax.fori_loop(0, replicas, body, 0, unroll=2)


def update(place, momentum, pieces):
    return pl.pallas_call(
        update_kernel,
        out_shape=jax.ShapeDtypeStruct(momentum.shape, momentum.dtype),
        in_specs=[SMEM, VMEM, VMEM],
        out_specs=VMEM,
        scratch_shapes=[pltpu.SMEM(place.shape, jnp.int32)],
        compiler_params=pltpu.CompilerParams(vmem_limit_bytes=32 * 2**20),
        name="update",
    )(place, momentum, pieces)


def on_device(partial_grads, block_owner, block_slot, left_roots, right_roots, momentum):
    owner_count = lax.axis_size("y") * lax.axis_size("z")
    planes = lax.axis_size("x")
    cores = lax.axis_size("core")
    replicas = planes * cores
    most = left_roots.shape[0]
    blocks, rows, width = partial_grads.shape[1:]
    half = blocks // cores
    each = half // planes
    core = lax.axis_index("core")
    plane = lax.axis_index("x")
    me = lax.axis_index(("y", "z"))
    grads = partial_grads[0]

    away = lax.dynamic_slice_in_dim(grads, (1 - core) * half, half, 0)
    other = lax.ppermute(away, "core", [(i, 1 - i) for i in range(cores)])

    owner = block_owner.reshape(cores, half)
    slot = block_slot.reshape(cores, half)
    entry = owner * most + slot
    rank = jnp.sum((entry[:, None, :] < entry[:, :, None]).astype(jnp.int32), axis=2)
    block_plane = rank % planes
    block_turn = rank // planes
    place = block_plane * each + block_turn
    own = lax.broadcasted_iota(jnp.int32, (cores, half), 0) == core
    mine = own & (block_plane == plane)
    turn_is = mine[None] & (
        block_turn[None] == lax.broadcasted_iota(jnp.int32, (each, cores, half), 0)
    )
    my_owner = jnp.sum(jnp.where(turn_is, owner[None], 0), axis=(1, 2))
    my_slot = jnp.sum(jnp.where(mine & (owner == me), slot, 0)).reshape(1)
    my_place = jnp.sum(jnp.where(own, place, 0), axis=0)
    piece_place = (
        (block_plane * cores + lax.broadcasted_iota(jnp.int32, (cores, half), 0)) * each
        + block_turn
    ).reshape(blocks)

    summed = pair_sum(core.reshape(1), my_place, grads, other)
    parts = lax.all_to_all(
        summed.reshape(planes, each, rows, width), "x", split_axis=0, concat_axis=0, tiled=True
    )
    to_owner = sum_to_owner(my_owner, parts, owner_count)
    grad = lax.all_to_all(to_owner, ("y", "z"), split_axis=0, concat_axis=0, tiled=True)
    grafted = precondition(my_slot, grad, left_roots, right_roots)
    back = lax.all_to_all(grafted, ("y", "z"), split_axis=0, concat_axis=0, tiled=True)
    pieces = split_columns(my_owner, back, replicas)
    pieces = lax.all_to_all(pieces, ("x", "core"), split_axis=0, concat_axis=0, tiled=True)
    return update(piece_place, momentum, pieces)


def solution(mesh):
    devices = mesh.devices.reshape(8, 2, 8, 8)
    split = Mesh(devices, ("x", "core", "y", "z"))
    rep, fsdp = ("x", "core"), ("y", "z")
    in_specs = (
        P(rep, None, fsdp, None),
        P(),
        P(),
        P(fsdp, None, None),
        P(fsdp, None, None),
        P(None, fsdp, rep),
    )
    out_specs = P(None, fsdp, rep)
    return jax.shard_map(
        on_device, mesh=split, in_specs=in_specs, out_specs=out_specs, check_vma=False
    )
```

time: 222 us -> 131 us (0.59)
  waiting for transfers between devices: 117 us -> 47 us
  starting transfers between devices: 0.04 us -> 40.2 us
  blocking collectives: 48.7 us -> 23.9 us
  local copies, waits for them, and re-layouts: 26.6 us -> 9.61 us
  between operations: 13.5 us -> 0.08 us
  matrix products: 11.4 us -> 0 us
  Pallas kernels: 0 us -> 7.89 us
  other arithmetic: 3.82 us -> 1.31 us
    reduce_scatter x1 -> x0, waiting for transfers between devices: 76.1 us -> none  [on_device(): lax.psum_scatter(partial_grads[0].astype(jnp.float32).astype(jnp.bfloat16...]
    all_to_all x0 -> x3, waiting for transfers between devices: none -> 46.9 us  [the longest x1 23.2 us: on_device(): lax.all_to_all(summed.reshape(planes, each, rows, width), 'x', split_axis...]
    all_gather x1 -> x0, waiting for transfers between devices: 40.4 us -> none  [on_device(): gathered = lax.all_gather(owned_cols, 'rep', axis=2, tiled=True)]
    all_to_all x2 -> x1, blocking collectives: 48.7 us -> 23.9 us  [on_device(): lax.all_to_all(grafted, ('y', 'z'), split_axis=0, concat_axis=0, tiled=True)]
    all_to_all x0 -> x3, starting transfers between devices: none -> 24.2 us  [the longest x1 13.4 us: on_device(): lax.all_to_all(to_owner, ('y', 'z'), split_axis=0, concat_axis=0, tiled=T...]
    ppermute x0 -> x1, starting transfers between devices: none -> 16.1 us  [on_device(): other = lax.ppermute(away, 'core', [(i, 1 - i) for i in range(cores)])]
    dot_general x3 -> x0, matrix products: 11.4 us -> none  [the longest x1 9.12 us: on_device(): jnp.einsum('sik,skc->sic', left_roots, right_prod, preferred_element_type...]
    pallas_call x0 -> x5, Pallas kernels: none -> 7.89 us  [the longest x1 1.86 us: precondition(): pl.pallas_call(precondition_kernel, out_shape=jax.ShapeDtypeStruct(grad.s...]
  transfers between devices with their start and end apart: 2 -> 4, of which waited for: 2 -> 4; matrix products, arithmetic and copies ran while one was open for 0% -> 3% of each run, Pallas kernels for 0% -> 0%
where the time goes in v1:
time: 131 us; the launch traced here: 130 us
  waiting for transfers between devices  47 us (36%)
  starting transfers between devices  40.2 us (31%)
  blocking collectives  23.9 us (18%)
  local copies, waits for them, and re-layouts  9.61 us (7%)
  Pallas kernels  7.89 us (6%)
  other arithmetic  1.31 us (1%)
    all_to_all x1, blocking collectives, on_device(): lax.all_to_all(grafted, ('y', 'z'), split_axis=0, concat_axis=0, tiled=True)  23.9 us
    all_to_all x1, waiting for transfers between devices, on_device(): lax.all_to_all(summed.reshape(planes, each, rows, width), 'x', split_axis...  23.2 us
    ppermute x1, starting transfers between devices, on_device(): other = lax.ppermute(away, 'core', [(i, 1 - i) for i in range(cores)])  16.1 us
    all_to_all x1, waiting for transfers between devices, on_device(): lax.all_to_all(to_owner, ('y', 'z'), split_axis=0, concat_axis=0, tiled=T...  15.5 us
    all_to_all x1, starting transfers between devices, on_device(): lax.all_to_all(to_owner, ('y', 'z'), split_axis=0, concat_axis=0, tiled=T...  13.4 us
    all_to_all x1, waiting for transfers between devices, on_device(): lax.all_to_all(pieces, ('x', 'core'), split_axis=0, concat_axis=0, tiled=...  8.18 us
    all_to_all x1, starting transfers between devices, on_device(): lax.all_to_all(pieces, ('x', 'core'), split_axis=0, concat_axis=0, tiled=...  7.19 us
    unnamed x13, local copies, waits for them, and re-layouts  5.52 us
  transfers between devices with their start and end apart: 4, of which 4 were waited for; matrix products, arithmetic and copies ran while one was open for 3% of the time, Pallas kernels for 0%

profile of v1, /device:TPU:1, one launch (start us, length us, event | category | flops | bytes accessed | tf_op | source)
XLA Modules:
  0.0 130.0 jit_solution(9988397515210355422)
XLA Ops:
  0.0 1.2 dynamic-slice_bitcast_fusion
  1.2 16.1 %collective-permute-start = (bf16[96,8,512]{2,1,0:T(8,128)(2,1)S(1)}, bf16[96,8,512]{2,1,0:T(8,128)(2,1)S(1)}, u32[]{:S(2)}, u32[]{:S(2)}) collective-permute-start(bf16[96,8,512]{2,1,0:T(8,128)(2,1)S(1)} %dynamic-slice_bitcast_fusion), channel_id=1, source_target_pairs={{0,64},{64,0},{1,65},{65,1},{2,66},{66,2},{3,67},{67,3},{4,68},{68... | collective-permute-start | bytes 2359304 | tf_op jit(solution)/shard_map/ppermute | solution.py:186
  17.3 0.8 reshape.83
  18.0 0.8 reshape.84
  18.8 0.2 convert_reduce_fusion
  19.0 0.1 select_reduce_fusion
  19.1 0.1 collective-permute-done.other_ref
  19.1 0.0 copy-start
  19.2 1.4 %copy-done = bf16[1,192,8,512]{3,2,1,0:T(8,128)(2,1)S(1)} copy-done((bf16[1,192,8,512]{3,2,1,0:T(8,128)(2,1)S(1)}, bf16[1,192,8,512]{3,2,1,0:T(8,128)(2,1)}, u32[]{:S(2)}) %copy-start) | copy-done | bytes 1572888
  20.6 0.0 copy-start.4
  20.6 0.0 copy-start.5
  20.6 1.7 %pair_sum.1 = bf16[96,8,512]{2,1,0:T(8,128)(2,1)} custom-call(s32[1]{0:T(128)} %bitcast.1.core_ref, s32[96]{0:T(128)S(1)} %get-tuple-element.5.place_ref, bf16[192,8,512]{2,1,0:T(8,128)(2,1)S(1)} %bitcast.6, bf16[96,8,512]{2,1,0:T(8,128)(2,1)S(1)} %collective-permute-done.other_ref), custom_call_target="tpu_custom_call" | custom-call | tf_op jit(solution)/shard_map/pair_sum/pallas_call | solution.py:29
  22.2 3.5 %all-to-all-start = ((bf16[8,12,8,512]{3,2,1,0:T(8,128)(2,1)}), bf16[8,12,8,512]{3,2,1,0:T(8,128)(2,1)S(1)}, u32[]{:S(2)}, u32[]{:S(2)}) async-start(bf16[8,12,8,512]{3,2,1,0:T(8,128)(2,1)} %bitcast.4), calls=%async_computation | async-start | bytes 1572864 | tf_op jit(solution)/shard_map/all_to_all | solution.py:209
  25.8 0.1 compare_and_fusion
  25.9 0.3 fusion.owner_ref
  26.2 23.2 %all-to-all-done.parts_ref = bf16[8,12,8,512]{3,2,1,0:T(8,128)(2,1)S(1)} async-done(((bf16[8,12,8,512]{3,2,1,0:T(8,128)(2,1)}), bf16[8,12,8,512]{3,2,1,0:T(8,128)(2,1)S(1)}, u32[]{:S(2)}, u32[]{:S(2)}) %all-to-all-start) | async-done | bytes 786464 | tf_op jit(solution)/shard_map/all_to_all | solution.py:209
  49.3 1.5 %sum_to_owner.1 = bf16[64,8,512]{2,1,0:T(8,128)(2,1)} custom-call(s32[12]{0:T(128)S(1)} %fusion.owner_ref, bf16[8,12,8,512]{3,2,1,0:T(8,128)(2,1)S(1)} %all-to-all-done.parts_ref), custom_call_target="tpu_custom_call" | custom-call | tf_op jit(solution)/shard_map/sum_to_owner/pallas_call | solution.py:56
  50.8 13.4 %all-to-all-start.1 = ((bf16[64,8,512]{2,1,0:T(8,128)(2,1)}), bf16[64,8,512]{2,1,0:T(8,128)(2,1)S(1)}, u32[]{:S(2)}, u32[]{:S(2)}) async-start(bf16[64,8,512]{2,1,0:T(8,128)(2,1)} %sum_to_owner.1), calls=%async_computation.1 | async-start | bytes 1048576 | tf_op jit(solution)/shard_map/all_to_all | solution.py:213
  64.2 0.1 reduce_sum.39
  64.3 0.1 iota.23
  64.4 0.1 iota.25
  64.5 0.1 iota.21
  64.6 0.0 copy-done.4
  64.6 0.0 copy-done.5
  64.6 0.6 fusion.2
  65.2 15.5 %all-to-all-done.1.grad_ref = bf16[64,8,512]{2,1,0:T(8,128)(2,1)S(1)} async-done(((bf16[64,8,512]{2,1,0:T(8,128)(2,1)}), bf16[64,8,512]{2,1,0:T(8,128)(2,1)S(1)}, u32[]{:S(2)}, u32[]{:S(2)}) %all-to-all-start.1) | async-done | bytes 524320 | tf_op jit(solution)/shard_map/all_to_all | solution.py:213
  80.7 0.0 copy-start.1
  80.7 1.9 %copy-done.1 = bf16[6,512,512]{2,1,0:T(8,128)(2,1)S(1)} copy-done((bf16[6,512,512]{2,1,0:T(8,128)(2,1)S(1)}, bf16[6,512,512]{2,1,0:T(8,128)(2,1)}, u32[]{:S(2)}) %copy-start.1) | copy-done | bytes 3145752
  82.6 0.0 copy-start.2
  82.6 1.9 %copy-done.2 = bf16[6,512,512]{2,1,0:T(8,128)(2,1)S(1)} copy-done((bf16[6,512,512]{2,1,0:T(8,128)(2,1)S(1)}, bf16[6,512,512]{2,1,0:T(8,128)(2,1)}, u32[]{:S(2)}) %copy-start.2) | copy-done | bytes 3145752
  84.5 0.0 copy-start.3
  84.5 1.9 %precondition.1 = bf16[64,8,512]{2,1,0:T(8,128)(2,1)S(1)} custom-call(s32[1]{0:T(128)} %bitcast.slot_ref, bf16[64,8,512]{2,1,0:T(8,128)(2,1)S(1)} %all-to-all-done.1.grad_ref, bf16[6,512,512]{2,1,0:T(8,128)(2,1)S(1)} %copy-done.1, bf16[6,512,512]{2,1,0:T(8,128)(2,1)S(1)} %copy-done.2), custom_call_target="tpu_custom_call" | custom-call | tf_op jit(solution)/shard_map/precondition/pallas_call | solution.py:86
  86.4 23.9 %all_to_all.20.rows_ref = bf16[64,8,512]{2,1,0:T(8,128)(2,1)S(1)} all-to-all(bf16[64,8,512]{2,1,0:T(8,128)(2,1)S(1)} %precondition.1), channel_id=1, replica_groups=mesh['x'=8,'core'=2,'y'=8,'z'=8] {'y','z'}, dimensions={0} | all-to-all | bytes 1048576 | tf_op jit(solution)/shard_map/all_to_all | solution.py:215
  110.3 1.3 %split_columns.1 = bf16[16,3,8,128]{3,2,1,0:T(8,128)(2,1)} custom-call(s32[12]{0:T(128)S(1)} %fusion.owner_ref, bf16[64,8,512]{2,1,0:T(8,128)(2,1)S(1)} %all_to_all.20.rows_ref), custom_call_target="tpu_custom_call" | custom-call | tf_op jit(solution)/shard_map/split_columns/pallas_call | solution.py:123
  111.6 7.2 %all-to-all-start.3 = ((bf16[16,3,8,128]{3,2,1,0:T(8,128)(2,1)}), bf16[16,3,8,128]{3,2,1,0:T(8,128)(2,1)S(1)}, u32[]{:S(2)}, u32[]{:S(2)}) async-start(bf16[16,3,8,128]{3,2,1,0:T(8,128)(2,1)} %split_columns.1), calls=%async_computation.3 | async-start | bytes 196608 | tf_op jit(solution)/shard_map/all_to_all | solution.py:217
  118.8 0.0 copy-done.3
  118.8 0.3 copy.9.momentum_ref
  119.1 8.2 %all-to-all-done.3.pieces_ref = bf16[16,3,8,128]{3,2,1,0:T(8,128)(2,1)S(1)} async-done(((bf16[16,3,8,128]{3,2,1,0:T(8,128)(2,1)}), bf16[16,3,8,128]{3,2,1,0:T(8,128)(2,1)S(1)}, u32[]{:S(2)}, u32[]{:S(2)}) %all-to-all-start.3) | async-done | bytes 98336 | tf_op jit(solution)/shard_map/all_to_all | solution.py:217
  127.3 1.6 %update.1 = f32[192,8,32]{2,1,0:T(8,128)S(1)} custom-call(s32[192]{0:T(256)S(1)} %get-tuple-element.8.place_ref, f32[192,8,32]{2,1,0:T(8,128)S(1)} %copy.9.momentum_ref, bf16[16,3,8,128]{3,2,1,0:T(8,128)(2,1)S(1)} %all-to-all-done.3.pieces_ref), custom_call_target="tpu_custom_call" | custom-call | tf_op jit(solution)/shard_map/update/pallas_call | solution.py:160
  128.9 1.1 copy.10
  (3 shorter events, 0.0 us)
Async XLA Ops:
  1.2 18.0 %collective-permute-start = (bf16[96,8,512]{2,1,0:T(8,128)(2,1)S(1)}, bf16[96,8,512]{2,1,0:T(8,128)(2,1)S(1)}, u32[]{:S(2)}, u32[]{:S(2)}) collective-permute-start(bf16[96,8,512]{2,1,0:T(8,128)(2,1)S(1)} %dynamic-slice_bitcast_fusion), channel_id=1, source_target_pairs={{0,64},{64,0},{1,65},{65,1},{2,66},{66,2},{3,67},{67,3},{4,68},{68... | collective-permute-start | bytes 2359304 | tf_op jit(solution)/shard_map/ppermute | solution.py:186
  19.1 1.4 %copy-start = (bf16[1,192,8,512]{3,2,1,0:T(8,128)(2,1)S(1)}, bf16[1,192,8,512]{3,2,1,0:T(8,128)(2,1)}, u32[]{:S(2)}) copy-start(bf16[1,192,8,512]{3,2,1,0:T(8,128)(2,1)} %param.6) | copy-start | bytes 4718596
  20.6 44.0 %copy-start.4 = (s32[192]{0:T(256)S(1)}, s32[192]{0:T(256)}, u32[]{:S(2)}) copy-start(s32[192]{0:T(256)} %param.8) | copy-start | bytes 2308
  20.6 44.0 %copy-start.5 = (s32[192]{0:T(256)S(1)}, s32[192]{0:T(256)}, u32[]{:S(2)}) copy-start(s32[192]{0:T(256)} %param.7) | copy-start | bytes 2308
  22.2 27.1 %all-to-all-start = ((bf16[8,12,8,512]{3,2,1,0:T(8,128)(2,1)}), bf16[8,12,8,512]{3,2,1,0:T(8,128)(2,1)S(1)}, u32[]{:S(2)}, u32[]{:S(2)}) async-start(bf16[8,12,8,512]{3,2,1,0:T(8,128)(2,1)} %bitcast.4), calls=%async_computation | async-start | bytes 1572864 | tf_op jit(solution)/shard_map/all_to_all | solution.py:209
  50.8 30.0 %all-to-all-start.1 = ((bf16[64,8,512]{2,1,0:T(8,128)(2,1)}), bf16[64,8,512]{2,1,0:T(8,128)(2,1)S(1)}, u32[]{:S(2)}, u32[]{:S(2)}) async-start(bf16[64,8,512]{2,1,0:T(8,128)(2,1)} %sum_to_owner.1), calls=%async_computation.1 | async-start | bytes 1048576 | tf_op jit(solution)/shard_map/all_to_all | solution.py:213
  80.7 1.9 %copy-start.1 = (bf16[6,512,512]{2,1,0:T(8,128)(2,1)S(1)}, bf16[6,512,512]{2,1,0:T(8,128)(2,1)}, u32[]{:S(2)}) copy-start(bf16[6,512,512]{2,1,0:T(8,128)(2,1)} %left_ref.1) | copy-start | bytes 9437188
  82.6 1.9 %copy-start.2 = (bf16[6,512,512]{2,1,0:T(8,128)(2,1)S(1)}, bf16[6,512,512]{2,1,0:T(8,128)(2,1)}, u32[]{:S(2)}) copy-start(bf16[6,512,512]{2,1,0:T(8,128)(2,1)} %right_ref.1) | copy-start | bytes 9437188
  84.5 34.3 %copy-start.3 = (f32[192,8,32]{0,2,1:T(8,128)S(1)}, f32[192,8,32]{0,2,1:T(8,128)}, u32[]{:S(2)}) copy-start(f32[192,8,32]{0,2,1:T(8,128)} %param.11) | copy-start | bytes 589828
  111.6 15.7 %all-to-all-start.3 = ((bf16[16,3,8,128]{3,2,1,0:T(8,128)(2,1)}), bf16[16,3,8,128]{3,2,1,0:T(8,128)(2,1)S(1)}, u32[]{:S(2)}, u32[]{:S(2)}) async-start(bf16[16,3,8,128]{3,2,1,0:T(8,128)(2,1)} %split_columns.1), calls=%async_computation.3 | async-start | bytes 196608 | tf_op jit(solution)/shard_map/all_to_all | solution.py:217

commit v2 on v1

v2 whole, which is shorter than its diff:
```python
import functools

import jax
import jax.numpy as jnp
from jax import lax
from jax.experimental import pallas as pl
from jax.experimental.pallas import tpu as pltpu
from jax.sharding import Mesh, PartitionSpec as P

LANES = 128
VMEM = pl.BlockSpec(memory_space=pltpu.VMEM)
SMEM = pl.BlockSpec(memory_space=pltpu.SMEM)


def halves_kernel(core_ref, grads_ref, own_ref, away_ref, sems):
    width = own_ref.shape[2]
    copies = []
    for i, (side, out_ref) in enumerate(((core_ref[0], own_ref), (1 - core_ref[0], away_ref))):
        columns = pl.ds(pl.multiple_of(side * width, width), width)
        copies.append(pltpu.make_async_copy(grads_ref.at[:, :, columns], out_ref, sems.at[i]))
    for copy in copies:
        copy.start()
    for copy in copies:
        copy.wait()


def halves(core, grads):
    blocks, rows, width = grads.shape
    half = jax.ShapeDtypeStruct((blocks, rows, width // 2), grads.dtype)
    return pl.pallas_call(
        halves_kernel,
        out_shape=(half, half),
        in_specs=[SMEM, pl.BlockSpec(memory_space=pltpu.HBM)],
        out_specs=(VMEM, VMEM),
        scratch_shapes=[pltpu.SemaphoreType.DMA((2,))],
        compiler_params=pltpu.CompilerParams(vmem_limit_bytes=32 * 2**20),
        name="halves",
    )(core, grads)


def pair_sum_kernel(place_ref, own_ref, other_ref, out_ref):
    def body(b, carry):
        total = own_ref[b].astype(jnp.float32) + other_ref[b].astype(jnp.float32)
        out_ref[place_ref[b]] = total.astype(out_ref.dtype)
        return carry

    lax.fori_loop(0, own_ref.shape[0], body, 0, unroll=16)


def pair_sum(place, own, other):
    return pl.pallas_call(
        pair_sum_kernel,
        out_shape=jax.ShapeDtypeStruct(own.shape, own.dtype),
        in_specs=[SMEM, VMEM, VMEM],
        out_specs=VMEM,
        compiler_params=pltpu.CompilerParams(vmem_limit_bytes=32 * 2**20),
        name="pair_sum",
    )(place, own, other)


def sum_to_owner_kernel(owner_ref, parts_ref, out_ref):
    out_ref[...] = jnp.zeros_like(out_ref)
    for j in range(parts_ref.shape[1]):
        total = parts_ref[0, j].astype(jnp.float32)
        for i in range(1, parts_ref.shape[0]):
            total = total + parts_ref[i, j].astype(jnp.float32)
        out_ref[owner_ref[j]] = total.astype(out_ref.dtype)


def sum_to_owner(owner, parts, owner_count):
    return pl.pallas_call(
        sum_to_owner_kernel,
        out_shape=jax.ShapeDtypeStruct((owner_count,) + parts.shape[2:], parts.dtype),
        in_specs=[SMEM, VMEM],
        out_specs=VMEM,
        compiler_params=pltpu.CompilerParams(vmem_limit_bytes=32 * 2**20),
        name="sum_to_owner",
    )(owner, parts)


def precondition_kernel(core_ref, own_ref, other_ref, left_ref, right_ref, out_ref, *, slice_cols):
    size = left_ref.shape[-1]
    half = own_ref.shape[-1]
    cores = size // half
    area = float(size * size)
    core = core_ref[0]
    right_prod = jnp.zeros((size, size), jnp.float32)
    grad_squares = jnp.zeros((1, 1), jnp.float32)
    for side, grad_ref in ((core, own_ref), (1 - core, other_ref)):
        grad = grad_ref[...].reshape(size, half)
        factor = right_ref[pl.ds(pl.multiple_of(side * half, half), half), :]
        right_prod += jnp.dot(grad, factor, preferred_element_type=jnp.float32)
        grad_float = grad.astype(jnp.float32)
        grad_squares += jnp.sum(grad_float * grad_float, keepdims=True)
    precond = jnp.dot(
        left_ref[...], right_prod.astype(jnp.bfloat16), preferred_element_type=jnp.float32
    )
    precond_squares = jnp.sum(precond * precond, keepdims=True)
    scale = jnp.sqrt(grad_squares / area) / jnp.sqrt(precond_squares / area + 1e-06)
    grafted = (precond * scale).astype(jnp.bfloat16)
    column = lax.broadcasted_iota(jnp.int32, (size, half), 1)
    source = (column // slice_cols) * (slice_cols * cores) + core * slice_cols + column % slice_cols
    pick = (lax.broadcasted_iota(jnp.int32, (size, half), 0) == source).astype(jnp.bfloat16)
    picked = jnp.dot(grafted, pick, preferred_element_type=jnp.float32)
    out_ref[...] = picked.astype(out_ref.dtype).reshape(out_ref.shape)


def precondition(core, own, other, left_root, right_root, slice_cols):
    return pl.pallas_call(
        functools.partial(precondition_kernel, slice_cols=slice_cols),
        out_shape=jax.ShapeDtypeStruct(own.shape, own.dtype),
        in_specs=[SMEM, VMEM, VMEM, VMEM, VMEM],
        out_specs=VMEM,
        compiler_params=pltpu.CompilerParams(vmem_limit_bytes=32 * 2**20),
        name="precondition",
    )(core, own, other, left_root, right_root)


def split_columns_kernel(owner_ref, rows_ref, out_ref):
    replicas, groups, rows, lanes = out_ref.shape
    width = rows_ref.shape[-1] // replicas
    per = lanes // width
    lane = lax.broadcasted_iota(jnp.int32, (rows, lanes), 1) // width
    for g in range(groups):
        blocks = [rows_ref[owner_ref[g * per + i]].astype(jnp.float32) for i in range(per)]
        for t in range(replicas // per):
            tiles = [block[:, t * lanes : (t + 1) * lanes] for block in blocks]
            for k in range(per):
                mixed = tiles[k]
                for i in range(per):
                    if i != k:
                        moved = pltpu.roll(tiles[i], ((i - k) % per) * width, 1)
                        mixed = jnp.where(lane == i, moved, mixed)
                out_ref[t * per + k, g] = mixed.astype(out_ref.dtype)


def split_columns(owner, rows, replicas):
    count = owner.shape[0]
    width = rows.shape[-1] // replicas
    per = LANES // width
    shape = (replicas, count // per, rows.shape[1], LANES)
    return pl.pallas_call(
        split_columns_kernel,
        out_shape=jax.ShapeDtypeStruct(shape, rows.dtype),
        in_specs=[SMEM, VMEM],
        out_specs=VMEM,
        compiler_params=pltpu.CompilerParams(vmem_limit_bytes=32 * 2**20),
        name="split_columns",
    )(owner, rows)


def update_kernel(place_ref, momentum_ref, pieces_ref, out_ref, block_ref):
    replicas, groups, _, lanes = pieces_ref.shape
    width = momentum_ref.shape[-1]
    per = lanes // width
    count = place_ref.shape[0]

    def invert(b, carry):
        block_ref[place_ref[b]] = b
        return carry

    lax.fori_loop(0, count, invert, 0, unroll=8)
    def body(r, carry):
        for g in range(groups):
            tile = pieces_ref[r, g].astype(jnp.float32)
            for i in range(per):
                piece = tile if i == 0 else pltpu.roll(tile, lanes - i * width, 1)
                b = block_ref[r * (groups * per) + g * per + i]
                out_ref[b] = 0.9 * momentum_ref[b] + 0.1 * piece[:, :width]
        return carry

    lax.fori_loop(0, replicas, body, 0, unroll=2)


def update(place, momentum, pieces):
    return pl.pallas_call(
        update_kernel,
        out_shape=jax.ShapeDtypeStruct(momentum.shape, momentum.dtype),
        in_specs=[SMEM, VMEM, VMEM],
        out_specs=VMEM,
        scratch_shapes=[pltpu.SMEM(place.shape, jnp.int32)],
        compiler_params=pltpu.CompilerParams(vmem_limit_bytes=32 * 2**20),
        name="update",
    )(place, momentum, pieces)


def on_device(partial_grads, block_owner, block_slot, left_roots, right_roots, momentum):
    owner_count = lax.axis_size("y") * lax.axis_size("z")
    planes = lax.axis_size("x")
    cores = lax.axis_size("core")
    most = left_roots.shape[0]
    blocks, rows, width = partial_grads.shape[1:]
    each = blocks // planes
    half = width // cores
    core = lax.axis_index("core")
    plane = lax.axis_index("x")
    me = lax.axis_index(("y", "z"))

    swap = [(i, 1 - i) for i in range(cores)]
    grads = pltpu.with_memory_space_constraint(partial_grads[0], pltpu.HBM)
    own, away = halves(core.reshape(1), grads)
    other = lax.ppermute(away, "core", swap)

    entry = block_owner * most + block_slot
    rank = jnp.sum((entry[None, :] < entry[:, None]).astype(jnp.int32), axis=1)
    block_plane = rank % planes
    block_turn = rank // planes
    place = block_plane * each + block_turn
    mine = block_plane == plane
    turn_is = mine[None] & (
        block_turn[None] == lax.broadcasted_iota(jnp.int32, (each, blocks), 0)
    )
    my_owner = jnp.sum(jnp.where(turn_is, block_owner[None], 0), axis=1)
    my_slot = jnp.sum(jnp.where(mine & (block_owner == me), block_slot, 0))
    left_root = lax.dynamic_index_in_dim(left_roots, my_slot, 0, keepdims=False)
    right_root = lax.dynamic_index_in_dim(right_roots, my_slot, 0, keepdims=False)

    summed = pair_sum(place, own, other)
    parts = lax.all_to_all(
        summed.reshape(planes, each, rows, half), "x", split_axis=0, concat_axis=0, tiled=True
    )
    to_owner = sum_to_owner(my_owner, parts, owner_count)
    grad_half = lax.all_to_all(to_owner, ("y", "z"), split_axis=0, concat_axis=0, tiled=True)
    other_half = lax.ppermute(grad_half, "core", swap)
    grafted = precondition(
        core.reshape(1), grad_half, other_half, left_root, right_root, half // planes
    )
    back = lax.all_to_all(grafted, ("y", "z"), split_axis=0, concat_axis=0, tiled=True)
    pieces = split_columns(my_owner, back, planes)
    pieces = lax.all_to_all(pieces, "x", split_axis=0, concat_axis=0, tiled=True)
    return update(place, momentum, pieces)


def solution(mesh):
    devices = mesh.devices.reshape(8, 2, 8, 8)
    split = Mesh(devices, ("x", "core", "y", "z"))
    rep, fsdp = ("x", "core"), ("y", "z")
    in_specs = (
        P(rep, None, fsdp, None),
        P(),
        P(),
        P(fsdp, None, None),
        P(fsdp, None, None),
        P(None, fsdp, rep),
    )
    out_specs = P(None, fsdp, rep)
    return jax.shard_map(
        on_device, mesh=split, in_specs=in_specs, out_specs=out_specs, check_vma=False
    )
```

time: 131 us -> 118 us (0.901)
  blocking collectives: 23.9 us -> 43.7 us
  waiting for transfers between devices: 47 us -> 30.7 us
  starting transfers between devices: 40.2 us -> 27.8 us
  local copies, waits for them, and re-layouts: 9.61 us -> 2.66 us
  between operations: 0.08 us -> 2.06 us
    all_to_all x0 -> x1, blocking collectives: none -> 26.2 us  [on_device(): lax.all_to_all(to_owner, ('y', 'z'), split_axis=0, concat_axis=0, tiled=T...]
    all_to_all x3 -> x2, starting transfers between devices: 24.2 us -> 6.91 us  [the longest x1 3.55 us: on_device(): lax.all_to_all(summed.reshape(planes, each, rows, half), 'x', split_axis=...]
    all_to_all x3 -> x2, waiting for transfers between devices: 46.9 us -> 30.7 us  [the longest x1 23.4 us: on_device(): lax.all_to_all(summed.reshape(planes, each, rows, half), 'x', split_axis=...]
    all_to_all x1, blocking collectives: 23.9 us -> 17.5 us  [on_device(): lax.all_to_all(grafted, ('y', 'z'), split_axis=0, concat_axis=0, tiled=True)]
    unnamed x13 -> x5, local copies, waits for them, and re-layouts: 5.52 us -> 0.33 us
    ppermute x1 -> x2, starting transfers between devices: 16.1 us -> 20.9 us  [the longest x1 16.1 us: on_device(): other = lax.ppermute(away, 'core', swap)]
    reshape x2 -> x0, local copies, waits for them, and re-layouts: 1.52 us -> none  [the longest x1 0.76 us: on_device(): owner = block_owner.reshape(cores, half)]
    pallas_call x2 -> x3, Pallas kernels: 3.52 us -> 4.73 us  [the longest x1 1.7 us: pair_sum(): pl.pallas_call(pair_sum_kernel, out_shape=jax.ShapeDtypeStruct(own.shape,...]
  transfers between devices with their start and end apart: 4 -> 4, of which waited for: 4 -> 2; matrix products, arithmetic and copies ran while one was open for 3% -> 3% of each run, Pallas kernels for 0% -> 0%
where the time goes in v2:
time: 118 us; the launch traced here: 117 us
  blocking collectives  43.7 us (37%)
  waiting for transfers between devices  30.7 us (26%)
  starting transfers between devices  27.8 us (24%)
  Pallas kernels  8.02 us (7%)
  local copies, waits for them, and re-layouts  2.66 us (2%)
  other arithmetic  2.36 us (2%)
  between operations  2.06 us (2%)
    all_to_all x1, blocking collectives, on_device(): lax.all_to_all(to_owner, ('y', 'z'), split_axis=0, concat_axis=0, tiled=T...  26.2 us
    all_to_all x1, waiting for transfers between devices, on_device(): lax.all_to_all(summed.reshape(planes, each, rows, half), 'x', split_axis=...  23.4 us
    all_to_all x1, blocking collectives, on_device(): lax.all_to_all(grafted, ('y', 'z'), split_axis=0, concat_axis=0, tiled=True)  17.5 us
    ppermute x1, starting transfers between devices, on_device(): other = lax.ppermute(away, 'core', swap)  16.1 us
    all_to_all x1, waiting for transfers between devices, on_device(): lax.all_to_all(pieces, 'x', split_axis=0, concat_axis=0, tiled=True)  7.22 us
    ppermute x1, starting transfers between devices, on_device(): other_half = lax.ppermute(grad_half, 'core', swap)  4.87 us
    all_to_all x1, starting transfers between devices, on_device(): lax.all_to_all(summed.reshape(planes, each, rows, half), 'x', split_axis=...  3.55 us
    all_to_all x1, starting transfers between devices, on_device(): lax.all_to_all(pieces, 'x', split_axis=0, concat_axis=0, tiled=True)  3.36 us
  transfers between devices with their start and end apart: 4, of which 2 were waited for; matrix products, arithmetic and copies ran while one was open for 3% of the time, Pallas kernels for 0%

profile of v2, /device:TPU:1, one launch (start us, length us, event | category | flops | bytes accessed | tf_op | source)
XLA Modules:
  0.0 117.3 jit_solution(17475256052591774283)
XLA Ops:
  0.0 0.0 copy-start.1
  0.0 1.4 %halves.1 = (bf16[192,8,256]{2,1,0:T(8,128)(2,1)S(1)}, bf16[192,8,256]{2,1,0:T(8,128)(2,1)S(1)}) custom-call(s32[1]{0:T(128)} %bitcast.core_ref, bf16[192,8,512]{2,1,0:T(8,128)(2,1)} %bitcast.7), custom_call_target="tpu_custom_call" | custom-call | tf_op jit(solution)/shard_map/halves/pallas_call | solution.py:30
  1.4 16.1 %collective-permute-start = (bf16[192,8,256]{2,1,0:T(8,128)(2,1)S(1)}, bf16[192,8,256]{2,1,0:T(8,128)(2,1)S(1)}, u32[]{:S(2)}, u32[]{:S(2)}) collective-permute-start(bf16[192,8,256]{2,1,0:T(8,128)(2,1)S(1)} %get-tuple-element.8), channel_id=1, source_target_pairs={{0,64},{64,0},{1,65},{65,1},{2,66},{66,2},{3,67},{67,3},{4,68},{68... | collective-permute-start | bytes 2359304 | tf_op jit(solution)/shard_map/ppermute | solution.py:202
  17.5 0.7 multiply_add_fusion.1
  18.2 0.2 convert_reduce_fusion
  18.4 1.3 %fusion.1 = (s32[]{:T(128)}, pred[192]{0:T(512)(128)(4,1)S(1)}, s32[192]{0:T(256)S(1)}) fusion(s32[192]{0:T(256)} %param.8, s32[192]{0:T(256)} %param.7, s32[]{:T(128)S(6)} %add.32, s32[]{:T(128)S(6)} %axis_index.43, s32[192]{0:T(256)S(1)} %convert_reduce_fusion), kind=kLoop, calls=%fused_computation.12 | loop fusion | flops 3071 | bytes 3276 | tf_op jit(solution)/shard_map/reduce_sum | solution.py:214
  19.7 0.0 collective-permute-done.other_ref
  19.7 1.7 %pair_sum.1 = bf16[192,8,256]{2,1,0:T(8,128)(2,1)} custom-call(s32[192]{0:T(256)S(1)} %get-tuple-element.12.place_ref, bf16[192,8,256]{2,1,0:T(8,128)(2,1)S(1)} %get-tuple-element.7.own_ref, bf16[192,8,256]{2,1,0:T(8,128)(2,1)S(1)} %collective-permute-done.other_ref), custom_call_target="tpu_custom_call" | custom-call | tf_op jit(solution)/shard_map/pair_sum/pallas_call | solution.py:51
  21.4 3.5 %all-to-all-start = ((bf16[8,24,8,256]{3,2,1,0:T(8,128)(2,1)}), bf16[8,24,8,256]{3,2,1,0:T(8,128)(2,1)S(1)}, u32[]{:S(2)}, u32[]{:S(2)}) async-start(bf16[8,24,8,256]{3,2,1,0:T(8,128)(2,1)} %bitcast.2), calls=%async_computation | async-start | bytes 1572864 | tf_op jit(solution)/shard_map/all_to_all | solution.py:219
  25.0 0.0 copy-done.1
  25.0 0.1 select_reduce_fusion.owner_ref
  25.1 0.0 copy-start
  25.1 23.4 %all-to-all-done.parts_ref = bf16[8,24,8,256]{3,2,1,0:T(8,128)(2,1)S(1)} async-done(((bf16[8,24,8,256]{3,2,1,0:T(8,128)(2,1)}), bf16[8,24,8,256]{3,2,1,0:T(8,128)(2,1)S(1)}, u32[]{:S(2)}, u32[]{:S(2)}) %all-to-all-start) | async-done | bytes 786464 | tf_op jit(solution)/shard_map/all_to_all | solution.py:219
  48.6 0.6 sum_to_owner.1
  49.2 26.2 %all_to_all.20.own_ref = bf16[64,8,256]{2,1,0:T(8,128)(2,1)S(1)} all-to-all(bf16[64,8,256]{2,1,0:T(8,128)(2,1)S(1)} %sum_to_owner.1), channel_id=1, replica_groups=mesh['x'=8,'core'=2,'y'=8,'z'=8] {'y','z'}, dimensions={0} | all-to-all | bytes 524288 | tf_op jit(solution)/shard_map/all_to_all | solution.py:223
  75.4 4.9 %collective-permute-start.1 = (bf16[64,8,256]{2,1,0:T(8,128)(2,1)S(1)}, bf16[64,8,256]{2,1,0:T(8,128)(2,1)S(1)}, u32[]{:S(2)}, u32[]{:S(2)}) collective-permute-start(bf16[64,8,256]{2,1,0:T(8,128)(2,1)S(1)} %all_to_all.20.own_ref), channel_id=1, source_target_pairs={{0,64},{64,0},{1,65},{65,1},{2,66},{66,2},{3,67},{67,3},{4,68},{68... | collective-permute-start | bytes 786440 | tf_op jit(solution)/shard_map/ppermute | solution.py:224
  82.3 1.3 %dynamic-slice_bitcast_fusion = (bf16[512,512]{1,0:T(8,128)(2,1)S(1)}, bf16[512,512]{1,0:T(8,128)(2,1)S(1)}) fusion(bf16[6,512,512]{2,1,0:T(8,128)(2,1)} %param.10, s32[]{:T(128)S(6)} %select_n.37, bf16[6,512,512]{2,1,0:T(8,128)(2,1)} %param.9), kind=kLoop, calls=%fused_computation | loop fusion | bytes 2097156 | tf_op jit(solution)/shard_map/jit(dynamic_index_in_dim)/squeeze | solution.py:216
  83.5 0.0 collective-permute-done.1.other_ref
  83.5 1.6 %precondition.1 = bf16[64,8,256]{2,1,0:T(8,128)(2,1)S(1)} custom-call(s32[1]{0:T(128)} %bitcast.core_ref, bf16[64,8,256]{2,1,0:T(8,128)(2,1)S(1)} %all_to_all.20.own_ref, bf16[64,8,256]{2,1,0:T(8,128)(2,1)S(1)} %collective-permute-done.1.other_ref, bf16[512,512]{1,0:T(8,128)(2,1)S(1)} %get-tuple-element.15.left_ref, ...), custom_call_target="tpu_custom_call" | custom-call | tf_op jit(solution)/shard_map/precondition/pallas_call | solution.py:109
  85.2 17.5 %all_to_all.21.rows_ref = bf16[64,8,256]{2,1,0:T(8,128)(2,1)S(1)} all-to-all(bf16[64,8,256]{2,1,0:T(8,128)(2,1)S(1)} %precondition.1), channel_id=1, replica_groups=mesh['x'=8,'core'=2,'y'=8,'z'=8] {'y','z'}, dimensions={0} | all-to-all | bytes 524288 | tf_op jit(solution)/shard_map/all_to_all | solution.py:228
  102.6 1.3 %split_columns.1 = bf16[8,6,8,128]{3,2,1,0:T(8,128)(2,1)} custom-call(s32[24]{0:T(128)S(1)} %select_reduce_fusion.owner_ref, bf16[64,8,256]{2,1,0:T(8,128)(2,1)S(1)} %all_to_all.21.rows_ref), custom_call_target="tpu_custom_call" | custom-call | tf_op jit(solution)/shard_map/split_columns/pallas_call | solution.py:142
  104.0 3.4 %all-to-all-start.3 = ((bf16[8,6,8,128]{3,2,1,0:T(8,128)(2,1)}), bf16[8,6,8,128]{3,2,1,0:T(8,128)(2,1)S(1)}, u32[]{:S(2)}, u32[]{:S(2)}) async-start(bf16[8,6,8,128]{3,2,1,0:T(8,128)(2,1)} %split_columns.1), calls=%async_computation.3 | async-start | bytes 196608 | tf_op jit(solution)/shard_map/all_to_all | solution.py:230
  107.4 0.0 copy-done
  107.4 0.3 copy.9.momentum_ref
  107.7 7.2 %all-to-all-done.3.pieces_ref = bf16[8,6,8,128]{3,2,1,0:T(8,128)(2,1)S(1)} async-done(((bf16[8,6,8,128]{3,2,1,0:T(8,128)(2,1)}), bf16[8,6,8,128]{3,2,1,0:T(8,128)(2,1)S(1)}, u32[]{:S(2)}, u32[]{:S(2)}) %all-to-all-start.3) | async-done | bytes 98336 | tf_op jit(solution)/shard_map/all_to_all | solution.py:230
  114.9 1.3 %update.1 = f32[192,8,32]{2,1,0:T(8,128)S(1)} custom-call(s32[192]{0:T(256)S(1)} %get-tuple-element.12.place_ref, f32[192,8,32]{2,1,0:T(8,128)S(1)} %copy.9.momentum_ref, bf16[8,6,8,128]{3,2,1,0:T(8,128)(2,1)S(1)} %all-to-all-done.3.pieces_ref), custom_call_target="tpu_custom_call" | custom-call | tf_op jit(solution)/shard_map/update/pallas_call | solution.py:176
  116.2 1.1 copy.10
  (1 shorter events, 0.0 us)
Async XLA Ops:
  0.0 25.0 %copy-start.1 = (s32[192]{0:T(256)S(1)}, s32[192]{0:T(256)}, u32[]{:S(2)}) copy-start(s32[192]{0:T(256)} %param.7) | copy-start | bytes 2308
  1.4 18.3 %collective-permute-start = (bf16[192,8,256]{2,1,0:T(8,128)(2,1)S(1)}, bf16[192,8,256]{2,1,0:T(8,128)(2,1)S(1)}, u32[]{:S(2)}, u32[]{:S(2)}) collective-permute-start(bf16[192,8,256]{2,1,0:T(8,128)(2,1)S(1)} %get-tuple-element.8), channel_id=1, source_target_pairs={{0,64},{64,0},{1,65},{65,1},{2,66},{66,2},{3,67},{67,3},{4,68},{68... | collective-permute-start | bytes 2359304 | tf_op jit(solution)/shard_map/ppermute | solution.py:202
  21.4 27.1 %all-to-all-start = ((bf16[8,24,8,256]{3,2,1,0:T(8,128)(2,1)}), bf16[8,24,8,256]{3,2,1,0:T(8,128)(2,1)S(1)}, u32[]{:S(2)}, u32[]{:S(2)}) async-start(bf16[8,24,8,256]{3,2,1,0:T(8,128)(2,1)} %bitcast.2), calls=%async_computation | async-start | bytes 1572864 | tf_op jit(solution)/shard_map/all_to_all | solution.py:219
  25.1 82.2 %copy-start = (f32[192,8,32]{0,2,1:T(8,128)S(1)}, f32[192,8,32]{0,2,1:T(8,128)}, u32[]{:S(2)}) copy-start(f32[192,8,32]{0,2,1:T(8,128)} %param.11) | copy-start | bytes 589828
  75.4 8.1 %collective-permute-start.1 = (bf16[64,8,256]{2,1,0:T(8,128)(2,1)S(1)}, bf16[64,8,256]{2,1,0:T(8,128)(2,1)S(1)}, u32[]{:S(2)}, u32[]{:S(2)}) collective-permute-start(bf16[64,8,256]{2,1,0:T(8,128)(2,1)S(1)} %all_to_all.20.own_ref), channel_id=1, source_target_pairs={{0,64},{64,0},{1,65},{65,1},{2,66},{66,2},{3,67},{67,3},{4,68},{68... | collective-permute-start | bytes 786440 | tf_op jit(solution)/shard_map/ppermute | solution.py:224
  104.0 10.9 %all-to-all-start.3 = ((bf16[8,6,8,128]{3,2,1,0:T(8,128)(2,1)}), bf16[8,6,8,128]{3,2,1,0:T(8,128)(2,1)S(1)}, u32[]{:S(2)}, u32[]{:S(2)}) async-start(bf16[8,6,8,128]{3,2,1,0:T(8,128)(2,1)} %split_columns.1), calls=%async_computation.3 | async-start | bytes 196608 | tf_op jit(solution)/shard_map/all_to_all | solution.py:230

commit v3 on v2

--- a/solution.py
+++ b/solution.py
@@ -8,54 +8,76 @@
 from jax.sharding import Mesh, PartitionSpec as P
 
 LANES = 128
+COPIES = 4
 VMEM = pl.BlockSpec(memory_space=pltpu.VMEM)
 SMEM = pl.BlockSpec(memory_space=pltpu.SMEM)
 
 
-def halves_kernel(core_ref, grads_ref, own_ref, away_ref, sems):
-    width = own_ref.shape[2]
-    copies = []
-    for i, (side, out_ref) in enumerate(((core_ref[0], own_ref), (1 - core_ref[0], away_ref))):
-        columns = pl.ds(pl.multiple_of(side * width, width), width)
-        copies.append(pltpu.make_async_copy(grads_ref.at[:, :, columns], out_ref, sems.at[i]))
+def column_copies(grads_ref, half_ref, sems, side):
+    width = half_ref.shape[2]
+    parts = sems.shape[0]
+    count = half_ref.shape[0] // parts
+    columns = pl.ds(pl.multiple_of(side * width, width), width)
+    return [
+        pltpu.make_async_copy(
+            grads_ref.at[pl.ds(i * count, count), :, columns],
+            half_ref.at[pl.ds(i * count, count)],
+            sems.at[i],
+        )
+        for i in range(parts)
+    ]
+
+
+def away_half_kernel(core_ref, grads_ref, away_ref, sems):
+    copies = column_copies(grads_ref, away_ref, sems, 1 - core_ref[0])
     for copy in copies:
         copy.start()
     for copy in copies:
         copy.wait()
 
 
-def halves(core, grads):
+def away_half(core, grads):
     blocks, rows, width = grads.shape
-    half = jax.ShapeDtypeStruct((blocks, rows, width // 2), grads.dtype)
-    return pl.pallas_call(
-        halves_kernel,
-        out_shape=(half, half),
+    return pl.pallas_call(
+        away_half_kernel,
+        out_shape=jax.ShapeDtypeStruct((blocks, rows, width // 2), grads.dtype),
         in_specs=[SMEM, pl.BlockSpec(memory_space=pltpu.HBM)],
-        out_specs=(VMEM, VMEM),
-        scratch_shapes=[pltpu.SemaphoreType.DMA((2,))],
-        compiler_params=pltpu.CompilerParams(vmem_limit_bytes=32 * 2**20),
-        name="halves",
+        out_specs=VMEM,
+        scratch_shapes=[pltpu.SemaphoreType.DMA((COPIES,))],
+        compiler_params=pltpu.CompilerParams(vmem_limit_bytes=32 * 2**20),
+        name="away_half",
     )(core, grads)
 
 
-def pair_sum_kernel(place_ref, own_ref, other_ref, out_ref):
+def pair_sum_kernel(core_ref, place_ref, grads_ref, other_ref, out_ref, own_ref, sems):
+    copies = column_copies(grads_ref, own_ref, sems, core_ref[0])
+    for copy in copies:
+        copy.start()
+    count = own_ref.shape[0] // len(copies)
+
     def body(b, carry):
         total = own_ref[b].astype(jnp.float32) + other_ref[b].astype(jnp.float32)
         out_ref[place_ref[b]] = total.astype(out_ref.dtype)
         return carry
 
-    lax.fori_loop(0, own_ref.shape[0], body, 0, unroll=16)
-
-
-def pair_sum(place, own, other):
+    for i, copy in enumerate(copies):
+        copy.wait()
+        lax.fori_loop(i * count, (i + 1) * count, body, 0, unroll=16)
+
+
+def pair_sum(core, place, grads, other):
     return pl.pallas_call(
         pair_sum_kernel,
-        out_shape=jax.ShapeDtypeStruct(own.shape, own.dtype),
-        in_specs=[SMEM, VMEM, VMEM],
-        out_specs=VMEM,
+        out_shape=jax.ShapeDtypeStruct(other.shape, other.dtype),
+        in_specs=[SMEM, SMEM, pl.BlockSpec(memory_space=pltpu.HBM), VMEM],
+        out_specs=VMEM,
+        scratch_shapes=[
+            pltpu.VMEM(other.shape, other.dtype),
+            pltpu.SemaphoreType.DMA((COPIES,)),
+        ],
         compiler_params=pltpu.CompilerParams(vmem_limit_bytes=32 * 2**20),
         name="pair_sum",
-    )(place, own, other)
+    )(core, place, grads, other)
 
 
 def sum_to_owner_kernel(owner_ref, parts_ref, out_ref):
@@ -149,39 +171,37 @@
     )(owner, rows)
 
 
-def update_kernel(place_ref, momentum_ref, pieces_ref, out_ref, block_ref):
-    replicas, groups, _, lanes = pieces_ref.shape
-    width = momentum_ref.shape[-1]
+def update_kernel(place_ref, momentum_ref, pieces_ref, out_ref):
+    replicas, groups, rows, lanes = pieces_ref.shape
+    width, count = momentum_ref.shape[1:]
     per = lanes // width
-    count = place_ref.shape[0]
-
-    def invert(b, carry):
-        block_ref[place_ref[b]] = b
-        return carry
-
-    lax.fori_loop(0, count, invert, 0, unroll=8)
-    def body(r, carry):
-        for g in range(groups):
-            tile = pieces_ref[r, g].astype(jnp.float32)
-            for i in range(per):
-                piece = tile if i == 0 else pltpu.roll(tile, lanes - i * width, 1)
-                b = block_ref[r * (groups * per) + g * per + i]
-                out_ref[b] = 0.9 * momentum_ref[b] + 0.1 * piece[:, :width]
-        return carry
-
-    lax.fori_loop(0, replicas, body, 0, unroll=2)
+    depth = replicas * groups * rows
+    flipped = pieces_ref[...].astype(jnp.float32).reshape(depth, lanes).T.astype(jnp.bfloat16)
+    place = place_ref[...]
+    group = place // per
+    turn = place % per
+    source = lax.broadcasted_iota(jnp.int32, (depth, count), 0) - group * rows
+    for row in range(rows):
+        pick = (source == row).astype(jnp.bfloat16)
+        spread = jnp.dot(flipped, pick, preferred_element_type=jnp.float32)
+        value = jnp.zeros((width, count), jnp.float32)
+        for i in range(per):
+            value = jnp.where(turn == i, spread[i * width : (i + 1) * width], value)
+        out_ref[row] = 0.9 * momentum_ref[row] + 0.1 * value
 
 
 def update(place, momentum, pieces):
-    return pl.pallas_call(
+    flipped = pl.pallas_call(
         update_kernel,
-        out_shape=jax.ShapeDtypeStruct(momentum.shape, momentum.dtype),
-        in_specs=[SMEM, VMEM, VMEM],
-        out_specs=VMEM,
-        scratch_shapes=[pltpu.SMEM(place.shape, jnp.int32)],
+        out_shape=jax.ShapeDtypeStruct(
+            (momentum.shape[1], momentum.shape[2], momentum.shape[0]), momentum.dtype
+        ),
+        in_specs=[VMEM, VMEM, VMEM],
+        out_specs=VMEM,
         compiler_params=pltpu.CompilerParams(vmem_limit_bytes=32 * 2**20),
         name="update",
-    )(place, momentum, pieces)
+    )(place.reshape(1, -1), jnp.transpose(momentum, (1, 2, 0)), pieces)
+    return jnp.transpose(flipped, (2, 0, 1))
 
 
 def on_device(partial_grads, block_owner, block_slot, left_roots, right_roots, momentum):
@@ -198,27 +218,26 @@
 
     swap = [(i, 1 - i) for i in range(cores)]
     grads = pltpu.with_memory_space_constraint(partial_grads[0], pltpu.HBM)
-    own, away = halves(core.reshape(1), grads)
+    away = away_half(core.reshape(1), grads)
     other = lax.ppermute(away, "core", swap)
 
     entry = block_owner * most + block_slot
-    rank = jnp.sum((entry[None, :] < entry[:, None]).astype(jnp.int32), axis=1)
-    block_plane = rank % planes
-    block_turn = rank // planes
-    place = block_plane * each + block_turn
-    mine = block_plane == plane
-    turn_is = mine[None] & (
-        block_turn[None] == lax.broadcasted_iota(jnp.int32, (each, blocks), 0)
-    )
+    rank = jnp.sum((entry[None, :] < entry[:, None]).astype(jnp.uint32), axis=1)
+    place = (rank % planes * each + rank // planes).astype(jnp.int32)
+    summed = pair_sum(core.reshape(1), place, grads, other)
+
+    summed, rank, place = lax.optimization_barrier((summed, rank, place))
+    parts = lax.all_to_all(
+        summed.reshape(planes, each, rows, half), "x", split_axis=0, concat_axis=0, tiled=True
+    )
+    turns = lax.broadcasted_iota(jnp.uint32, (each, blocks), 0)
+    turn_is = rank[None] == turns * planes + plane.astype(jnp.uint32)
     my_owner = jnp.sum(jnp.where(turn_is, block_owner[None], 0), axis=1)
-    my_slot = jnp.sum(jnp.where(mine & (block_owner == me), block_slot, 0))
+    mine = (rank % planes == plane.astype(jnp.uint32)) & (block_owner == me)
+    my_slot = jnp.sum(jnp.where(mine, block_slot, 0))
     left_root = lax.dynamic_index_in_dim(left_roots, my_slot, 0, keepdims=False)
     right_root = lax.dynamic_index_in_dim(right_roots, my_slot, 0, keepdims=False)
-
-    summed = pair_sum(place, own, other)
-    parts = lax.all_to_all(
-        summed.reshape(planes, each, rows, half), "x", split_axis=0, concat_axis=0, tiled=True
-    )
+    parts, left_root, right_root = lax.optimization_barrier((parts, left_root, right_root))
     to_owner = sum_to_owner(my_owner, parts, owner_count)
     grad_half = lax.all_to_all(to_owner, ("y", "z"), split_axis=0, concat_axis=0, tiled=True)
     other_half = lax.ppermute(grad_half, "core", swap)

time: 118 us -> 114 us (0.966)
  blocking collectives: 43.7 us -> 53.2 us
  waiting for transfers between devices: 30.7 us -> 21.5 us
  starting transfers between devices: 27.8 us -> 24.5 us
  local copies, waits for them, and re-layouts: 2.66 us -> 1.33 us
    all_to_all x0 -> x1, blocking collectives: none -> 9.95 us  [on_device(): lax.all_to_all(pieces, 'x', split_axis=0, concat_axis=0, tiled=True)]
    all_to_all x1 -> x0, waiting for transfers between devices: 7.22 us -> none  [on_device(): lax.all_to_all(pieces, 'x', split_axis=0, concat_axis=0, tiled=True)]
    all_to_all x1, waiting for transfers between devices: 23.4 us -> 19.4 us  [on_device(): lax.all_to_all(summed.reshape(planes, each, rows, half), 'x', split_axis=...]
    all_to_all x1 -> x0, starting transfers between devices: 3.36 us -> none  [on_device(): lax.all_to_all(pieces, 'x', split_axis=0, concat_axis=0, tiled=True)]
  transfers between devices with their start and end apart: 4 -> 3, of which waited for: 2 -> 3; matrix products, arithmetic and copies ran while one was open for 3% -> 3% of each run, Pallas kernels for 0% -> 0%
where the time goes in v3:
time: 114 us; the launch traced here: 113 us
  blocking collectives  53.2 us (47%)
  starting transfers between devices  24.5 us (21%)
  waiting for transfers between devices  21.5 us (19%)
  Pallas kernels  8.17 us (7%)
  between operations  2.01 us (2%)
  other arithmetic  1.78 us (2%)
  local copies, waits for them, and re-layouts  1.33 us (1%)
    all_to_all x1, blocking collectives, on_device(): lax.all_to_all(to_owner, ('y', 'z'), split_axis=0, concat_axis=0, tiled=T...  26.1 us
    all_to_all x1, waiting for transfers between devices, on_device(): lax.all_to_all(summed.reshape(planes, each, rows, half), 'x', split_axis=...  19.4 us
    all_to_all x1, blocking collectives, on_device(): lax.all_to_all(grafted, ('y', 'z'), split_axis=0, concat_axis=0, tiled=True)  17.1 us
    ppermute x1, starting transfers between devices, on_device(): other = lax.ppermute(away, 'core', swap)  16.1 us
    all_to_all x1, blocking collectives, on_device(): lax.all_to_all(pieces, 'x', split_axis=0, concat_axis=0, tiled=True)  9.95 us
    ppermute x1, starting transfers between devices, on_device(): other_half = lax.ppermute(grad_half, 'core', swap)  4.92 us
    all_to_all x1, starting transfers between devices, on_device(): lax.all_to_all(summed.reshape(planes, each, rows, half), 'x', split_axis=...  3.56 us
    pallas_call x1, Pallas kernels, pair_sum(): pl.pallas_call(pair_sum_kernel, out_shape=jax.ShapeDtypeStruct(other.shap...  2.74 us
  transfers between devices with their start and end apart: 3, of which 3 were waited for; matrix products, arithmetic and copies ran while one was open for 3% of the time, Pallas kernels for 0%

profile of v3, /device:TPU:1, one launch (start us, length us, event | category | flops | bytes accessed | tf_op | source)
XLA Modules:
  0.0 112.6 jit_solution(2327692975625450613)
XLA Ops:
  0.0 0.0 copy-start.1
  0.0 0.0 copy-start.2
  0.0 1.3 %away_half.1 = bf16[192,8,256]{2,1,0:T(8,128)(2,1)S(1)} custom-call(s32[1]{0:T(128)} %bitcast.core_ref, bf16[192,8,512]{2,1,0:T(8,128)(2,1)} %bitcast.12), custom_call_target="tpu_custom_call" | custom-call | tf_op jit(solution)/shard_map/away_half/pallas_call | solution.py:41
  1.3 16.1 %collective-permute-start = (bf16[192,8,256]{2,1,0:T(8,128)(2,1)S(1)}, bf16[192,8,256]{2,1,0:T(8,128)(2,1)S(1)}, u32[]{:S(2)}, u32[]{:S(2)}) collective-permute-start(bf16[192,8,256]{2,1,0:T(8,128)(2,1)S(1)} %away_half.1), channel_id=1, source_target_pairs={{0,64},{64,0},{1,65},{65,1},{2,66},{66,2},{3,67},{67,3},{4,68},{68... | collective-permute-start | bytes 2359304 | tf_op jit(solution)/shard_map/ppermute | solution.py:222
  17.4 0.7 multiply_add_fusion
  18.1 0.2 convert_reduce_fusion
  18.3 1.0 collective-permute-done.other_ref
  19.2 2.7 %pair_sum.1 = bf16[192,8,256]{2,1,0:T(8,128)(2,1)} custom-call(s32[1]{0:T(128)} %bitcast.core_ref, s32[192]{0:T(256)S(1)} %fusion.1.place_ref, bf16[192,8,512]{2,1,0:T(8,128)(2,1)} %bitcast.13, bf16[192,8,256]{2,1,0:T(8,128)(2,1)S(1)} %collective-permute-done.other_ref), custom_call_target="tpu_custom_call" | custom-call | tf_op jit(solution)/shard_map/pair_sum/pallas_call | solution.py:69
  22.0 3.6 %all-to-all-start = ((bf16[8,24,8,256]{3,2,1,0:T(8,128)(2,1)}), bf16[8,24,8,256]{3,2,1,0:T(8,128)(2,1)S(1)}, u32[]{:S(2)}, u32[]{:S(2)}) async-start(bf16[8,24,8,256]{3,2,1,0:T(8,128)(2,1)} %bitcast.4), calls=%async_computation | async-start | bytes 1572864 | tf_op jit(solution)/shard_map/all_to_all | solution.py:230
  25.6 0.0 copy-done.1
  25.6 0.0 copy-done.2
  25.6 0.7 fusion.2
  28.2 0.2 select_reduce_fusion.owner_ref
  28.4 0.0 copy-start
  28.4 1.3 %dynamic-slice_bitcast_fusion = (bf16[512,512]{1,0:T(8,128)(2,1)S(1)}, bf16[512,512]{1,0:T(8,128)(2,1)S(1)}) fusion(bf16[6,512,512]{2,1,0:T(8,128)(2,1)} %param.12, s32[]{:T(128)S(6)} %select_n.18, bf16[6,512,512]{2,1,0:T(8,128)(2,1)} %param.11), kind=kLoop, calls=%fused_computation | loop fusion | bytes 2097156 | tf_op jit(solution)/shard_map/jit(dynamic_index_in_dim)/squeeze | solution.py:239
  29.7 19.4 %all-to-all-done.parts_ref = bf16[8,24,8,256]{3,2,1,0:T(8,128)(2,1)S(1)} async-done(((bf16[8,24,8,256]{3,2,1,0:T(8,128)(2,1)}), bf16[8,24,8,256]{3,2,1,0:T(8,128)(2,1)S(1)}, u32[]{:S(2)}, u32[]{:S(2)}) %all-to-all-start) | async-done | bytes 786464 | tf_op jit(solution)/shard_map/all_to_all | solution.py:230
  49.1 0.6 sum_to_owner.1
  49.8 26.1 %all_to_all.20.own_ref = bf16[64,8,256]{2,1,0:T(8,128)(2,1)S(1)} all-to-all(bf16[64,8,256]{2,1,0:T(8,128)(2,1)S(1)} %sum_to_owner.1), channel_id=1, replica_groups=mesh['x'=8,'core'=2,'y'=8,'z'=8] {'y','z'}, dimensions={0} | all-to-all | bytes 524288 | tf_op jit(solution)/shard_map/all_to_all | solution.py:242
  75.9 4.9 %collective-permute-start.1 = (bf16[64,8,256]{2,1,0:T(8,128)(2,1)S(1)}, bf16[64,8,256]{2,1,0:T(8,128)(2,1)S(1)}, u32[]{:S(2)}, u32[]{:S(2)}) collective-permute-start(bf16[64,8,256]{2,1,0:T(8,128)(2,1)S(1)} %all_to_all.20.own_ref), channel_id=1, source_target_pairs={{0,64},{64,0},{1,65},{65,1},{2,66},{66,2},{3,67},{67,3},{4,68},{68... | collective-permute-start | bytes 786440 | tf_op jit(solution)/shard_map/ppermute | solution.py:243
  80.8 1.1 %collective-permute-done.1.other_ref = bf16[64,8,256]{2,1,0:T(8,128)(2,1)S(1)} collective-permute-done((bf16[64,8,256]{2,1,0:T(8,128)(2,1)S(1)}, bf16[64,8,256]{2,1,0:T(8,128)(2,1)S(1)}, u32[]{:S(2)}, u32[]{:S(2)}) %collective-permute-start.1) | collective-permute-done | bytes 262176 | tf_op jit(solution)/shard_map/ppermute | solution.py:243
  81.9 1.6 %precondition.1 = bf16[64,8,256]{2,1,0:T(8,128)(2,1)S(1)} custom-call(s32[1]{0:T(128)} %bitcast.core_ref, bf16[64,8,256]{2,1,0:T(8,128)(2,1)S(1)} %all_to_all.20.own_ref, bf16[64,8,256]{2,1,0:T(8,128)(2,1)S(1)} %collective-permute-done.1.other_ref, bf16[512,512]{1,0:T(8,128)(2,1)S(1)} %get-tuple-element.16.left_ref, ...), custom_call_target="tpu_custom_call" | custom-call | tf_op jit(solution)/shard_map/precondition/pallas_call | solution.py:131
  83.6 17.1 %all_to_all.21.rows_ref = bf16[64,8,256]{2,1,0:T(8,128)(2,1)S(1)} all-to-all(bf16[64,8,256]{2,1,0:T(8,128)(2,1)S(1)} %precondition.1), channel_id=1, replica_groups=mesh['x'=8,'core'=2,'y'=8,'z'=8] {'y','z'}, dimensions={0} | all-to-all | bytes 524288 | tf_op jit(solution)/shard_map/all_to_all | solution.py:247
  100.7 0.7 split_columns.1
  101.4 10.0 %all_to_all.22.pieces_ref = bf16[8,6,8,128]{3,2,1,0:T(8,128)(2,1)S(1)} all-to-all(bf16[8,6,8,128]{3,2,1,0:T(8,128)(2,1)S(1)} %split_columns.1), channel_id=1, replica_groups=mesh['x'=8,'core'=2,'y'=8,'z'=8] {'x'}, dimensions={0} | all-to-all | bytes 196608 | tf_op jit(solution)/shard_map/all_to_all | solution.py:249
  111.4 0.0 copy-done
  111.4 1.2 %update.1 = f32[8,32,192]{2,1,0:T(8,128)} custom-call(s32[1,192]{1,0:T(1,128)S(1)} %bitcast.11, f32[8,32,192]{2,1,0:T(8,128)S(1)} %bitcast.10, bf16[8,6,8,128]{3,2,1,0:T(8,128)(2,1)S(1)} %all_to_all.22.pieces_ref), custom_call_target="tpu_custom_call" | custom-call | tf_op jit(solution)/shard_map/update/pallas_call | solution.py:194
  (2 shorter events, 0.0 us)
Async XLA Ops:
  0.0 25.6 %copy-start.1 = (s32[192]{0:T(256)S(1)}, s32[192]{0:T(256)}, u32[]{:S(2)}) copy-start(s32[192]{0:T(256)} %param.9) | copy-start | bytes 2308
  0.0 25.6 %copy-start.2 = (s32[192]{0:T(256)S(1)}, s32[192]{0:T(256)}, u32[]{:S(2)}) copy-start(s32[192]{0:T(256)} %param.10) | copy-start | bytes 2308
  1.3 18.0 %collective-permute-start = (bf16[192,8,256]{2,1,0:T(8,128)(2,1)S(1)}, bf16[192,8,256]{2,1,0:T(8,128)(2,1)S(1)}, u32[]{:S(2)}, u32[]{:S(2)}) collective-permute-start(bf16[192,8,256]{2,1,0:T(8,128)(2,1)S(1)} %away_half.1), channel_id=1, source_target_pairs={{0,64},{64,0},{1,65},{65,1},{2,66},{66,2},{3,67},{67,3},{4,68},{68... | collective-permute-start | bytes 2359304 | tf_op jit(solution)/shard_map/ppermute | solution.py:222
  22.0 27.1 %all-to-all-start = ((bf16[8,24,8,256]{3,2,1,0:T(8,128)(2,1)}), bf16[8,24,8,256]{3,2,1,0:T(8,128)(2,1)S(1)}, u32[]{:S(2)}, u32[]{:S(2)}) async-start(bf16[8,24,8,256]{3,2,1,0:T(8,128)(2,1)} %bitcast.4), calls=%async_computation | async-start | bytes 1572864 | tf_op jit(solution)/shard_map/all_to_all | solution.py:230
  28.4 83.0 %copy-start = (f32[192,8,32]{0,2,1:T(8,128)S(1)}, f32[192,8,32]{0,2,1:T(8,128)}, u32[]{:S(2)}) copy-start(f32[192,8,32]{0,2,1:T(8,128)} %param.13) | copy-start | bytes 589828
  75.9 6.1 %collective-permute-start.1 = (bf16[64,8,256]{2,1,0:T(8,128)(2,1)S(1)}, bf16[64,8,256]{2,1,0:T(8,128)(2,1)S(1)}, u32[]{:S(2)}, u32[]{:S(2)}) collective-permute-start(bf16[64,8,256]{2,1,0:T(8,128)(2,1)S(1)} %all_to_all.20.own_ref), channel_id=1, source_target_pairs={{0,64},{64,0},{1,65},{65,1},{2,66},{66,2},{3,67},{67,3},{4,68},{68... | collective-permute-start | bytes 786440 | tf_op jit(solution)/shard_map/ppermute | solution.py:243

commit v4 on v3

--- a/solution.py
+++ b/solution.py
@@ -13,12 +13,12 @@
 SMEM = pl.BlockSpec(memory_space=pltpu.SMEM)
 
 
-def column_copies(grads_ref, half_ref, sems, side):
+def column_half_kernel(side_ref, grads_ref, half_ref, sems):
     width = half_ref.shape[2]
     parts = sems.shape[0]
     count = half_ref.shape[0] // parts
-    columns = pl.ds(pl.multiple_of(side * width, width), width)
-    return [
+    columns = pl.ds(pl.multiple_of(side_ref[0] * width, width), width)
+    copies = [
         pltpu.make_async_copy(
             grads_ref.at[pl.ds(i * count, count), :, columns],
             half_ref.at[pl.ds(i * count, count)],
@@ -26,58 +26,39 @@
         )
         for i in range(parts)
     ]
-
-
-def away_half_kernel(core_ref, grads_ref, away_ref, sems):
-    copies = column_copies(grads_ref, away_ref, sems, 1 - core_ref[0])
     for copy in copies:
         copy.start()
     for copy in copies:
         copy.wait()
 
 
-def away_half(core, grads):
+def column_half(side, grads):
     blocks, rows, width = grads.shape
     return pl.pallas_call(
-        away_half_kernel,
+        column_half_kernel,
         out_shape=jax.ShapeDtypeStruct((blocks, rows, width // 2), grads.dtype),
         in_specs=[SMEM, pl.BlockSpec(memory_space=pltpu.HBM)],
         out_specs=VMEM,
         scratch_shapes=[pltpu.SemaphoreType.DMA((COPIES,))],
         compiler_params=pltpu.CompilerParams(vmem_limit_bytes=32 * 2**20),
-        name="away_half",
-    )(core, grads)
-
-
-def pair_sum_kernel(core_ref, place_ref, grads_ref, other_ref, out_ref, own_ref, sems):
-    copies = column_copies(grads_ref, own_ref, sems, core_ref[0])
-    for copy in copies:
-        copy.start()
-    count = own_ref.shape[0] // len(copies)
-
-    def body(b, carry):
-        total = own_ref[b].astype(jnp.float32) + other_ref[b].astype(jnp.float32)
-        out_ref[place_ref[b]] = total.astype(out_ref.dtype)
-        return carry
-
-    for i, copy in enumerate(copies):
-        copy.wait()
-        lax.fori_loop(i * count, (i + 1) * count, body, 0, unroll=16)
-
-
-def pair_sum(core, place, grads, other):
+        name="column_half",
+    )(side.reshape(1), grads)
+
+
+def pair_sum_kernel(place_ref, own_ref, other_ref, out_ref):
+    for b in range(own_ref.shape[0]):
+        out_ref[place_ref[b]] = own_ref[b] + other_ref[b]
+
+
+def pair_sum(place, own, other):
     return pl.pallas_call(
         pair_sum_kernel,
-        out_shape=jax.ShapeDtypeStruct(other.shape, other.dtype),
-        in_specs=[SMEM, SMEM, pl.BlockSpec(memory_space=pltpu.HBM), VMEM],
-        out_specs=VMEM,
-        scratch_shapes=[
-            pltpu.VMEM(other.shape, other.dtype),
-            pltpu.SemaphoreType.DMA((COPIES,)),
-        ],
+        out_shape=jax.ShapeDtypeStruct(own.shape, own.dtype),
+        in_specs=[SMEM, VMEM, VMEM],
+        out_specs=VMEM,
         compiler_params=pltpu.CompilerParams(vmem_limit_bytes=32 * 2**20),
         name="pair_sum",
-    )(core, place, grads, other)
+    )(place, own, other)
 
 
 def sum_to_owner_kernel(owner_ref, parts_ref, out_ref):
@@ -100,10 +81,52 @@
     )(owner, parts)
 
 
-def precondition_kernel(core_ref, own_ref, other_ref, left_ref, right_ref, out_ref, *, slice_cols):
+def fetch_roots_kernel(
+    slot_ref, core_ref, left_table, right_table, left_ref, right_ref, raw_ref, sems, *, slice_cols
+):
+    slot = slot_ref[0]
+    left_copy = pltpu.make_async_copy(left_table.at[slot], left_ref, sems.at[0])
+    right_copy = pltpu.make_async_copy(right_table.at[slot], raw_ref, sems.at[1])
+    right_copy.start()
+    left_copy.start()
+    size = raw_ref.shape[0]
+    half = size // 2
+    column = lax.broadcasted_iota(jnp.int32, (size, size), 1)
+    inner = column % half
+    side = jnp.where(column < half, core_ref[0], 1 - core_ref[0])
+    source = inner // slice_cols * (2 * slice_cols) + side * slice_cols + inner % slice_cols
+    pick = (lax.broadcasted_iota(jnp.int32, (size, size), 0) == source).astype(jnp.bfloat16)
+    right_copy.wait()
+    ordered = jnp.dot(raw_ref[...], pick, preferred_element_type=jnp.float32)
+    right_ref[...] = ordered.astype(right_ref.dtype)
+    left_copy.wait()
+
+
+def fetch_roots(slot, core, left_roots, right_roots, slice_cols):
+    root = jax.ShapeDtypeStruct(left_roots.shape[1:], left_roots.dtype)
+    hbm = pl.BlockSpec(memory_space=pltpu.HBM)
+    return pl.pallas_call(
+        functools.partial(fetch_roots_kernel, slice_cols=slice_cols),
+        out_shape=(root, root),
+        in_specs=[SMEM, SMEM, hbm, hbm],
+        out_specs=(VMEM, VMEM),
+        scratch_shapes=[
+            pltpu.VMEM(root.shape, root.dtype),
+            pltpu.SemaphoreType.DMA((2,)),
+        ],
+        compiler_params=pltpu.CompilerParams(vmem_limit_bytes=32 * 2**20),
+        name="fetch_roots",
+    )(
+        slot.reshape(1),
+        core.reshape(1),
+        pltpu.with_memory_space_constraint(left_roots, pltpu.HBM),
+        pltpu.with_memory_space_constraint(right_roots, pltpu.HBM),
+    )
+
+
+def precondition_kernel(core_ref, own_ref, other_ref, left_ref, right_ref, out_ref):
     size = left_ref.shape[-1]
     half = own_ref.shape[-1]
-    cores = size // half
     area = float(size * size)
     core = core_ref[0]
     right_prod = jnp.zeros((size, size), jnp.float32)
@@ -119,23 +142,19 @@
     )
     precond_squares = jnp.sum(precond * precond, keepdims=True)
     scale = jnp.sqrt(grad_squares / area) / jnp.sqrt(precond_squares / area + 1e-06)
-    grafted = (precond * scale).astype(jnp.bfloat16)
-    column = lax.broadcasted_iota(jnp.int32, (size, half), 1)
-    source = (column // slice_cols) * (slice_cols * cores) + core * slice_cols + column % slice_cols
-    pick = (lax.broadcasted_iota(jnp.int32, (size, half), 0) == source).astype(jnp.bfloat16)
-    picked = jnp.dot(grafted, pick, preferred_element_type=jnp.float32)
-    out_ref[...] = picked.astype(out_ref.dtype).reshape(out_ref.shape)
-
-
-def precondition(core, own, other, left_root, right_root, slice_cols):
-    return pl.pallas_call(
-        functools.partial(precondition_kernel, slice_cols=slice_cols),
+    grafted = (precond[:, :half] * scale).astype(out_ref.dtype)
+    out_ref[...] = grafted.reshape(out_ref.shape)
+
+
+def precondition(core, own, other, left_root, right_root):
+    return pl.pallas_call(
+        precondition_kernel,
         out_shape=jax.ShapeDtypeStruct(own.shape, own.dtype),
         in_specs=[SMEM, VMEM, VMEM, VMEM, VMEM],
         out_specs=VMEM,
         compiler_params=pltpu.CompilerParams(vmem_limit_bytes=32 * 2**20),
         name="precondition",
-    )(core, own, other, left_root, right_root)
+    )(core.reshape(1), own, other, left_root, right_root)
 
 
 def split_columns_kernel(owner_ref, rows_ref, out_ref):
@@ -218,13 +237,15 @@
 
     swap = [(i, 1 - i) for i in range(cores)]
     grads = pltpu.with_memory_space_constraint(partial_grads[0], pltpu.HBM)
-    away = away_half(core.reshape(1), grads)
+    away = column_half(1 - core, grads)
     other = lax.ppermute(away, "core", swap)
+    core_later, away = lax.optimization_barrier((core, away))
+    own = column_half(core_later, grads)
 
     entry = block_owner * most + block_slot
     rank = jnp.sum((entry[None, :] < entry[:, None]).astype(jnp.uint32), axis=1)
     place = (rank % planes * each + rank // planes).astype(jnp.int32)
-    summed = pair_sum(core.reshape(1), place, grads, other)
+    summed = pair_sum(place, own, other)
 
     summed, rank, place = lax.optimization_barrier((summed, rank, place))
     parts = lax.all_to_all(
@@ -235,15 +256,12 @@
     my_owner = jnp.sum(jnp.where(turn_is, block_owner[None], 0), axis=1)
     mine = (rank % planes == plane.astype(jnp.uint32)) & (block_owner == me)
     my_slot = jnp.sum(jnp.where(mine, block_slot, 0))
-    left_root = lax.dynamic_index_in_dim(left_roots, my_slot, 0, keepdims=False)
-    right_root = lax.dynamic_index_in_dim(right_roots, my_slot, 0, keepdims=False)
+    left_root, right_root = fetch_roots(my_slot, core, left_roots, right_roots, half // planes)
     parts, left_root, right_root = lax.optimization_barrier((parts, left_root, right_root))
     to_owner = sum_to_owner(my_owner, parts, owner_count)
     grad_half = lax.all_to_all(to_owner, ("y", "z"), split_axis=0, concat_axis=0, tiled=True)
     other_half = lax.ppermute(grad_half, "core", swap)
-    grafted = precondition(
-        core.reshape(1), grad_half, other_half, left_root, right_root, half // planes
-    )
+    grafted = precondition(core, grad_half, other_half, left_root, right_root)
     back = lax.all_to_all(grafted, ("y", "z"), split_axis=0, concat_axis=0, tiled=True)
     pieces = split_columns(my_owner, back, planes)
     pieces = lax.all_to_all(pieces, "x", split_axis=0, concat_axis=0, tiled=True)

time: 114 us -> 113 us (level)
  between operations: 2.01 us -> 0.13 us
  Pallas kernels: 8.17 us -> 9.85 us
  local copies, waits for them, and re-layouts: 1.33 us -> 0.01 us
    pallas_call x3 -> x5, Pallas kernels: 5.64 us -> 7.33 us  [the longest x2 2.53 us: column_half(): pl.pallas_call(column_half_kernel, out_shape=jax.ShapeDtypeStruct((blocks...]
    squeeze x1 -> x0, local copies, waits for them, and re-layouts: 1.32 us -> none  [on_device(): lax.dynamic_index_in_dim(right_roots, my_slot, 0, keepdims=False)]
  transfers between devices with their start and end apart: 3 -> 3, of which waited for: 3 -> 3; matrix products, arithmetic and copies ran while one was open for 3% -> 1% of each run, Pallas kernels for 0% -> 3%
where the time goes in v4:
time: 113 us; the launch traced here: 111 us
  blocking collectives  53.2 us (47%)
  starting transfers between devices  24.5 us (22%)
  waiting for transfers between devices  22.1 us (20%)
  Pallas kernels  9.85 us (9%)
    all_to_all x1, blocking collectives, on_device(): lax.all_to_all(to_owner, ('y', 'z'), split_axis=0, concat_axis=0, tiled=T...  26.1 us
    all_to_all x1, waiting for transfers between devices, on_device(): lax.all_to_all(summed.reshape(planes, each, rows, half), 'x', split_axis=...  20.5 us
    all_to_all x1, blocking collectives, on_device(): lax.all_to_all(grafted, ('y', 'z'), split_axis=0, concat_axis=0, tiled=True)  17.1 us
    ppermute x1, starting transfers between devices, on_device(): other = lax.ppermute(away, 'core', swap)  16.1 us
    all_to_all x1, blocking collectives, on_device(): lax.all_to_all(pieces, 'x', split_axis=0, concat_axis=0, tiled=True)  9.95 us
    ppermute x1, starting transfers between devices, on_device(): other_half = lax.ppermute(grad_half, 'core', swap)  4.92 us
    all_to_all x1, starting transfers between devices, on_device(): lax.all_to_all(summed.reshape(planes, each, rows, half), 'x', split_axis=...  3.55 us
    pallas_call x2, Pallas kernels, column_half(): pl.pallas_call(column_half_kernel, out_shape=jax.ShapeDtypeStruct((blocks...  2.53 us
  transfers between devices with their start and end apart: 3, of which 3 were waited for; matrix products, arithmetic and copies ran while one was open for 1% of the time, Pallas kernels for 3%

profile of v4, /device:TPU:1, one launch (start us, length us, event | category | flops | bytes accessed | tf_op | source)
XLA Modules:
  0.0 110.9 jit_solution(3452752011298140369)
XLA Ops:
  0.0 0.0 copy-start.2
  0.0 0.0 copy-start.1
  0.0 1.3 %column_half.2 = bf16[192,8,256]{2,1,0:T(8,128)(2,1)S(1)} custom-call(s32[1]{0:T(128)} %bitcast.side_ref, bf16[192,8,512]{2,1,0:T(8,128)(2,1)} %bitcast.11), custom_call_target="tpu_custom_call" | custom-call | tf_op jit(solution)/shard_map/column_half/pallas_call | solution.py:37
  1.3 16.1 %collective-permute-start = (bf16[192,8,256]{2,1,0:T(8,128)(2,1)S(1)}, bf16[192,8,256]{2,1,0:T(8,128)(2,1)S(1)}, u32[]{:S(2)}, u32[]{:S(2)}) collective-permute-start(bf16[192,8,256]{2,1,0:T(8,128)(2,1)S(1)} %column_half.2), channel_id=1, source_target_pairs={{0,64},{64,0},{1,65},{65,1},{2,66},{66,2},{3,67},{67,3},{4,68},{68... | collective-permute-start | bytes 2359304 | tf_op jit(solution)/shard_map/ppermute | solution.py:241
  17.4 1.3 %column_half.3.own_ref = bf16[192,8,256]{2,1,0:T(8,128)(2,1)S(1)} custom-call(s32[1]{0:T(128)} %bitcast.2.side_ref, bf16[192,8,512]{2,1,0:T(8,128)(2,1)} %bitcast.12), custom_call_target="tpu_custom_call" | custom-call | tf_op jit(solution)/shard_map/column_half/pallas_call | solution.py:37
  18.6 0.0 copy-done.2
  18.6 0.0 copy-done.1
  18.7 0.2 convert_reduce_fusion
  18.9 0.4 collective-permute-done.other_ref
  19.2 1.6 %pair_sum.1 = bf16[192,8,256]{2,1,0:T(8,128)(2,1)} custom-call(s32[192]{0:T(256)S(1)} %fusion.1.place_ref, bf16[192,8,256]{2,1,0:T(8,128)(2,1)S(1)} %column_half.3.own_ref, bf16[192,8,256]{2,1,0:T(8,128)(2,1)S(1)} %collective-permute-done.other_ref), custom_call_target="tpu_custom_call" | custom-call | tf_op jit(solution)/shard_map/pair_sum/pallas_call | solution.py:54
  20.8 3.5 %all-to-all-start = ((bf16[8,24,8,256]{3,2,1,0:T(8,128)(2,1)}), bf16[8,24,8,256]{3,2,1,0:T(8,128)(2,1)S(1)}, u32[]{:S(2)}, u32[]{:S(2)}) async-start(bf16[8,24,8,256]{3,2,1,0:T(8,128)(2,1)} %bitcast.6), calls=%async_computation | async-start | bytes 1572864 | tf_op jit(solution)/shard_map/all_to_all | solution.py:251
  24.4 0.7 fusion.2
  25.1 2.1 %fetch_roots.1 = (bf16[512,512]{1,0:T(8,128)(2,1)S(1)}, bf16[512,512]{1,0:T(8,128)(2,1)S(1)}) custom-call(s32[1]{0:T(128)} %bitcast.7.slot_ref, s32[1]{0:T(128)} %bitcast.5.core_ref, bf16[6,512,512]{2,1,0:T(8,128)(2,1)} %left_table.1, bf16[6,512,512]{2,1,0:T(8,128)(2,1)} %right_table.1), custom_call_target="tpu_custom_call" | custom-call | tf_op jit(solution)/shard_map/fetch_roots/pallas_call | solution.py:108
  27.2 0.0 copy-start
  27.2 0.2 select_reduce_fusion.owner_ref
  27.4 20.5 %all-to-all-done.parts_ref = bf16[8,24,8,256]{3,2,1,0:T(8,128)(2,1)S(1)} async-done(((bf16[8,24,8,256]{3,2,1,0:T(8,128)(2,1)}), bf16[8,24,8,256]{3,2,1,0:T(8,128)(2,1)S(1)}, u32[]{:S(2)}, u32[]{:S(2)}) %all-to-all-start) | async-done | bytes 786464 | tf_op jit(solution)/shard_map/all_to_all | solution.py:251
  47.9 0.6 sum_to_owner.1
  48.6 26.1 %all_to_all.20.own_ref = bf16[64,8,256]{2,1,0:T(8,128)(2,1)S(1)} all-to-all(bf16[64,8,256]{2,1,0:T(8,128)(2,1)S(1)} %sum_to_owner.1), channel_id=1, replica_groups=mesh['x'=8,'core'=2,'y'=8,'z'=8] {'y','z'}, dimensions={0} | all-to-all | bytes 524288 | tf_op jit(solution)/shard_map/all_to_all | solution.py:262
  74.7 4.9 %collective-permute-start.1 = (bf16[64,8,256]{2,1,0:T(8,128)(2,1)S(1)}, bf16[64,8,256]{2,1,0:T(8,128)(2,1)S(1)}, u32[]{:S(2)}, u32[]{:S(2)}) collective-permute-start(bf16[64,8,256]{2,1,0:T(8,128)(2,1)S(1)} %all_to_all.20.own_ref), channel_id=1, source_target_pairs={{0,64},{64,0},{1,65},{65,1},{2,66},{66,2},{3,67},{67,3},{4,68},{68... | collective-permute-start | bytes 786440 | tf_op jit(solution)/shard_map/ppermute | solution.py:263
  79.6 1.1 %collective-permute-done.1.other_ref = bf16[64,8,256]{2,1,0:T(8,128)(2,1)S(1)} collective-permute-done((bf16[64,8,256]{2,1,0:T(8,128)(2,1)S(1)}, bf16[64,8,256]{2,1,0:T(8,128)(2,1)S(1)}, u32[]{:S(2)}, u32[]{:S(2)}) %collective-permute-start.1) | collective-permute-done | bytes 262176 | tf_op jit(solution)/shard_map/ppermute | solution.py:263
  80.8 1.1 %precondition.1 = bf16[64,8,256]{2,1,0:T(8,128)(2,1)S(1)} custom-call(s32[1]{0:T(128)} %bitcast.5.core_ref, bf16[64,8,256]{2,1,0:T(8,128)(2,1)S(1)} %all_to_all.20.own_ref, bf16[64,8,256]{2,1,0:T(8,128)(2,1)S(1)} %collective-permute-done.1.other_ref, bf16[512,512]{1,0:T(8,128)(2,1)S(1)} %get-tuple-element.22.left_ref, ...), custom_call_target="tpu_custom_call" | custom-call | tf_op jit(solution)/shard_map/precondition/pallas_call | solution.py:150
  81.9 17.1 %all_to_all.21.rows_ref = bf16[64,8,256]{2,1,0:T(8,128)(2,1)S(1)} all-to-all(bf16[64,8,256]{2,1,0:T(8,128)(2,1)S(1)} %precondition.1), channel_id=1, replica_groups=mesh['x'=8,'core'=2,'y'=8,'z'=8] {'y','z'}, dimensions={0} | all-to-all | bytes 524288 | tf_op jit(solution)/shard_map/all_to_all | solution.py:265
  99.0 0.7 split_columns.1
  99.7 10.0 %all_to_all.22.pieces_ref = bf16[8,6,8,128]{3,2,1,0:T(8,128)(2,1)S(1)} all-to-all(bf16[8,6,8,128]{3,2,1,0:T(8,128)(2,1)S(1)} %split_columns.1), channel_id=1, replica_groups=mesh['x'=8,'core'=2,'y'=8,'z'=8] {'x'}, dimensions={0} | all-to-all | bytes 196608 | tf_op jit(solution)/shard_map/all_to_all | solution.py:267
  109.7 0.0 copy-done
  109.7 1.2 %update.1 = f32[8,32,192]{2,1,0:T(8,128)} custom-call(s32[1,192]{1,0:T(1,128)S(1)} %bitcast.10, f32[8,32,192]{2,1,0:T(8,128)S(1)} %bitcast.9, bf16[8,6,8,128]{3,2,1,0:T(8,128)(2,1)S(1)} %all_to_all.22.pieces_ref), custom_call_target="tpu_custom_call" | custom-call | tf_op jit(solution)/shard_map/update/pallas_call | solution.py:213
  (3 shorter events, 0.0 us)
Async XLA Ops:
  0.0 18.6 %copy-start.2 = (s32[192]{0:T(256)S(1)}, s32[192]{0:T(256)}, u32[]{:S(2)}) copy-start(s32[192]{0:T(256)} %param.10) | copy-start | bytes 2308
  0.0 18.6 %copy-start.1 = (s32[192]{0:T(256)S(1)}, s32[192]{0:T(256)}, u32[]{:S(2)}) copy-start(s32[192]{0:T(256)} %param.9) | copy-start | bytes 2308
  1.3 18.0 %collective-permute-start = (bf16[192,8,256]{2,1,0:T(8,128)(2,1)S(1)}, bf16[192,8,256]{2,1,0:T(8,128)(2,1)S(1)}, u32[]{:S(2)}, u32[]{:S(2)}) collective-permute-start(bf16[192,8,256]{2,1,0:T(8,128)(2,1)S(1)} %column_half.2), channel_id=1, source_target_pairs={{0,64},{64,0},{1,65},{65,1},{2,66},{66,2},{3,67},{67,3},{4,68},{68... | collective-permute-start | bytes 2359304 | tf_op jit(solution)/shard_map/ppermute | solution.py:241
  20.8 27.1 %all-to-all-start = ((bf16[8,24,8,256]{3,2,1,0:T(8,128)(2,1)}), bf16[8,24,8,256]{3,2,1,0:T(8,128)(2,1)S(1)}, u32[]{:S(2)}, u32[]{:S(2)}) async-start(bf16[8,24,8,256]{3,2,1,0:T(8,128)(2,1)} %bitcast.6), calls=%async_computation | async-start | bytes 1572864 | tf_op jit(solution)/shard_map/all_to_all | solution.py:251
  27.2 82.5 %copy-start = (f32[192,8,32]{0,2,1:T(8,128)S(1)}, f32[192,8,32]{0,2,1:T(8,128)}, u32[]{:S(2)}) copy-start(f32[192,8,32]{0,2,1:T(8,128)} %param.13) | copy-start | bytes 589828
  74.7 6.1 %collective-permute-start.1 = (bf16[64,8,256]{2,1,0:T(8,128)(2,1)S(1)}, bf16[64,8,256]{2,1,0:T(8,128)(2,1)S(1)}, u32[]{:S(2)}, u32[]{:S(2)}) collective-permute-start(bf16[64,8,256]{2,1,0:T(8,128)(2,1)S(1)} %all_to_all.20.own_ref), channel_id=1, source_target_pairs={{0,64},{64,0},{1,65},{65,1},{2,66},{66,2},{3,67},{67,3},{4,68},{68... | collective-permute-start | bytes 786440 | tf_op jit(solution)/shard_map/ppermute | solution.py:263

commit v5 on v4

--- a/solution.py
+++ b/solution.py
@@ -45,20 +45,34 @@
     )(side.reshape(1), grads)
 
 
-def pair_sum_kernel(place_ref, own_ref, other_ref, out_ref):
-    for b in range(own_ref.shape[0]):
-        out_ref[place_ref[b]] = own_ref[b] + other_ref[b]
-
-
-def pair_sum(place, own, other):
+def pair_sum_kernel(block_ref, own_ref, other_ref, out_ref, sum_ref, sems):
+    planes = sems.shape[0]
+    each = own_ref.shape[0] // planes
+    copies = []
+    for plane in range(planes):
+        for p in range(plane * each, (plane + 1) * each):
+            b = block_ref[p]
+            sum_ref[p] = own_ref[b] + other_ref[b]
+        part = pl.ds(plane * each, each)
+        copies.append(pltpu.make_async_copy(sum_ref.at[part], out_ref.at[part], sems.at[plane]))
+        copies[-1].start()
+    for copy in copies:
+        copy.wait()
+
+
+def pair_sum(block_at, own, other, planes):
     return pl.pallas_call(
         pair_sum_kernel,
         out_shape=jax.ShapeDtypeStruct(own.shape, own.dtype),
         in_specs=[SMEM, VMEM, VMEM],
-        out_specs=VMEM,
+        out_specs=pl.BlockSpec(memory_space=pltpu.HBM),
+        scratch_shapes=[
+            pltpu.VMEM(own.shape, own.dtype),
+            pltpu.SemaphoreType.DMA((planes,)),
+        ],
         compiler_params=pltpu.CompilerParams(vmem_limit_bytes=32 * 2**20),
         name="pair_sum",
-    )(place, own, other)
+    )(block_at, own, other)
 
 
 def sum_to_owner_kernel(owner_ref, parts_ref, out_ref):
@@ -124,37 +138,61 @@
     )
 
 
-def precondition_kernel(core_ref, own_ref, other_ref, left_ref, right_ref, out_ref):
+def half_product(core_ref, grad_ref, right_ref, opposite):
+    size, half = right_ref.shape[0], grad_ref.shape[-1]
+    side = 1 - core_ref[0] if opposite else core_ref[0]
+    grad = grad_ref[...].reshape(size, half)
+    factor = right_ref[pl.ds(pl.multiple_of(side * half, half), half), :]
+    product = jnp.dot(grad, factor, preferred_element_type=jnp.float32)
+    grad_float = grad.astype(jnp.float32)
+    return product, jnp.sum(grad_float * grad_float, keepdims=True)
+
+
+def own_product_kernel(core_ref, own_ref, right_ref, product_ref, squares_ref):
+    product, squares = half_product(core_ref, own_ref, right_ref, False)
+    product_ref[...] = product
+    squares_ref[...] = jnp.broadcast_to(squares, squares_ref.shape)
+
+
+def own_product(core, own, right_root):
+    return pl.pallas_call(
+        own_product_kernel,
+        out_shape=(
+            jax.ShapeDtypeStruct(right_root.shape, jnp.float32),
+            jax.ShapeDtypeStruct((1, LANES), jnp.float32),
+        ),
+        in_specs=[SMEM, VMEM, VMEM],
+        out_specs=(VMEM, VMEM),
+        compiler_params=pltpu.CompilerParams(vmem_limit_bytes=32 * 2**20),
+        name="own_product",
+    )(core.reshape(1), own, right_root)
+
+
+def precondition_kernel(
+    core_ref, product_ref, squares_ref, other_ref, left_ref, right_ref, out_ref
+):
     size = left_ref.shape[-1]
-    half = own_ref.shape[-1]
+    half = other_ref.shape[-1]
     area = float(size * size)
-    core = core_ref[0]
-    right_prod = jnp.zeros((size, size), jnp.float32)
-    grad_squares = jnp.zeros((1, 1), jnp.float32)
-    for side, grad_ref in ((core, own_ref), (1 - core, other_ref)):
-        grad = grad_ref[...].reshape(size, half)
-        factor = right_ref[pl.ds(pl.multiple_of(side * half, half), half), :]
-        right_prod += jnp.dot(grad, factor, preferred_element_type=jnp.float32)
-        grad_float = grad.astype(jnp.float32)
-        grad_squares += jnp.sum(grad_float * grad_float, keepdims=True)
-    precond = jnp.dot(
-        left_ref[...], right_prod.astype(jnp.bfloat16), preferred_element_type=jnp.float32
-    )
+    product, squares = half_product(core_ref, other_ref, right_ref, True)
+    right_prod = (product_ref[...] + product).astype(jnp.bfloat16)
+    grad_squares = squares_ref[:, :1] + squares
+    precond = jnp.dot(left_ref[...], right_prod, preferred_element_type=jnp.float32)
     precond_squares = jnp.sum(precond * precond, keepdims=True)
     scale = jnp.sqrt(grad_squares / area) / jnp.sqrt(precond_squares / area + 1e-06)
     grafted = (precond[:, :half] * scale).astype(out_ref.dtype)
     out_ref[...] = grafted.reshape(out_ref.shape)
 
 
-def precondition(core, own, other, left_root, right_root):
+def precondition(core, product, squares, other, left_root, right_root):
     return pl.pallas_call(
         precondition_kernel,
-        out_shape=jax.ShapeDtypeStruct(own.shape, own.dtype),
-        in_specs=[SMEM, VMEM, VMEM, VMEM, VMEM],
+        out_shape=jax.ShapeDtypeStruct(other.shape, other.dtype),
+        in_specs=[SMEM, VMEM, VMEM, VMEM, VMEM, VMEM],
         out_specs=VMEM,
         compiler_params=pltpu.CompilerParams(vmem_limit_bytes=32 * 2**20),
         name="precondition",
-    )(core.reshape(1), own, other, left_root, right_root)
+    )(core.reshape(1), product, squares, other, left_root, right_root)
 
 
 def split_columns_kernel(owner_ref, rows_ref, out_ref):
@@ -245,7 +283,9 @@
     entry = block_owner * most + block_slot
     rank = jnp.sum((entry[None, :] < entry[:, None]).astype(jnp.uint32), axis=1)
     place = (rank % planes * each + rank // planes).astype(jnp.int32)
-    summed = pair_sum(place, own, other)
+    order = lax.iota(jnp.int32, blocks)
+    block_at = jnp.sum(jnp.where(place[None, :] == order[:, None], order[None, :], 0), axis=1)
+    summed = pair_sum(block_at, own, other, planes)
 
     summed, rank, place = lax.optimization_barrier((summed, rank, place))
     parts = lax.all_to_all(
@@ -261,7 +301,8 @@
     to_owner = sum_to_owner(my_owner, parts, owner_count)
     grad_half = lax.all_to_all(to_owner, ("y", "z"), split_axis=0, concat_axis=0, tiled=True)
     other_half = lax.ppermute(grad_half, "core", swap)
-    grafted = precondition(core, grad_half, other_half, left_root, right_root)
+    product, squares = own_product(core, grad_half, right_root)
+    grafted = precondition(core, product, squares, other_half, left_root, right_root)
     back = lax.all_to_all(grafted, ("y", "z"), split_axis=0, concat_axis=0, tiled=True)
     pieces = split_columns(my_owner, back, planes)
     pieces = lax.all_to_all(pieces, "x", split_axis=0, concat_axis=0, tiled=True)

time: 113 us -> 113 us (level)
  no operation moved by 1% of the time
where the time goes in v5:
time: 113 us; the launch traced here: 111 us
  blocking collectives  53.2 us (47%)
  starting transfers between devices  24.5 us (22%)
  waiting for transfers between devices  21.6 us (19%)
  Pallas kernels  10.1 us (9%)
  other arithmetic  1.2 us (1%)
    all_to_all x1, blocking collectives, on_device(): lax.all_to_all(to_owner, ('y', 'z'), split_axis=0, concat_axis=0, tiled=T...  26.1 us
    all_to_all x1, waiting for transfers between devices, on_device(): lax.all_to_all(summed.reshape(planes, each, rows, half), 'x', split_axis=...  20.5 us
    all_to_all x1, blocking collectives, on_device(): lax.all_to_all(grafted, ('y', 'z'), split_axis=0, concat_axis=0, tiled=True)  17.1 us
    ppermute x1, starting transfers between devices, on_device(): other = lax.ppermute(away, 'core', swap)  16.1 us
    all_to_all x1, blocking collectives, on_device(): lax.all_to_all(pieces, 'x', split_axis=0, concat_axis=0, tiled=True)  9.95 us
    ppermute x1, starting transfers between devices, on_device(): other_half = lax.ppermute(grad_half, 'core', swap)  4.92 us
    all_to_all x1, starting transfers between devices, on_device(): lax.all_to_all(summed.reshape(planes, each, rows, half), 'x', split_axis=...  3.56 us
    pallas_call x2, Pallas kernels, column_half(): pl.pallas_call(column_half_kernel, out_shape=jax.ShapeDtypeStruct((blocks...  2.53 us
  transfers between devices with their start and end apart: 3, of which 3 were waited for; matrix products, arithmetic and copies ran while one was open for 1% of the time, Pallas kernels for 3%

profile of v5, /device:TPU:1, one launch (start us, length us, event | category | flops | bytes accessed | tf_op | source)
XLA Modules:
  0.0 110.8 jit_solution(10516347961910547856)
XLA Ops:
  0.0 0.0 copy-start.1
  0.0 0.0 copy-start.2
  0.0 1.3 %column_half.2 = bf16[192,8,256]{2,1,0:T(8,128)(2,1)S(1)} custom-call(s32[1]{0:T(128)} %bitcast.side_ref, bf16[192,8,512]{2,1,0:T(8,128)(2,1)} %bitcast.11), custom_call_target="tpu_custom_call" | custom-call | tf_op jit(solution)/shard_map/column_half/pallas_call | solution.py:37
  1.3 16.1 %collective-permute-start = (bf16[192,8,256]{2,1,0:T(8,128)(2,1)S(1)}, bf16[192,8,256]{2,1,0:T(8,128)(2,1)S(1)}, u32[]{:S(2)}, u32[]{:S(2)}) collective-permute-start(bf16[192,8,256]{2,1,0:T(8,128)(2,1)S(1)} %column_half.2), channel_id=1, source_target_pairs={{0,64},{64,0},{1,65},{65,1},{2,66},{66,2},{3,67},{67,3},{4,68},{68... | collective-permute-start | bytes 2359304 | tf_op jit(solution)/shard_map/ppermute | solution.py:279
  17.4 1.3 %column_half.3.own_ref = bf16[192,8,256]{2,1,0:T(8,128)(2,1)S(1)} custom-call(s32[1]{0:T(128)} %bitcast.2.side_ref, bf16[192,8,512]{2,1,0:T(8,128)(2,1)} %bitcast.12), custom_call_target="tpu_custom_call" | custom-call | tf_op jit(solution)/shard_map/column_half/pallas_call | solution.py:37
  18.6 0.0 copy-done.1
  18.6 0.0 copy-done.2
  18.7 0.2 convert_reduce_fusion
  18.9 0.1 select_reduce_fusion.block_ref
  19.0 0.3 collective-permute-done.other_ref
  19.2 1.5 %pair_sum.1 = bf16[192,8,256]{2,1,0:T(8,128)(2,1)} custom-call(s32[192]{0:T(256)S(1)} %select_reduce_fusion.block_ref, bf16[192,8,256]{2,1,0:T(8,128)(2,1)S(1)} %column_half.3.own_ref, bf16[192,8,256]{2,1,0:T(8,128)(2,1)S(1)} %collective-permute-done.other_ref), custom_call_target="tpu_custom_call" | custom-call | tf_op jit(solution)/shard_map/pair_sum/pallas_call | solution.py:64
  20.8 3.6 %all-to-all-start = ((bf16[8,24,8,256]{3,2,1,0:T(8,128)(2,1)}), bf16[8,24,8,256]{3,2,1,0:T(8,128)(2,1)S(1)}, u32[]{:S(2)}, u32[]{:S(2)}) async-start(bf16[8,24,8,256]{3,2,1,0:T(8,128)(2,1)} %bitcast.6), calls=%async_computation | async-start | bytes 1572864 | tf_op jit(solution)/shard_map/all_to_all | solution.py:291
  24.4 0.7 fusion.2
  25.1 2.1 %fetch_roots.1 = (bf16[512,512]{1,0:T(8,128)(2,1)S(1)}, bf16[512,512]{1,0:T(8,128)(2,1)S(1)}) custom-call(s32[1]{0:T(128)} %bitcast.7.slot_ref, s32[1]{0:T(128)} %bitcast.5.core_ref, bf16[6,512,512]{2,1,0:T(8,128)(2,1)} %left_table.1, bf16[6,512,512]{2,1,0:T(8,128)(2,1)} %right_table.1), custom_call_target="tpu_custom_call" | custom-call | tf_op jit(solution)/shard_map/fetch_roots/pallas_call | solution.py:122
  27.2 0.0 copy-start
  27.2 0.2 select_reduce_fusion.1.owner_ref
  27.4 20.5 %all-to-all-done.parts_ref = bf16[8,24,8,256]{3,2,1,0:T(8,128)(2,1)S(1)} async-done(((bf16[8,24,8,256]{3,2,1,0:T(8,128)(2,1)}), bf16[8,24,8,256]{3,2,1,0:T(8,128)(2,1)S(1)}, u32[]{:S(2)}, u32[]{:S(2)}) %all-to-all-start) | async-done | bytes 786464 | tf_op jit(solution)/shard_map/all_to_all | solution.py:291
  47.9 0.6 sum_to_owner.1
  48.5 26.1 %all_to_all.20.own_ref = bf16[64,8,256]{2,1,0:T(8,128)(2,1)S(1)} all-to-all(bf16[64,8,256]{2,1,0:T(8,128)(2,1)S(1)} %sum_to_owner.1), channel_id=1, replica_groups=mesh['x'=8,'core'=2,'y'=8,'z'=8] {'y','z'}, dimensions={0} | all-to-all | bytes 524288 | tf_op jit(solution)/shard_map/all_to_all | solution.py:302
  74.7 4.9 %collective-permute-start.1 = (bf16[64,8,256]{2,1,0:T(8,128)(2,1)S(1)}, bf16[64,8,256]{2,1,0:T(8,128)(2,1)S(1)}, u32[]{:S(2)}, u32[]{:S(2)}) collective-permute-start(bf16[64,8,256]{2,1,0:T(8,128)(2,1)S(1)} %all_to_all.20.own_ref), channel_id=1, source_target_pairs={{0,64},{64,0},{1,65},{65,1},{2,66},{66,2},{3,67},{67,3},{4,68},{68... | collective-permute-start | bytes 786440 | tf_op jit(solution)/shard_map/ppermute | solution.py:303
  79.6 0.3 own_product.1
  79.9 0.8 collective-permute-done.1.other_ref
  80.7 1.1 precondition.1
  81.8 17.1 %all_to_all.21.rows_ref = bf16[64,8,256]{2,1,0:T(8,128)(2,1)S(1)} all-to-all(bf16[64,8,256]{2,1,0:T(8,128)(2,1)S(1)} %precondition.1), channel_id=1, replica_groups=mesh['x'=8,'core'=2,'y'=8,'z'=8] {'y','z'}, dimensions={0} | all-to-all | bytes 524288 | tf_op jit(solution)/shard_map/all_to_all | solution.py:306
  98.9 0.7 split_columns.1
  99.6 10.0 %all_to_all.22.pieces_ref = bf16[8,6,8,128]{3,2,1,0:T(8,128)(2,1)S(1)} all-to-all(bf16[8,6,8,128]{3,2,1,0:T(8,128)(2,1)S(1)} %split_columns.1), channel_id=1, replica_groups=mesh['x'=8,'core'=2,'y'=8,'z'=8] {'x'}, dimensions={0} | all-to-all | bytes 196608 | tf_op jit(solution)/shard_map/all_to_all | solution.py:308
  109.6 0.0 copy-done
  109.6 1.2 %update.1 = f32[8,32,192]{2,1,0:T(8,128)} custom-call(s32[1,192]{1,0:T(1,128)S(1)} %bitcast.10, f32[8,32,192]{2,1,0:T(8,128)S(1)} %bitcast.9, bf16[8,6,8,128]{3,2,1,0:T(8,128)(2,1)S(1)} %all_to_all.22.pieces_ref), custom_call_target="tpu_custom_call" | custom-call | tf_op jit(solution)/shard_map/update/pallas_call | solution.py:251
  (3 shorter events, 0.0 us)
Async XLA Ops:
  0.0 18.6 %copy-start.1 = (s32[192]{0:T(256)S(1)}, s32[192]{0:T(256)}, u32[]{:S(2)}) copy-start(s32[192]{0:T(256)} %param.9) | copy-start | bytes 2308
  0.0 18.6 %copy-start.2 = (s32[192]{0:T(256)S(1)}, s32[192]{0:T(256)}, u32[]{:S(2)}) copy-start(s32[192]{0:T(256)} %param.10) | copy-start | bytes 2308
  1.3 18.0 %collective-permute-start = (bf16[192,8,256]{2,1,0:T(8,128)(2,1)S(1)}, bf16[192,8,256]{2,1,0:T(8,128)(2,1)S(1)}, u32[]{:S(2)}, u32[]{:S(2)}) collective-permute-start(bf16[192,8,256]{2,1,0:T(8,128)(2,1)S(1)} %column_half.2), channel_id=1, source_target_pairs={{0,64},{64,0},{1,65},{65,1},{2,66},{66,2},{3,67},{67,3},{4,68},{68... | collective-permute-start | bytes 2359304 | tf_op jit(solution)/shard_map/ppermute | solution.py:279
  20.8 27.1 %all-to-all-start = ((bf16[8,24,8,256]{3,2,1,0:T(8,128)(2,1)}), bf16[8,24,8,256]{3,2,1,0:T(8,128)(2,1)S(1)}, u32[]{:S(2)}, u32[]{:S(2)}) async-start(bf16[8,24,8,256]{3,2,1,0:T(8,128)(2,1)} %bitcast.6), calls=%async_computation | async-start | bytes 1572864 | tf_op jit(solution)/shard_map/all_to_all | solution.py:291
  27.2 82.4 %copy-start = (f32[192,8,32]{0,2,1:T(8,128)S(1)}, f32[192,8,32]{0,2,1:T(8,128)}, u32[]{:S(2)}) copy-start(f32[192,8,32]{0,2,1:T(8,128)} %param.13) | copy-start | bytes 589828
  74.7 6.1 %collective-permute-start.1 = (bf16[64,8,256]{2,1,0:T(8,128)(2,1)S(1)}, bf16[64,8,256]{2,1,0:T(8,128)(2,1)S(1)}, u32[]{:S(2)}, u32[]{:S(2)}) collective-permute-start(bf16[64,8,256]{2,1,0:T(8,128)(2,1)S(1)} %all_to_all.20.own_ref), channel_id=1, source_target_pairs={{0,64},{64,0},{1,65},{65,1},{2,66},{66,2},{3,67},{67,3},{4,68},{68... | collective-permute-start | bytes 786440 | tf_op jit(solution)/shard_map/ppermute | solution.py:303

commit v6 on v5

--- a/solution.py
+++ b/solution.py
@@ -45,31 +45,24 @@
     )(side.reshape(1), grads)
 
 
-def pair_sum_kernel(block_ref, own_ref, other_ref, out_ref, sum_ref, sems):
-    planes = sems.shape[0]
-    each = own_ref.shape[0] // planes
-    copies = []
-    for plane in range(planes):
-        for p in range(plane * each, (plane + 1) * each):
-            b = block_ref[p]
-            sum_ref[p] = own_ref[b] + other_ref[b]
-        part = pl.ds(plane * each, each)
-        copies.append(pltpu.make_async_copy(sum_ref.at[part], out_ref.at[part], sems.at[plane]))
-        copies[-1].start()
-    for copy in copies:
-        copy.wait()
-
-
-def pair_sum(block_at, own, other, planes):
+def pair_sum_kernel(block_ref, own_ref, other_ref, keep_ref, away_ref):
+    count = keep_ref.shape[0]
+    for p in range(own_ref.shape[0]):
+        b = block_ref[p]
+        total = own_ref[b] + other_ref[b]
+        if p < count:
+            keep_ref[p] = total
+        else:
+            away_ref[p - count] = total
+
+
+def pair_sum(block_at, own, other):
+    part = jax.ShapeDtypeStruct((own.shape[0] // 2,) + own.shape[1:], own.dtype)
     return pl.pallas_call(
         pair_sum_kernel,
-        out_shape=jax.ShapeDtypeStruct(own.shape, own.dtype),
+        out_shape=(part, part),
         in_specs=[SMEM, VMEM, VMEM],
-        out_specs=pl.BlockSpec(memory_space=pltpu.HBM),
-        scratch_shapes=[
-            pltpu.VMEM(own.shape, own.dtype),
-            pltpu.SemaphoreType.DMA((planes,)),
-        ],
+        out_specs=(VMEM, VMEM),
         compiler_params=pltpu.CompilerParams(vmem_limit_bytes=32 * 2**20),
         name="pair_sum",
     )(block_at, own, other)
@@ -261,17 +254,28 @@
     return jnp.transpose(flipped, (2, 0, 1))
 
 
+def neighbour(place):
+    x, core = place // 2, place % 2
+    step = 1 if (x + core) % 2 == 0 else -1
+    return (x + step) % 8 * 2 + core
+
+
 def on_device(partial_grads, block_owner, block_slot, left_roots, right_roots, momentum):
-    owner_count = lax.axis_size("y") * lax.axis_size("z")
-    planes = lax.axis_size("x")
+    along_x = ("xh", "xl")
+    rep = along_x + ("core",)
+    fsdp = ("y", "z")
+    owner_count = lax.axis_size(fsdp)
+    planes = lax.axis_size(along_x)
+    pairs = lax.axis_size("xh")
     cores = lax.axis_size("core")
     most = left_roots.shape[0]
     blocks, rows, width = partial_grads.shape[1:]
     each = blocks // planes
     half = width // cores
     core = lax.axis_index("core")
-    plane = lax.axis_index("x")
-    me = lax.axis_index(("y", "z"))
+    plane = lax.axis_index(along_x).astype(jnp.uint32)
+    parity = lax.axis_index("xl").astype(jnp.uint32)
+    me = lax.axis_index(fsdp)
 
     swap = [(i, 1 - i) for i in range(cores)]
     grads = pltpu.with_memory_space_constraint(partial_grads[0], pltpu.HBM)
@@ -282,37 +286,44 @@
 
     entry = block_owner * most + block_slot
     rank = jnp.sum((entry[None, :] < entry[:, None]).astype(jnp.uint32), axis=1)
+    block_plane = rank % planes
+    turn = rank // planes
+    spot = ((block_plane + parity) % 2 * pairs + block_plane // 2) * each + turn
+    order = lax.iota(jnp.uint32, blocks)
+    block_at = jnp.sum(jnp.where(spot[None, :] == order[:, None], order[None, :], 0), axis=1)
+    keep, away = pair_sum(block_at.astype(jnp.int32), own, other)
+
+    away, rank = lax.optimization_barrier((away, rank))
+    met = lax.ppermute(away, rep, [(i, neighbour(i)) for i in range(planes * cores)])
     place = (rank % planes * each + rank // planes).astype(jnp.int32)
-    order = lax.iota(jnp.int32, blocks)
-    block_at = jnp.sum(jnp.where(place[None, :] == order[:, None], order[None, :], 0), axis=1)
-    summed = pair_sum(block_at, own, other, planes)
-
-    summed, rank, place = lax.optimization_barrier((summed, rank, place))
-    parts = lax.all_to_all(
-        summed.reshape(planes, each, rows, half), "x", split_axis=0, concat_axis=0, tiled=True
-    )
     turns = lax.broadcasted_iota(jnp.uint32, (each, blocks), 0)
-    turn_is = rank[None] == turns * planes + plane.astype(jnp.uint32)
+    turn_is = rank[None] == turns * planes + plane
     my_owner = jnp.sum(jnp.where(turn_is, block_owner[None], 0), axis=1)
-    mine = (rank % planes == plane.astype(jnp.uint32)) & (block_owner == me)
+    mine = (rank % planes == plane) & (block_owner == me)
     my_slot = jnp.sum(jnp.where(mine, block_slot, 0))
     left_root, right_root = fetch_roots(my_slot, core, left_roots, right_roots, half // planes)
-    parts, left_root, right_root = lax.optimization_barrier((parts, left_root, right_root))
+    met, left_root, right_root, my_owner, place = lax.optimization_barrier(
+        (met, left_root, right_root, my_owner, place)
+    )
+
+    parts = lax.all_to_all(
+        (keep + met).reshape(pairs, each, rows, half), "xh", split_axis=0, concat_axis=0, tiled=True
+    )
     to_owner = sum_to_owner(my_owner, parts, owner_count)
-    grad_half = lax.all_to_all(to_owner, ("y", "z"), split_axis=0, concat_axis=0, tiled=True)
+    grad_half = lax.all_to_all(to_owner, fsdp, split_axis=0, concat_axis=0, tiled=True)
     other_half = lax.ppermute(grad_half, "core", swap)
     product, squares = own_product(core, grad_half, right_root)
     grafted = precondition(core, product, squares, other_half, left_root, right_root)
-    back = lax.all_to_all(grafted, ("y", "z"), split_axis=0, concat_axis=0, tiled=True)
+    back = lax.all_to_all(grafted, fsdp, split_axis=0, concat_axis=0, tiled=True)
     pieces = split_columns(my_owner, back, planes)
-    pieces = lax.all_to_all(pieces, "x", split_axis=0, concat_axis=0, tiled=True)
+    pieces = lax.all_to_all(pieces, along_x, split_axis=0, concat_axis=0, tiled=True)
     return update(place, momentum, pieces)
 
 
 def solution(mesh):
-    devices = mesh.devices.reshape(8, 2, 8, 8)
-    split = Mesh(devices, ("x", "core", "y", "z"))
-    rep, fsdp = ("x", "core"), ("y", "z")
+    devices = mesh.devices.reshape(4, 2, 2, 8, 8)
+    split = Mesh(devices, ("xh", "xl", "core", "y", "z"))
+    rep, fsdp = ("xh", "xl", "core"), ("y", "z")
     in_specs = (
         P(rep, None, fsdp, None),
         P(),

time: 113 us -> 112 us (level)
  blocking collectives: 53.2 us -> 69.6 us
  waiting for transfers between devices: 21.6 us -> 5.53 us
    all_to_all x1 -> x0, waiting for transfers between devices: 20.5 us -> none  [on_device(): lax.all_to_all(summed.reshape(planes, each, rows, half), 'x', split_axis=...]
    all_to_all x3 -> x4, blocking collectives: 53.2 us -> 69.6 us  [the longest x1 26 us: on_device(): lax.all_to_all(to_owner, fsdp, split_axis=0, concat_axis=0, tiled=True)]
    ppermute x0 -> x1, waiting for transfers between devices: none -> 4.7 us  [on_device(): lax.ppermute(away, rep, [(i, neighbour(i)) for i in range(planes * cores)])]
    all_to_all x1 -> x0, starting transfers between devices: 3.56 us -> none  [on_device(): lax.all_to_all(summed.reshape(planes, each, rows, half), 'x', split_axis=...]
    ppermute x0 -> x1, starting transfers between devices: none -> 1.92 us  [on_device(): lax.ppermute(away, rep, [(i, neighbour(i)) for i in range(planes * cores)])]
  transfers between devices with their start and end apart: 3 -> 3, of which waited for: 3 -> 2; matrix products, arithmetic and copies ran while one was open for 1% -> 2% of each run, Pallas kernels for 3% -> 3%
where the time goes in v6:
time: 112 us; the launch traced here: 110 us
  blocking collectives  69.6 us (62%)
  starting transfers between devices  23.4 us (21%)
  Pallas kernels  9.3 us (8%)
  waiting for transfers between devices  5.53 us (5%)
  other arithmetic  2.03 us (2%)
    all_to_all x1, blocking collectives, on_device(): lax.all_to_all(to_owner, fsdp, split_axis=0, concat_axis=0, tiled=True)  26 us
    all_to_all x1, blocking collectives, on_device(): lax.all_to_all(grafted, fsdp, split_axis=0, concat_axis=0, tiled=True)  17.2 us
    ppermute x1, starting transfers between devices, on_device(): other = lax.ppermute(away, 'core', swap)  16.1 us
    all_to_all x1, blocking collectives, on_device(): lax.all_to_all((keep + met).reshape(pairs, each, rows, half), 'xh', split...  15.8 us
    all_to_all x1, blocking collectives, on_device(): lax.all_to_all(pieces, along_x, split_axis=0, concat_axis=0, tiled=True)  10.6 us
    ppermute x1, starting transfers between devices, on_device(): other_half = lax.ppermute(grad_half, 'core', swap)  5.42 us
    ppermute x1, waiting for transfers between devices, on_device(): lax.ppermute(away, rep, [(i, neighbour(i)) for i in range(planes * cores)])  4.7 us
    pallas_call x2, Pallas kernels, column_half(): pl.pallas_call(column_half_kernel, out_shape=jax.ShapeDtypeStruct((blocks...  2.53 us
  transfers between devices with their start and end apart: 3, of which 2 were waited for; matrix products, arithmetic and copies ran while one was open for 2% of the time, Pallas kernels for 3%

profile of v6, /device:TPU:1, one launch (start us, length us, event | category | flops | bytes accessed | tf_op | source)
XLA Modules:
  0.0 110.0 jit_solution(11347902552263786709)
XLA Ops:
  0.0 0.0 copy-start.1
  0.0 0.0 copy-start.2
  0.0 1.3 %column_half.2 = bf16[192,8,256]{2,1,0:T(8,128)(2,1)S(1)} custom-call(s32[1]{0:T(128)} %bitcast.side_ref, bf16[192,8,512]{2,1,0:T(8,128)(2,1)} %bitcast.11), custom_call_target="tpu_custom_call" | custom-call | tf_op jit(solution)/shard_map/column_half/pallas_call | solution.py:37
  1.3 16.1 %collective-permute-start = (bf16[192,8,256]{2,1,0:T(8,128)(2,1)S(1)}, bf16[192,8,256]{2,1,0:T(8,128)(2,1)S(1)}, u32[]{:S(2)}, u32[]{:S(2)}) collective-permute-start(bf16[192,8,256]{2,1,0:T(8,128)(2,1)S(1)} %column_half.2), channel_id=1, source_target_pairs={{0,64},{64,0},{1,65},{65,1},{2,66},{66,2},{3,67},{67,3},{4,68},{68... | collective-permute-start | bytes 2359304 | tf_op jit(solution)/shard_map/ppermute | solution.py:283
  17.4 0.7 multiply_add_fusion
  18.1 0.2 convert_reduce_fusion
  18.3 0.1 select_reduce_fusion
  18.4 1.3 %column_half.3.own_ref = bf16[192,8,256]{2,1,0:T(8,128)(2,1)S(1)} custom-call(s32[1]{0:T(128)} %bitcast.2.side_ref, bf16[192,8,512]{2,1,0:T(8,128)(2,1)} %bitcast.12), custom_call_target="tpu_custom_call" | custom-call | tf_op jit(solution)/shard_map/column_half/pallas_call | solution.py:37
  19.7 0.0 collective-permute-done.other_ref
  19.7 0.8 pair_sum.1
  20.5 1.9 %collective-permute-start.1 = (bf16[96,8,256]{2,1,0:T(8,128)(2,1)S(1)}, bf16[96,8,256]{2,1,0:T(8,128)(2,1)S(1)}, u32[]{:S(2)}, u32[]{:S(2)}) collective-permute-start(bf16[96,8,256]{2,1,0:T(8,128)(2,1)S(1)} %get-tuple-element.23), channel_id=1, source_target_pairs={{0,128},{64,960},{128,0},{192,320},{256,384},{320,192},{384,256},{... | collective-permute-start | bytes 1179656 | tf_op jit(solution)/shard_map/ppermute | solution.py:297
  22.4 0.0 copy-done.1
  22.4 0.0 copy-done.2
  22.4 0.7 fusion.3
  23.1 2.2 %fetch_roots.1 = (bf16[512,512]{1,0:T(8,128)(2,1)S(1)}, bf16[512,512]{1,0:T(8,128)(2,1)S(1)}) custom-call(s32[1]{0:T(128)} %bitcast.3.slot_ref, s32[1]{0:T(128)} %bitcast.4.core_ref, bf16[6,512,512]{2,1,0:T(8,128)(2,1)} %left_table.1, bf16[6,512,512]{2,1,0:T(8,128)(2,1)} %right_table.1), custom_call_target="tpu_custom_call" | custom-call | tf_op jit(solution)/shard_map/fetch_roots/pallas_call | solution.py:115
  25.3 0.2 select_reduce_fusion.1.owner_ref
  25.5 4.7 %collective-permute-done.1 = bf16[96,8,256]{2,1,0:T(8,128)(2,1)S(1)} collective-permute-done((bf16[96,8,256]{2,1,0:T(8,128)(2,1)S(1)}, bf16[96,8,256]{2,1,0:T(8,128)(2,1)S(1)}, u32[]{:S(2)}, u32[]{:S(2)}) %collective-permute-start.1) | collective-permute-done | bytes 393248 | tf_op jit(solution)/shard_map/ppermute | solution.py:297
  30.2 0.1 add.46
  30.3 0.0 copy-start
  30.3 15.8 %all_to_all.20.parts_ref = bf16[4,24,8,256]{3,2,1,0:T(8,128)(2,1)S(1)} all-to-all(bf16[4,24,8,256]{3,2,1,0:T(8,128)(2,1)S(1)} %bitcast.13), channel_id=1, replica_groups=mesh['xh'=4,'xl'=2,'core'=2,'y'=8,'z'=8] {'xh'}, dimensions={0} | all-to-all | bytes 786432 | tf_op jit(solution)/shard_map/all_to_all | solution.py:309
  46.1 0.6 sum_to_owner.1
  46.7 26.0 %all_to_all.21.own_ref = bf16[64,8,256]{2,1,0:T(8,128)(2,1)S(1)} all-to-all(bf16[64,8,256]{2,1,0:T(8,128)(2,1)S(1)} %sum_to_owner.1), channel_id=1, replica_groups=mesh['xh'=4,'xl'=2,'core'=2,'y'=8,'z'=8] {'y','z'}, dimensions={0} | all-to-all | bytes 524288 | tf_op jit(solution)/shard_map/all_to_all | solution.py:313
  72.7 5.4 %collective-permute-start.2 = (bf16[64,8,256]{2,1,0:T(8,128)(2,1)S(1)}, bf16[64,8,256]{2,1,0:T(8,128)(2,1)S(1)}, u32[]{:S(2)}, u32[]{:S(2)}) collective-permute-start(bf16[64,8,256]{2,1,0:T(8,128)(2,1)S(1)} %all_to_all.21.own_ref), channel_id=1, source_target_pairs={{0,64},{64,0},{1,65},{65,1},{2,66},{66,2},{3,67},{67,3},{4,68},{68... | collective-permute-start | bytes 786440 | tf_op jit(solution)/shard_map/ppermute | solution.py:314
  78.1 0.3 own_product.1
  78.5 0.8 collective-permute-done.2.other_ref
  79.3 1.1 precondition.1
  80.3 17.2 %all_to_all.22.rows_ref = bf16[64,8,256]{2,1,0:T(8,128)(2,1)S(1)} all-to-all(bf16[64,8,256]{2,1,0:T(8,128)(2,1)S(1)} %precondition.1), channel_id=1, replica_groups=mesh['xh'=4,'xl'=2,'core'=2,'y'=8,'z'=8] {'y','z'}, dimensions={0} | all-to-all | bytes 524288 | tf_op jit(solution)/shard_map/all_to_all | solution.py:317
  97.6 0.7 split_columns.1
  98.3 10.6 %all_to_all.23.pieces_ref = bf16[8,6,8,128]{3,2,1,0:T(8,128)(2,1)S(1)} all-to-all(bf16[8,6,8,128]{3,2,1,0:T(8,128)(2,1)S(1)} %split_columns.1), channel_id=1, replica_groups=mesh['xh'=4,'xl'=2,'core'=2,'y'=8,'z'=8] {'xh','xl'}, dimensions={0} | all-to-all | bytes 196608 | tf_op jit(solution)/shard_map/all_to_all | solution.py:319
  108.8 0.0 copy-done
  108.8 1.2 %update.1 = f32[8,32,192]{2,1,0:T(8,128)} custom-call(s32[1,192]{1,0:T(1,128)S(1)} %bitcast.10, f32[8,32,192]{2,1,0:T(8,128)S(1)} %bitcast.9, bf16[8,6,8,128]{3,2,1,0:T(8,128)(2,1)S(1)} %all_to_all.23.pieces_ref), custom_call_target="tpu_custom_call" | custom-call | tf_op jit(solution)/shard_map/update/pallas_call | solution.py:244
  (4 shorter events, 0.0 us)
Async XLA Ops:
  0.0 22.4 %copy-start.1 = (s32[192]{0:T(256)S(1)}, s32[192]{0:T(256)}, u32[]{:S(2)}) copy-start(s32[192]{0:T(256)} %param.11) | copy-start | bytes 2308
  0.0 22.4 %copy-start.2 = (s32[192]{0:T(256)S(1)}, s32[192]{0:T(256)}, u32[]{:S(2)}) copy-start(s32[192]{0:T(256)} %param.12) | copy-start | bytes 2308
  1.3 18.4 %collective-permute-start = (bf16[192,8,256]{2,1,0:T(8,128)(2,1)S(1)}, bf16[192,8,256]{2,1,0:T(8,128)(2,1)S(1)}, u32[]{:S(2)}, u32[]{:S(2)}) collective-permute-start(bf16[192,8,256]{2,1,0:T(8,128)(2,1)S(1)} %column_half.2), channel_id=1, source_target_pairs={{0,64},{64,0},{1,65},{65,1},{2,66},{66,2},{3,67},{67,3},{4,68},{68... | collective-permute-start | bytes 2359304 | tf_op jit(solution)/shard_map/ppermute | solution.py:283
  20.5 9.7 %collective-permute-start.1 = (bf16[96,8,256]{2,1,0:T(8,128)(2,1)S(1)}, bf16[96,8,256]{2,1,0:T(8,128)(2,1)S(1)}, u32[]{:S(2)}, u32[]{:S(2)}) collective-permute-start(bf16[96,8,256]{2,1,0:T(8,128)(2,1)S(1)} %get-tuple-element.23), channel_id=1, source_target_pairs={{0,128},{64,960},{128,0},{192,320},{256,384},{320,192},{384,256},{... | collective-permute-start | bytes 1179656 | tf_op jit(solution)/shard_map/ppermute | solution.py:297
  30.3 78.5 %copy-start = (f32[192,8,32]{0,2,1:T(8,128)S(1)}, f32[192,8,32]{0,2,1:T(8,128)}, u32[]{:S(2)}) copy-start(f32[192,8,32]{0,2,1:T(8,128)} %param.15) | copy-start | bytes 589828
  72.7 6.6 %collective-permute-start.2 = (bf16[64,8,256]{2,1,0:T(8,128)(2,1)S(1)}, bf16[64,8,256]{2,1,0:T(8,128)(2,1)S(1)}, u32[]{:S(2)}, u32[]{:S(2)}) collective-permute-start(bf16[64,8,256]{2,1,0:T(8,128)(2,1)S(1)} %all_to_all.21.own_ref), channel_id=1, source_target_pairs={{0,64},{64,0},{1,65},{65,1},{2,66},{66,2},{3,67},{67,3},{4,68},{68... | collective-permute-start | bytes 786440 | tf_op jit(solution)/shard_map/ppermute | solution.py:314

commit v7 on v6

--- a/solution.py
+++ b/solution.py
@@ -45,24 +45,18 @@
     )(side.reshape(1), grads)
 
 
-def pair_sum_kernel(block_ref, own_ref, other_ref, keep_ref, away_ref):
-    count = keep_ref.shape[0]
-    for p in range(own_ref.shape[0]):
-        b = block_ref[p]
-        total = own_ref[b] + other_ref[b]
-        if p < count:
-            keep_ref[p] = total
-        else:
-            away_ref[p - count] = total
-
-
-def pair_sum(block_at, own, other):
-    part = jax.ShapeDtypeStruct((own.shape[0] // 2,) + own.shape[1:], own.dtype)
-    return pl.pallas_call(
-        pair_sum_kernel,
-        out_shape=(part, part),
+def pair_sum_kernel(first, block_ref, own_ref, other_ref, out_ref):
+    for p in range(out_ref.shape[0]):
+        b = block_ref[first + p]
+        out_ref[p] = own_ref[b] + other_ref[b]
+
+
+def pair_sum(block_at, own, other, first, count):
+    return pl.pallas_call(
+        functools.partial(pair_sum_kernel, first),
+        out_shape=jax.ShapeDtypeStruct((count,) + own.shape[1:], own.dtype),
         in_specs=[SMEM, VMEM, VMEM],
-        out_specs=(VMEM, VMEM),
+        out_specs=VMEM,
         compiler_params=pltpu.CompilerParams(vmem_limit_bytes=32 * 2**20),
         name="pair_sum",
     )(block_at, own, other)
@@ -283,17 +277,20 @@
     other = lax.ppermute(away, "core", swap)
     core_later, away = lax.optimization_barrier((core, away))
     own = column_half(core_later, grads)
-
-    entry = block_owner * most + block_slot
+    own, owner_later, slot_later = lax.optimization_barrier((own, block_owner, block_slot))
+
+    entry = owner_later * most + slot_later
     rank = jnp.sum((entry[None, :] < entry[:, None]).astype(jnp.uint32), axis=1)
     block_plane = rank % planes
     turn = rank // planes
     spot = ((block_plane + parity) % 2 * pairs + block_plane // 2) * each + turn
     order = lax.iota(jnp.uint32, blocks)
     block_at = jnp.sum(jnp.where(spot[None, :] == order[:, None], order[None, :], 0), axis=1)
-    keep, away = pair_sum(block_at.astype(jnp.int32), own, other)
-
-    away, rank = lax.optimization_barrier((away, rank))
+    block_at = block_at.astype(jnp.int32)
+    away = pair_sum(block_at, own, other, blocks // 2, blocks // 2)
+
+    away, rank, block_at = lax.optimization_barrier((away, rank, block_at))
+    keep = pair_sum(block_at, own, other, 0, blocks // 2)
     met = lax.ppermute(away, rep, [(i, neighbour(i)) for i in range(planes * cores)])
     place = (rank % planes * each + rank // planes).astype(jnp.int32)
     turns = lax.broadcasted_iota(jnp.uint32, (each, blocks), 0)
@@ -302,8 +299,8 @@
     mine = (rank % planes == plane) & (block_owner == me)
     my_slot = jnp.sum(jnp.where(mine, block_slot, 0))
     left_root, right_root = fetch_roots(my_slot, core, left_roots, right_roots, half // planes)
-    met, left_root, right_root, my_owner, place = lax.optimization_barrier(
-        (met, left_root, right_root, my_owner, place)
+    met, keep, left_root, right_root, my_owner, place = lax.optimization_barrier(
+        (met, keep, left_root, right_root, my_owner, place)
     )
 
     parts = lax.all_to_all(

time: 112 us -> 112 us (level)
  transfers between devices with their start and end apart: 3 -> 3, of which waited for: 2 -> 3; matrix products, arithmetic and copies ran while one was open for 2% -> 1% of each run, Pallas kernels for 3% -> 4%
where the time goes in v7:
time: 112 us; the launch traced here: 110 us
  blocking collectives  69.7 us (62%)
  starting transfers between devices  23.4 us (21%)
  Pallas kernels  9.86 us (9%)
  waiting for transfers between devices  5.11 us (5%)
  other arithmetic  1.33 us (1%)
    all_to_all x1, blocking collectives, on_device(): lax.all_to_all(to_owner, fsdp, split_axis=0, concat_axis=0, tiled=True)  26.8 us
    all_to_all x1, blocking collectives, on_device(): lax.all_to_all(grafted, fsdp, split_axis=0, concat_axis=0, tiled=True)  17.2 us
    ppermute x1, starting transfers between devices, on_device(): other = lax.ppermute(away, 'core', swap)  16.1 us
    all_to_all x1, blocking collectives, on_device(): lax.all_to_all((keep + met).reshape(pairs, each, rows, half), 'xh', split...  15.1 us
    all_to_all x1, blocking collectives, on_device(): lax.all_to_all(pieces, along_x, split_axis=0, concat_axis=0, tiled=True)  10.6 us
    ppermute x1, starting transfers between devices, on_device(): other_half = lax.ppermute(grad_half, 'core', swap)  5.4 us
    ppermute x1, waiting for transfers between devices, on_device(): lax.ppermute(away, rep, [(i, neighbour(i)) for i in range(planes * cores)])  4.06 us
    pallas_call x2, Pallas kernels, column_half(): pl.pallas_call(column_half_kernel, out_shape=jax.ShapeDtypeStruct((blocks...  2.53 us
  transfers between devices with their start and end apart: 3, of which 3 were waited for; matrix products, arithmetic and copies ran while one was open for 1% of the time, Pallas kernels for 4%

profile of v7, /device:TPU:1, one launch (start us, length us, event | category | flops | bytes accessed | tf_op | source)
XLA Modules:
  0.0 109.6 jit_solution(660287780315887184)
XLA Ops:
  0.0 0.0 copy-start.1
  0.0 0.0 copy-start.2
  0.0 1.3 %column_half.2 = bf16[192,8,256]{2,1,0:T(8,128)(2,1)S(1)} custom-call(s32[1]{0:T(128)} %bitcast.side_ref, bf16[192,8,512]{2,1,0:T(8,128)(2,1)} %bitcast.11), custom_call_target="tpu_custom_call" | custom-call | tf_op jit(solution)/shard_map/column_half/pallas_call | solution.py:37
  1.3 16.1 %collective-permute-start = (bf16[192,8,256]{2,1,0:T(8,128)(2,1)S(1)}, bf16[192,8,256]{2,1,0:T(8,128)(2,1)S(1)}, u32[]{:S(2)}, u32[]{:S(2)}) collective-permute-start(bf16[192,8,256]{2,1,0:T(8,128)(2,1)S(1)} %column_half.2), channel_id=1, source_target_pairs={{0,64},{64,0},{1,65},{65,1},{2,66},{66,2},{3,67},{67,3},{4,68},{68... | collective-permute-start | bytes 2359304 | tf_op jit(solution)/shard_map/ppermute | solution.py:277
  17.4 1.3 %column_half.3.own_ref = bf16[192,8,256]{2,1,0:T(8,128)(2,1)S(1)} custom-call(s32[1]{0:T(128)} %bitcast.2.side_ref, bf16[192,8,512]{2,1,0:T(8,128)(2,1)} %bitcast.12), custom_call_target="tpu_custom_call" | custom-call | tf_op jit(solution)/shard_map/column_half/pallas_call | solution.py:37
  18.6 0.0 copy-done.1
  18.6 0.0 copy-done.2
  18.7 0.2 convert_reduce_fusion
  18.9 0.1 select_reduce_fusion
  19.0 0.2 collective-permute-done.other_ref
  19.2 0.7 pair_sum.2
  19.9 1.9 %collective-permute-start.1 = (bf16[96,8,256]{2,1,0:T(8,128)(2,1)S(1)}, bf16[96,8,256]{2,1,0:T(8,128)(2,1)S(1)}, u32[]{:S(2)}, u32[]{:S(2)}) collective-permute-start(bf16[96,8,256]{2,1,0:T(8,128)(2,1)S(1)} %pair_sum.2), channel_id=1, source_target_pairs={{0,128},{64,960},{128,0},{192,320},{256,384},{320,192},{384,256},{... | collective-permute-start | bytes 1179656 | tf_op jit(solution)/shard_map/ppermute | solution.py:294
  21.8 0.7 fusion.3
  22.6 2.2 %fetch_roots.1 = (bf16[512,512]{1,0:T(8,128)(2,1)S(1)}, bf16[512,512]{1,0:T(8,128)(2,1)S(1)}) custom-call(s32[1]{0:T(128)} %bitcast.3.slot_ref, s32[1]{0:T(128)} %bitcast.4.core_ref, bf16[6,512,512]{2,1,0:T(8,128)(2,1)} %left_table.1, bf16[6,512,512]{2,1,0:T(8,128)(2,1)} %right_table.1), custom_call_target="tpu_custom_call" | custom-call | tf_op jit(solution)/shard_map/fetch_roots/pallas_call | solution.py:109
  24.7 0.7 pair_sum.3
  25.4 0.2 select_reduce_fusion.1.owner_ref
  25.6 4.1 %collective-permute-done.1 = bf16[96,8,256]{2,1,0:T(8,128)(2,1)S(1)} collective-permute-done((bf16[96,8,256]{2,1,0:T(8,128)(2,1)S(1)}, bf16[96,8,256]{2,1,0:T(8,128)(2,1)S(1)}, u32[]{:S(2)}, u32[]{:S(2)}) %collective-permute-start.1) | collective-permute-done | bytes 393248 | tf_op jit(solution)/shard_map/ppermute | solution.py:294
  29.6 0.1 add.46
  29.7 0.0 copy-start
  29.8 15.1 %all_to_all.20.parts_ref = bf16[4,24,8,256]{3,2,1,0:T(8,128)(2,1)S(1)} all-to-all(bf16[4,24,8,256]{3,2,1,0:T(8,128)(2,1)S(1)} %bitcast.13), channel_id=1, replica_groups=mesh['xh'=4,'xl'=2,'core'=2,'y'=8,'z'=8] {'xh'}, dimensions={0} | all-to-all | bytes 786432 | tf_op jit(solution)/shard_map/all_to_all | solution.py:306
  44.9 0.6 sum_to_owner.1
  45.5 26.8 %all_to_all.21.own_ref = bf16[64,8,256]{2,1,0:T(8,128)(2,1)S(1)} all-to-all(bf16[64,8,256]{2,1,0:T(8,128)(2,1)S(1)} %sum_to_owner.1), channel_id=1, replica_groups=mesh['xh'=4,'xl'=2,'core'=2,'y'=8,'z'=8] {'y','z'}, dimensions={0} | all-to-all | bytes 524288 | tf_op jit(solution)/shard_map/all_to_all | solution.py:310
  72.3 5.4 %collective-permute-start.2 = (bf16[64,8,256]{2,1,0:T(8,128)(2,1)S(1)}, bf16[64,8,256]{2,1,0:T(8,128)(2,1)S(1)}, u32[]{:S(2)}, u32[]{:S(2)}) collective-permute-start(bf16[64,8,256]{2,1,0:T(8,128)(2,1)S(1)} %all_to_all.21.own_ref), channel_id=1, source_target_pairs={{0,64},{64,0},{1,65},{65,1},{2,66},{66,2},{3,67},{67,3},{4,68},{68... | collective-permute-start | bytes 786440 | tf_op jit(solution)/shard_map/ppermute | solution.py:311
  77.7 0.3 own_product.1
  78.0 0.8 collective-permute-done.2.other_ref
  78.9 1.1 precondition.1
  79.9 17.2 %all_to_all.22.rows_ref = bf16[64,8,256]{2,1,0:T(8,128)(2,1)S(1)} all-to-all(bf16[64,8,256]{2,1,0:T(8,128)(2,1)S(1)} %precondition.1), channel_id=1, replica_groups=mesh['xh'=4,'xl'=2,'core'=2,'y'=8,'z'=8] {'y','z'}, dimensions={0} | all-to-all | bytes 524288 | tf_op jit(solution)/shard_map/all_to_all | solution.py:314
  97.1 0.7 split_columns.1
  97.8 10.6 %all_to_all.23.pieces_ref = bf16[8,6,8,128]{3,2,1,0:T(8,128)(2,1)S(1)} all-to-all(bf16[8,6,8,128]{3,2,1,0:T(8,128)(2,1)S(1)} %split_columns.1), channel_id=1, replica_groups=mesh['xh'=4,'xl'=2,'core'=2,'y'=8,'z'=8] {'xh','xl'}, dimensions={0} | all-to-all | bytes 196608 | tf_op jit(solution)/shard_map/all_to_all | solution.py:316
  108.4 0.0 copy-done
  108.4 1.2 %update.1 = f32[8,32,192]{2,1,0:T(8,128)} custom-call(s32[1,192]{1,0:T(1,128)S(1)} %bitcast.10, f32[8,32,192]{2,1,0:T(8,128)S(1)} %bitcast.9, bf16[8,6,8,128]{3,2,1,0:T(8,128)(2,1)S(1)} %all_to_all.23.pieces_ref), custom_call_target="tpu_custom_call" | custom-call | tf_op jit(solution)/shard_map/update/pallas_call | solution.py:238
  (5 shorter events, 0.0 us)
Async XLA Ops:
  0.0 18.6 %copy-start.1 = (s32[192]{0:T(256)S(1)}, s32[192]{0:T(256)}, u32[]{:S(2)}) copy-start(s32[192]{0:T(256)} %param.11) | copy-start | bytes 2308
  0.0 18.6 %copy-start.2 = (s32[192]{0:T(256)S(1)}, s32[192]{0:T(256)}, u32[]{:S(2)}) copy-start(s32[192]{0:T(256)} %param.12) | copy-start | bytes 2308
  1.3 18.0 %collective-permute-start = (bf16[192,8,256]{2,1,0:T(8,128)(2,1)S(1)}, bf16[192,8,256]{2,1,0:T(8,128)(2,1)S(1)}, u32[]{:S(2)}, u32[]{:S(2)}) collective-permute-start(bf16[192,8,256]{2,1,0:T(8,128)(2,1)S(1)} %column_half.2), channel_id=1, source_target_pairs={{0,64},{64,0},{1,65},{65,1},{2,66},{66,2},{3,67},{67,3},{4,68},{68... | collective-permute-start | bytes 2359304 | tf_op jit(solution)/shard_map/ppermute | solution.py:277
  19.9 9.7 %collective-permute-start.1 = (bf16[96,8,256]{2,1,0:T(8,128)(2,1)S(1)}, bf16[96,8,256]{2,1,0:T(8,128)(2,1)S(1)}, u32[]{:S(2)}, u32[]{:S(2)}) collective-permute-start(bf16[96,8,256]{2,1,0:T(8,128)(2,1)S(1)} %pair_sum.2), channel_id=1, source_target_pairs={{0,128},{64,960},{128,0},{192,320},{256,384},{320,192},{384,256},{... | collective-permute-start | bytes 1179656 | tf_op jit(solution)/shard_map/ppermute | solution.py:294
  29.7 78.7 %copy-start = (f32[192,8,32]{0,2,1:T(8,128)S(1)}, f32[192,8,32]{0,2,1:T(8,128)}, u32[]{:S(2)}) copy-start(f32[192,8,32]{0,2,1:T(8,128)} %param.15) | copy-start | bytes 589828
  72.3 6.6 %collective-permute-start.2 = (bf16[64,8,256]{2,1,0:T(8,128)(2,1)S(1)}, bf16[64,8,256]{2,1,0:T(8,128)(2,1)S(1)}, u32[]{:S(2)}, u32[]{:S(2)}) collective-permute-start(bf16[64,8,256]{2,1,0:T(8,128)(2,1)S(1)} %all_to_all.21.own_ref), channel_id=1, source_target_pairs={{0,64},{64,0},{1,65},{65,1},{2,66},{66,2},{3,67},{67,3},{4,68},{68... | collective-permute-start | bytes 786440 | tf_op jit(solution)/shard_map/ppermute | solution.py:311

commit v8 on v7

--- a/solution.py
+++ b/solution.py
@@ -45,21 +45,23 @@
     )(side.reshape(1), grads)
 
 
-def pair_sum_kernel(first, block_ref, own_ref, other_ref, out_ref):
+def pair_sum_kernel(first, core_ref, block_ref, own_ref, other_ref, out_ref):
+    width = own_ref.shape[2]
+    columns = pl.ds(pl.multiple_of(core_ref[0] * width, width), width)
     for p in range(out_ref.shape[0]):
         b = block_ref[first + p]
-        out_ref[p] = own_ref[b] + other_ref[b]
-
-
-def pair_sum(block_at, own, other, first, count):
+        out_ref[p] = own_ref[b] + other_ref[b, :, columns]
+
+
+def pair_sum(core, block_at, own, other, first, count):
     return pl.pallas_call(
         functools.partial(pair_sum_kernel, first),
         out_shape=jax.ShapeDtypeStruct((count,) + own.shape[1:], own.dtype),
-        in_specs=[SMEM, VMEM, VMEM],
+        in_specs=[SMEM, SMEM, VMEM, VMEM],
         out_specs=VMEM,
         compiler_params=pltpu.CompilerParams(vmem_limit_bytes=32 * 2**20),
         name="pair_sum",
-    )(block_at, own, other)
+    )(core.reshape(1), block_at, own, other)
 
 
 def sum_to_owner_kernel(owner_ref, parts_ref, out_ref):
@@ -215,18 +217,18 @@
     )(owner, rows)
 
 
-def update_kernel(place_ref, momentum_ref, pieces_ref, out_ref):
+def update_kernel(place_ref, momentum_ref, pieces_ref, out_ref, rows_ref):
     replicas, groups, rows, lanes = pieces_ref.shape
     width, count = momentum_ref.shape[1:]
     per = lanes // width
-    depth = replicas * groups * rows
-    flipped = pieces_ref[...].astype(jnp.float32).reshape(depth, lanes).T.astype(jnp.bfloat16)
+    depth = replicas * groups
+    rows_ref[...] = pieces_ref[...].astype(jnp.float32).reshape(depth * rows, lanes)
     place = place_ref[...]
-    group = place // per
     turn = place % per
-    source = lax.broadcasted_iota(jnp.int32, (depth, count), 0) - group * rows
+    group = lax.broadcasted_iota(jnp.int32, (depth, count), 0)
+    pick = (group == place // per).astype(jnp.bfloat16)
     for row in range(rows):
-        pick = (source == row).astype(jnp.bfloat16)
+        flipped = rows_ref[pl.ds(row, depth, stride=rows), :].T.astype(jnp.bfloat16)
         spread = jnp.dot(flipped, pick, preferred_element_type=jnp.float32)
         value = jnp.zeros((width, count), jnp.float32)
         for i in range(per):
@@ -235,6 +237,7 @@
 
 
 def update(place, momentum, pieces):
+    replicas, groups, rows, lanes = pieces.shape
     flipped = pl.pallas_call(
         update_kernel,
         out_shape=jax.ShapeDtypeStruct(
@@ -242,6 +245,7 @@
         ),
         in_specs=[VMEM, VMEM, VMEM],
         out_specs=VMEM,
+        scratch_shapes=[pltpu.VMEM((replicas * groups * rows, lanes), jnp.float32)],
         compiler_params=pltpu.CompilerParams(vmem_limit_bytes=32 * 2**20),
         name="update",
     )(place.reshape(1, -1), jnp.transpose(momentum, (1, 2, 0)), pieces)
@@ -272,11 +276,8 @@
     me = lax.axis_index(fsdp)
 
     swap = [(i, 1 - i) for i in range(cores)]
-    grads = pltpu.with_memory_space_constraint(partial_grads[0], pltpu.HBM)
-    away = column_half(1 - core, grads)
-    other = lax.ppermute(away, "core", swap)
-    core_later, away = lax.optimization_barrier((core, away))
-    own = column_half(core_later, grads)
+    other = lax.ppermute(partial_grads[0], "core", swap)
+    own = column_half(core, pltpu.with_memory_space_constraint(partial_grads[0], pltpu.HBM))
     own, owner_later, slot_later = lax.optimization_barrier((own, block_owner, block_slot))
 
     entry = owner_later * most + slot_later
@@ -287,10 +288,10 @@
     order = lax.iota(jnp.uint32, blocks)
     block_at = jnp.sum(jnp.where(spot[None, :] == order[:, None], order[None, :], 0), axis=1)
     block_at = block_at.astype(jnp.int32)
-    away = pair_sum(block_at, own, other, blocks // 2, blocks // 2)
+    away = pair_sum(core, block_at, own, other, blocks // 2, blocks // 2)
 
     away, rank, block_at = lax.optimization_barrier((away, rank, block_at))
-    keep = pair_sum(block_at, own, other, 0, blocks // 2)
+    keep = pair_sum(core, block_at, own, other, 0, blocks // 2)
     met = lax.ppermute(away, rep, [(i, neighbour(i)) for i in range(planes * cores)])
     place = (rank % planes * each + rank // planes).astype(jnp.int32)
     turns = lax.broadcasted_iota(jnp.uint32, (each, blocks), 0)

time: 112 us -> 112 us (level)
  Pallas kernels: 9.86 us -> 8.6 us
    pallas_call x2 -> x1, Pallas kernels: 2.53 us -> 1.26 us  [column_half(): pl.pallas_call(column_half_kernel, out_shape=jax.ShapeDtypeStruct((blocks...]
  transfers between devices with their start and end apart: 3 -> 3, of which waited for: 3 -> 3; matrix products, arithmetic and copies ran while one was open for 1% -> 2% of each run, Pallas kernels for 4% -> 4%
where the time goes in v8:
time: 112 us; the launch traced here: 110 us
  blocking collectives  69.7 us (62%)
  starting transfers between devices  23.5 us (21%)
  Pallas kernels  8.6 us (8%)
  waiting for transfers between devices  5.69 us (5%)
  other arithmetic  2.03 us (2%)
    all_to_all x1, blocking collectives, on_device(): lax.all_to_all(to_owner, fsdp, split_axis=0, concat_axis=0, tiled=True)  26.8 us
    all_to_all x1, blocking collectives, on_device(): lax.all_to_all(grafted, fsdp, split_axis=0, concat_axis=0, tiled=True)  17.2 us
    ppermute x1, starting transfers between devices, on_device(): other = lax.ppermute(partial_grads[0], 'core', swap)  16.2 us
    all_to_all x1, blocking collectives, on_device(): lax.all_to_all((keep + met).reshape(pairs, each, rows, half), 'xh', split...  15.1 us
    all_to_all x1, blocking collectives, on_device(): lax.all_to_all(pieces, along_x, split_axis=0, concat_axis=0, tiled=True)  10.5 us
    ppermute x1, starting transfers between devices, on_device(): other_half = lax.ppermute(grad_half, 'core', swap)  5.4 us
    ppermute x1, waiting for transfers between devices, on_device(): lax.ppermute(away, rep, [(i, neighbour(i)) for i in range(planes * cores)])  3.97 us
  transfers between devices with their start and end apart: 3, of which 3 were waited for; matrix products, arithmetic and copies ran while one was open for 2% of the time, Pallas kernels for 4%

profile of v8, /device:TPU:1, one launch (start us, length us, event | category | flops | bytes accessed | tf_op | source)
XLA Modules:
  0.0 109.7 jit_solution(9284363445336107545)
XLA Ops:
  0.0 0.0 copy-start.1
  0.0 0.0 copy-start.2
  0.0 16.2 %collective-permute-start = (bf16[192,8,512]{2,1,0:T(8,128)(2,1)}, bf16[192,8,512]{2,1,0:T(8,128)(2,1)S(1)}, u32[]{:S(2)}, u32[]{:S(2)}) collective-permute-start(bf16[192,8,512]{2,1,0:T(8,128)(2,1)} %bitcast.9), channel_id=1, source_target_pairs={{0,64},{64,0},{1,65},{65,1},{2,66},{66,2},{3,67},{67,3},{4,68},{68... | collective-permute-start | bytes 4718600 | tf_op jit(solution)/shard_map/ppermute | solution.py:279
  16.2 1.3 %column_half.1.own_ref = bf16[192,8,256]{2,1,0:T(8,128)(2,1)S(1)} custom-call(s32[1]{0:T(128)} %bitcast.side_ref.core_ref, bf16[192,8,512]{2,1,0:T(8,128)(2,1)} %bitcast.10), custom_call_target="tpu_custom_call" | custom-call | tf_op jit(solution)/shard_map/column_half/pallas_call | solution.py:37
  17.5 0.7 multiply_add_fusion
  18.2 0.2 convert_reduce_fusion
  18.4 0.1 select_reduce_fusion
  18.5 0.9 collective-permute-done.other_ref
  19.4 0.7 pair_sum.2
  20.2 1.9 %collective-permute-start.1 = (bf16[96,8,256]{2,1,0:T(8,128)(2,1)S(1)}, bf16[96,8,256]{2,1,0:T(8,128)(2,1)S(1)}, u32[]{:S(2)}, u32[]{:S(2)}) collective-permute-start(bf16[96,8,256]{2,1,0:T(8,128)(2,1)S(1)} %pair_sum.2), channel_id=1, source_target_pairs={{0,128},{64,960},{128,0},{192,320},{256,384},{320,192},{384,256},{... | collective-permute-start | bytes 1179656 | tf_op jit(solution)/shard_map/ppermute | solution.py:295
  22.1 0.0 copy-done.1
  22.1 0.0 copy-done.2
  22.1 0.7 fusion.3
  22.8 2.2 %fetch_roots.1 = (bf16[512,512]{1,0:T(8,128)(2,1)S(1)}, bf16[512,512]{1,0:T(8,128)(2,1)S(1)}) custom-call(s32[1]{0:T(128)} %bitcast.2.slot_ref, s32[1]{0:T(128)} %bitcast.side_ref.core_ref, bf16[6,512,512]{2,1,0:T(8,128)(2,1)} %left_table.1, bf16[6,512,512]{2,1,0:T(8,128)(2,1)} %right_table.1), custom_call_target="tpu_custom_call" | custom-call | tf_op jit(solution)/shard_map/fetch_roots/pallas_call | solution.py:111
  25.0 0.7 pair_sum.3
  25.7 0.2 select_reduce_fusion.1.owner_ref
  25.9 4.0 %collective-permute-done.1 = bf16[96,8,256]{2,1,0:T(8,128)(2,1)S(1)} collective-permute-done((bf16[96,8,256]{2,1,0:T(8,128)(2,1)S(1)}, bf16[96,8,256]{2,1,0:T(8,128)(2,1)S(1)}, u32[]{:S(2)}, u32[]{:S(2)}) %collective-permute-start.1) | collective-permute-done | bytes 393248 | tf_op jit(solution)/shard_map/ppermute | solution.py:295
  29.9 0.1 add.46
  30.0 0.0 copy-start
  30.0 15.1 %all_to_all.20.parts_ref = bf16[4,24,8,256]{3,2,1,0:T(8,128)(2,1)S(1)} all-to-all(bf16[4,24,8,256]{3,2,1,0:T(8,128)(2,1)S(1)} %bitcast.11), channel_id=1, replica_groups=mesh['xh'=4,'xl'=2,'core'=2,'y'=8,'z'=8] {'xh'}, dimensions={0} | all-to-all | bytes 786432 | tf_op jit(solution)/shard_map/all_to_all | solution.py:307
  45.1 0.6 sum_to_owner.1
  45.7 26.8 %all_to_all.21.own_ref = bf16[64,8,256]{2,1,0:T(8,128)(2,1)S(1)} all-to-all(bf16[64,8,256]{2,1,0:T(8,128)(2,1)S(1)} %sum_to_owner.1), channel_id=1, replica_groups=mesh['xh'=4,'xl'=2,'core'=2,'y'=8,'z'=8] {'y','z'}, dimensions={0} | all-to-all | bytes 524288 | tf_op jit(solution)/shard_map/all_to_all | solution.py:311
  72.6 5.4 %collective-permute-start.2 = (bf16[64,8,256]{2,1,0:T(8,128)(2,1)S(1)}, bf16[64,8,256]{2,1,0:T(8,128)(2,1)S(1)}, u32[]{:S(2)}, u32[]{:S(2)}) collective-permute-start(bf16[64,8,256]{2,1,0:T(8,128)(2,1)S(1)} %all_to_all.21.own_ref), channel_id=1, source_target_pairs={{0,64},{64,0},{1,65},{65,1},{2,66},{66,2},{3,67},{67,3},{4,68},{68... | collective-permute-start | bytes 786440 | tf_op jit(solution)/shard_map/ppermute | solution.py:312
  78.0 0.3 own_product.1
  78.3 0.8 collective-permute-done.2.other_ref
  79.1 1.1 precondition.1
  80.2 17.2 %all_to_all.22.rows_ref = bf16[64,8,256]{2,1,0:T(8,128)(2,1)S(1)} all-to-all(bf16[64,8,256]{2,1,0:T(8,128)(2,1)S(1)} %precondition.1), channel_id=1, replica_groups=mesh['xh'=4,'xl'=2,'core'=2,'y'=8,'z'=8] {'y','z'}, dimensions={0} | all-to-all | bytes 524288 | tf_op jit(solution)/shard_map/all_to_all | solution.py:315
  97.4 0.7 split_columns.1
  98.1 10.5 %all_to_all.23.pieces_ref = bf16[8,6,8,128]{3,2,1,0:T(8,128)(2,1)S(1)} all-to-all(bf16[8,6,8,128]{3,2,1,0:T(8,128)(2,1)S(1)} %split_columns.1), channel_id=1, replica_groups=mesh['xh'=4,'xl'=2,'core'=2,'y'=8,'z'=8] {'xh','xl'}, dimensions={0} | all-to-all | bytes 196608 | tf_op jit(solution)/shard_map/all_to_all | solution.py:317
  108.6 0.0 copy-done
  108.6 1.1 update.1
  (4 shorter events, 0.0 us)
Async XLA Ops:
  0.0 22.1 %copy-start.1 = (s32[192]{0:T(256)S(1)}, s32[192]{0:T(256)}, u32[]{:S(2)}) copy-start(s32[192]{0:T(256)} %param.11) | copy-start | bytes 2308
  0.0 22.1 %copy-start.2 = (s32[192]{0:T(256)S(1)}, s32[192]{0:T(256)}, u32[]{:S(2)}) copy-start(s32[192]{0:T(256)} %param.12) | copy-start | bytes 2308
  0.0 19.4 %collective-permute-start = (bf16[192,8,512]{2,1,0:T(8,128)(2,1)}, bf16[192,8,512]{2,1,0:T(8,128)(2,1)S(1)}, u32[]{:S(2)}, u32[]{:S(2)}) collective-permute-start(bf16[192,8,512]{2,1,0:T(8,128)(2,1)} %bitcast.9), channel_id=1, source_target_pairs={{0,64},{64,0},{1,65},{65,1},{2,66},{66,2},{3,67},{67,3},{4,68},{68... | collective-permute-start | bytes 4718600 | tf_op jit(solution)/shard_map/ppermute | solution.py:279
  20.2 9.7 %collective-permute-start.1 = (bf16[96,8,256]{2,1,0:T(8,128)(2,1)S(1)}, bf16[96,8,256]{2,1,0:T(8,128)(2,1)S(1)}, u32[]{:S(2)}, u32[]{:S(2)}) collective-permute-start(bf16[96,8,256]{2,1,0:T(8,128)(2,1)S(1)} %pair_sum.2), channel_id=1, source_target_pairs={{0,128},{64,960},{128,0},{192,320},{256,384},{320,192},{384,256},{... | collective-permute-start | bytes 1179656 | tf_op jit(solution)/shard_map/ppermute | solution.py:295
  30.0 78.6 %copy-start = (f32[192,8,32]{0,2,1:T(8,128)S(1)}, f32[192,8,32]{0,2,1:T(8,128)}, u32[]{:S(2)}) copy-start(f32[192,8,32]{0,2,1:T(8,128)} %param.15) | copy-start | bytes 589828
  72.6 6.6 %collective-permute-start.2 = (bf16[64,8,256]{2,1,0:T(8,128)(2,1)S(1)}, bf16[64,8,256]{2,1,0:T(8,128)(2,1)S(1)}, u32[]{:S(2)}, u32[]{:S(2)}) collective-permute-start(bf16[64,8,256]{2,1,0:T(8,128)(2,1)S(1)} %all_to_all.21.own_ref), channel_id=1, source_target_pairs={{0,64},{64,0},{1,65},{65,1},{2,66},{66,2},{3,67},{67,3},{4,68},{68... | collective-permute-start | bytes 786440 | tf_op jit(solution)/shard_map/ppermute | solution.py:312

commit v9 on v7

--- a/solution.py
+++ b/solution.py
@@ -215,33 +215,43 @@
     )(owner, rows)
 
 
-def update_kernel(place_ref, momentum_ref, pieces_ref, out_ref):
+def update_kernel(place_ref, momentum_ref, pieces_ref, out_ref, rows_ref, new_ref, sems):
     replicas, groups, rows, lanes = pieces_ref.shape
     width, count = momentum_ref.shape[1:]
     per = lanes // width
-    depth = replicas * groups * rows
-    flipped = pieces_ref[...].astype(jnp.float32).reshape(depth, lanes).T.astype(jnp.bfloat16)
+    depth = replicas * groups
+    rows_ref[...] = pieces_ref[...].astype(jnp.float32).reshape(depth * rows, lanes)
     place = place_ref[...]
-    group = place // per
     turn = place % per
-    source = lax.broadcasted_iota(jnp.int32, (depth, count), 0) - group * rows
+    group = lax.broadcasted_iota(jnp.int32, (depth, count), 0)
+    pick = (group == place // per).astype(jnp.bfloat16)
+    copies = []
     for row in range(rows):
-        pick = (source == row).astype(jnp.bfloat16)
+        flipped = rows_ref[pl.ds(row, depth, stride=rows), :].T.astype(jnp.bfloat16)
         spread = jnp.dot(flipped, pick, preferred_element_type=jnp.float32)
         value = jnp.zeros((width, count), jnp.float32)
         for i in range(per):
             value = jnp.where(turn == i, spread[i * width : (i + 1) * width], value)
-        out_ref[row] = 0.9 * momentum_ref[row] + 0.1 * value
+        new_ref[row] = 0.9 * momentum_ref[row] + 0.1 * value
+        copies.append(pltpu.make_async_copy(new_ref.at[row], out_ref.at[row], sems.at[row]))
+        copies[-1].start()
+    for copy in copies:
+        copy.wait()
 
 
 def update(place, momentum, pieces):
+    replicas, groups, rows, lanes = pieces.shape
+    shape = (momentum.shape[1], momentum.shape[2], momentum.shape[0])
     flipped = pl.pallas_call(
         update_kernel,
-        out_shape=jax.ShapeDtypeStruct(
-            (momentum.shape[1], momentum.shape[2], momentum.shape[0]), momentum.dtype
-        ),
+        out_shape=jax.ShapeDtypeStruct(shape, momentum.dtype),
         in_specs=[VMEM, VMEM, VMEM],
-        out_specs=VMEM,
+        out_specs=pl.BlockSpec(memory_space=pltpu.HBM),
+        scratch_shapes=[
+            pltpu.VMEM((replicas * groups * rows, lanes), jnp.float32),
+            pltpu.VMEM(shape, momentum.dtype),
+            pltpu.SemaphoreType.DMA((rows,)),
+        ],
         compiler_params=pltpu.CompilerParams(vmem_limit_bytes=32 * 2**20),
         name="update",
     )(place.reshape(1, -1), jnp.transpose(momentum, (1, 2, 0)), pieces)

time: 112 us -> 111 us (level)
  no operation moved by 1% of the time
where the time goes in v9:
time: 111 us; the launch traced here: 109 us
  blocking collectives  69.7 us (63%)
  starting transfers between devices  23.4 us (21%)
  Pallas kernels  9.73 us (9%)
  waiting for transfers between devices  5.11 us (5%)
  other arithmetic  1.33 us (1%)
    all_to_all x1, blocking collectives, on_device(): lax.all_to_all(to_owner, fsdp, split_axis=0, concat_axis=0, tiled=True)  26.8 us
    all_to_all x1, blocking collectives, on_device(): lax.all_to_all(grafted, fsdp, split_axis=0, concat_axis=0, tiled=True)  17.2 us
    ppermute x1, starting transfers between devices, on_device(): other = lax.ppermute(away, 'core', swap)  16.1 us
    all_to_all x1, blocking collectives, on_device(): lax.all_to_all((keep + met).reshape(pairs, each, rows, half), 'xh', split...  15.1 us
    all_to_all x1, blocking collectives, on_device(): lax.all_to_all(pieces, along_x, split_axis=0, concat_axis=0, tiled=True)  10.6 us
    ppermute x1, starting transfers between devices, on_device(): other_half = lax.ppermute(grad_half, 'core', swap)  5.4 us
    ppermute x1, waiting for transfers between devices, on_device(): lax.ppermute(away, rep, [(i, neighbour(i)) for i in range(planes * cores)])  4.06 us
    pallas_call x2, Pallas kernels, column_half(): pl.pallas_call(column_half_kernel, out_shape=jax.ShapeDtypeStruct((blocks...  2.53 us
  transfers between devices with their start and end apart: 3, of which 3 were waited for; matrix products, arithmetic and copies ran while one was open for 1% of the time, Pallas kernels for 4%

profile of v9, /device:TPU:1, one launch (start us, length us, event | category | flops | bytes accessed | tf_op | source)
XLA Modules:
  0.0 109.5 jit_solution(14326237069397585599)
XLA Ops:
  0.0 0.0 copy-start.1
  0.0 0.0 copy-start.2
  0.0 1.3 %column_half.2 = bf16[192,8,256]{2,1,0:T(8,128)(2,1)S(1)} custom-call(s32[1]{0:T(128)} %bitcast.side_ref, bf16[192,8,512]{2,1,0:T(8,128)(2,1)} %bitcast.11), custom_call_target="tpu_custom_call" | custom-call | tf_op jit(solution)/shard_map/column_half/pallas_call | solution.py:37
  1.3 16.1 %collective-permute-start = (bf16[192,8,256]{2,1,0:T(8,128)(2,1)S(1)}, bf16[192,8,256]{2,1,0:T(8,128)(2,1)S(1)}, u32[]{:S(2)}, u32[]{:S(2)}) collective-permute-start(bf16[192,8,256]{2,1,0:T(8,128)(2,1)S(1)} %column_half.2), channel_id=1, source_target_pairs={{0,64},{64,0},{1,65},{65,1},{2,66},{66,2},{3,67},{67,3},{4,68},{68... | collective-permute-start | bytes 2359304 | tf_op jit(solution)/shard_map/ppermute | solution.py:287
  17.4 1.3 %column_half.3.own_ref = bf16[192,8,256]{2,1,0:T(8,128)(2,1)S(1)} custom-call(s32[1]{0:T(128)} %bitcast.2.side_ref, bf16[192,8,512]{2,1,0:T(8,128)(2,1)} %bitcast.12), custom_call_target="tpu_custom_call" | custom-call | tf_op jit(solution)/shard_map/column_half/pallas_call | solution.py:37
  18.6 0.0 copy-done.1
  18.6 0.0 copy-done.2
  18.7 0.2 convert_reduce_fusion
  18.9 0.1 select_reduce_fusion
  19.0 0.2 collective-permute-done.other_ref
  19.2 0.7 pair_sum.2
  19.9 1.9 %collective-permute-start.1 = (bf16[96,8,256]{2,1,0:T(8,128)(2,1)S(1)}, bf16[96,8,256]{2,1,0:T(8,128)(2,1)S(1)}, u32[]{:S(2)}, u32[]{:S(2)}) collective-permute-start(bf16[96,8,256]{2,1,0:T(8,128)(2,1)S(1)} %pair_sum.2), channel_id=1, source_target_pairs={{0,128},{64,960},{128,0},{192,320},{256,384},{320,192},{384,256},{... | collective-permute-start | bytes 1179656 | tf_op jit(solution)/shard_map/ppermute | solution.py:304
  21.8 0.7 fusion.3
  22.6 2.2 %fetch_roots.1 = (bf16[512,512]{1,0:T(8,128)(2,1)S(1)}, bf16[512,512]{1,0:T(8,128)(2,1)S(1)}) custom-call(s32[1]{0:T(128)} %bitcast.3.slot_ref, s32[1]{0:T(128)} %bitcast.4.core_ref, bf16[6,512,512]{2,1,0:T(8,128)(2,1)} %left_table.1, bf16[6,512,512]{2,1,0:T(8,128)(2,1)} %right_table.1), custom_call_target="tpu_custom_call" | custom-call | tf_op jit(solution)/shard_map/fetch_roots/pallas_call | solution.py:109
  24.7 0.7 pair_sum.3
  25.4 0.2 select_reduce_fusion.1.owner_ref
  25.6 4.1 %collective-permute-done.1 = bf16[96,8,256]{2,1,0:T(8,128)(2,1)S(1)} collective-permute-done((bf16[96,8,256]{2,1,0:T(8,128)(2,1)S(1)}, bf16[96,8,256]{2,1,0:T(8,128)(2,1)S(1)}, u32[]{:S(2)}, u32[]{:S(2)}) %collective-permute-start.1) | collective-permute-done | bytes 393248 | tf_op jit(solution)/shard_map/ppermute | solution.py:304
  29.6 0.1 add.46
  29.7 0.0 copy-start
  29.8 15.1 %all_to_all.20.parts_ref = bf16[4,24,8,256]{3,2,1,0:T(8,128)(2,1)S(1)} all-to-all(bf16[4,24,8,256]{3,2,1,0:T(8,128)(2,1)S(1)} %bitcast.13), channel_id=1, replica_groups=mesh['xh'=4,'xl'=2,'core'=2,'y'=8,'z'=8] {'xh'}, dimensions={0} | all-to-all | bytes 786432 | tf_op jit(solution)/shard_map/all_to_all | solution.py:316
  44.9 0.6 sum_to_owner.1
  45.5 26.8 %all_to_all.21.own_ref = bf16[64,8,256]{2,1,0:T(8,128)(2,1)S(1)} all-to-all(bf16[64,8,256]{2,1,0:T(8,128)(2,1)S(1)} %sum_to_owner.1), channel_id=1, replica_groups=mesh['xh'=4,'xl'=2,'core'=2,'y'=8,'z'=8] {'y','z'}, dimensions={0} | all-to-all | bytes 524288 | tf_op jit(solution)/shard_map/all_to_all | solution.py:320
  72.3 5.4 %collective-permute-start.2 = (bf16[64,8,256]{2,1,0:T(8,128)(2,1)S(1)}, bf16[64,8,256]{2,1,0:T(8,128)(2,1)S(1)}, u32[]{:S(2)}, u32[]{:S(2)}) collective-permute-start(bf16[64,8,256]{2,1,0:T(8,128)(2,1)S(1)} %all_to_all.21.own_ref), channel_id=1, source_target_pairs={{0,64},{64,0},{1,65},{65,1},{2,66},{66,2},{3,67},{67,3},{4,68},{68... | collective-permute-start | bytes 786440 | tf_op jit(solution)/shard_map/ppermute | solution.py:321
  77.7 0.3 own_product.1
  78.0 0.8 collective-permute-done.2.other_ref
  78.9 1.1 precondition.1
  79.9 17.2 %all_to_all.22.rows_ref = bf16[64,8,256]{2,1,0:T(8,128)(2,1)S(1)} all-to-all(bf16[64,8,256]{2,1,0:T(8,128)(2,1)S(1)} %precondition.1), channel_id=1, replica_groups=mesh['xh'=4,'xl'=2,'core'=2,'y'=8,'z'=8] {'y','z'}, dimensions={0} | all-to-all | bytes 524288 | tf_op jit(solution)/shard_map/all_to_all | solution.py:324
  97.1 0.7 split_columns.1
  97.8 10.6 %all_to_all.23.pieces_ref = bf16[8,6,8,128]{3,2,1,0:T(8,128)(2,1)S(1)} all-to-all(bf16[8,6,8,128]{3,2,1,0:T(8,128)(2,1)S(1)} %split_columns.1), channel_id=1, replica_groups=mesh['xh'=4,'xl'=2,'core'=2,'y'=8,'z'=8] {'xh','xl'}, dimensions={0} | all-to-all | bytes 196608 | tf_op jit(solution)/shard_map/all_to_all | solution.py:326
  108.4 0.0 copy-done
  108.4 1.1 update.1
  (5 shorter events, 0.0 us)
Async XLA Ops:
  0.0 18.6 %copy-start.1 = (s32[192]{0:T(256)S(1)}, s32[192]{0:T(256)}, u32[]{:S(2)}) copy-start(s32[192]{0:T(256)} %param.11) | copy-start | bytes 2308
  0.0 18.6 %copy-start.2 = (s32[192]{0:T(256)S(1)}, s32[192]{0:T(256)}, u32[]{:S(2)}) copy-start(s32[192]{0:T(256)} %param.12) | copy-start | bytes 2308
  1.3 18.0 %collective-permute-start = (bf16[192,8,256]{2,1,0:T(8,128)(2,1)S(1)}, bf16[192,8,256]{2,1,0:T(8,128)(2,1)S(1)}, u32[]{:S(2)}, u32[]{:S(2)}) collective-permute-start(bf16[192,8,256]{2,1,0:T(8,128)(2,1)S(1)} %column_half.2), channel_id=1, source_target_pairs={{0,64},{64,0},{1,65},{65,1},{2,66},{66,2},{3,67},{67,3},{4,68},{68... | collective-permute-start | bytes 2359304 | tf_op jit(solution)/shard_map/ppermute | solution.py:287
  19.9 9.7 %collective-permute-start.1 = (bf16[96,8,256]{2,1,0:T(8,128)(2,1)S(1)}, bf16[96,8,256]{2,1,0:T(8,128)(2,1)S(1)}, u32[]{:S(2)}, u32[]{:S(2)}) collective-permute-start(bf16[96,8,256]{2,1,0:T(8,128)(2,1)S(1)} %pair_sum.2), channel_id=1, source_target_pairs={{0,128},{64,960},{128,0},{192,320},{256,384},{320,192},{384,256},{... | collective-permute-start | bytes 1179656 | tf_op jit(solution)/shard_map/ppermute | solution.py:304
  29.7 78.7 %copy-start = (f32[192,8,32]{0,2,1:T(8,128)S(1)}, f32[192,8,32]{0,2,1:T(8,128)}, u32[]{:S(2)}) copy-start(f32[192,8,32]{0,2,1:T(8,128)} %param.15) | copy-start | bytes 589828
  72.3 6.6 %collective-permute-start.2 = (bf16[64,8,256]{2,1,0:T(8,128)(2,1)S(1)}, bf16[64,8,256]{2,1,0:T(8,128)(2,1)S(1)}, u32[]{:S(2)}, u32[]{:S(2)}) collective-permute-start(bf16[64,8,256]{2,1,0:T(8,128)(2,1)S(1)} %all_to_all.21.own_ref), channel_id=1, source_target_pairs={{0,64},{64,0},{1,65},{65,1},{2,66},{66,2},{3,67},{67,3},{4,68},{68... | collective-permute-start | bytes 786440 | tf_op jit(solution)/shard_map/ppermute | solution.py:321

commit v10 on v9

--- a/solution.py
+++ b/solution.py
@@ -258,10 +258,25 @@
     return jnp.transpose(flipped, (2, 0, 1))
 
 
-def neighbour(place):
-    x, core = place // 2, place % 2
-    step = 1 if (x + core) % 2 == 0 else -1
-    return (x + step) % 8 * 2 + core
+def partner(stage, x, core):
+    y = (x - core) % 8
+    y = (y ^ 1, y ^ 2, 7 - y)[stage]
+    return (y + core) % 8
+
+
+def partners(stage):
+    return [(x * 2 + c, partner(stage, x, c) * 2 + c) for x in range(8) for c in range(2)]
+
+
+def plane_orders():
+    table = []
+    for x in range(8):
+        for core in range(2):
+            planes = [x]
+            for stage in (2, 1, 0):
+                planes = planes + [partner(stage, p, core) for p in planes]
+            table.append(planes)
+    return table
 
 
 def on_device(partial_grads, block_owner, block_slot, left_roots, right_roots, momentum):
@@ -270,7 +285,6 @@
     fsdp = ("y", "z")
     owner_count = lax.axis_size(fsdp)
     planes = lax.axis_size(along_x)
-    pairs = lax.axis_size("xh")
     cores = lax.axis_size("core")
     most = left_roots.shape[0]
     blocks, rows, width = partial_grads.shape[1:]
@@ -278,7 +292,6 @@
     half = width // cores
     core = lax.axis_index("core")
     plane = lax.axis_index(along_x).astype(jnp.uint32)
-    parity = lax.axis_index("xl").astype(jnp.uint32)
     me = lax.axis_index(fsdp)
 
     swap = [(i, 1 - i) for i in range(cores)]
@@ -293,7 +306,10 @@
     rank = jnp.sum((entry[None, :] < entry[:, None]).astype(jnp.uint32), axis=1)
     block_plane = rank % planes
     turn = rank // planes
-    spot = ((block_plane + parity) % 2 * pairs + block_plane // 2) * each + turn
+    own_order = jnp.asarray(plane_orders(), jnp.uint32)[lax.axis_index(rep)]
+    step = lax.iota(jnp.uint32, planes)
+    at = jnp.sum(jnp.where(own_order[None, :] == block_plane[:, None], step[None, :], 0), axis=1)
+    spot = at * each + turn
     order = lax.iota(jnp.uint32, blocks)
     block_at = jnp.sum(jnp.where(spot[None, :] == order[:, None], order[None, :], 0), axis=1)
     block_at = block_at.astype(jnp.int32)
@@ -301,7 +317,7 @@
 
     away, rank, block_at = lax.optimization_barrier((away, rank, block_at))
     keep = pair_sum(block_at, own, other, 0, blocks // 2)
-    met = lax.ppermute(away, rep, [(i, neighbour(i)) for i in range(planes * cores)])
+    met = lax.ppermute(away, rep, partners(0))
     place = (rank % planes * each + rank // planes).astype(jnp.int32)
     turns = lax.broadcasted_iota(jnp.uint32, (each, blocks), 0)
     turn_is = rank[None] == turns * planes + plane
@@ -313,9 +329,14 @@
         (met, keep, left_root, right_root, my_owner, place)
     )
 
-    parts = lax.all_to_all(
-        (keep + met).reshape(pairs, each, rows, half), "xh", split_axis=0, concat_axis=0, tiled=True
-    )
+    quarter, eighth = blocks // 4, blocks // 8
+    away = keep[quarter:] + met[quarter:]
+    met_next = lax.ppermute(away, rep, partners(1))
+    keep = keep[:quarter] + met[:quarter]
+    away = keep[eighth:] + met_next[eighth:]
+    met_last = lax.ppermute(away, rep, partners(2))
+    keep = keep[:eighth] + met_next[:eighth]
+    parts = jnp.stack([keep, met_last])
     to_owner = sum_to_owner(my_owner, parts, owner_count)
     grad_half = lax.all_to_all(to_owner, fsdp, split_axis=0, concat_axis=0, tiled=True)
     other_half = lax.ppermute(grad_half, "core", swap)

time: 111 us -> 115 us (1.036)
  the two profiles are of different devices: /device:TPU:1 before, /device:TPU:2 now
where the time goes in v10:
time: 115 us; the launch traced here: 114 us
  blocking collectives  61.9 us (54%)
  starting transfers between devices  22.9 us (20%)
  waiting for transfers between devices  17.4 us (15%)
  Pallas kernels  9.69 us (8%)
  other arithmetic  1.4 us (1%)
    all_to_all x1, blocking collectives, on_device(): lax.all_to_all(to_owner, fsdp, split_axis=0, concat_axis=0, tiled=True)  29.3 us
    all_to_all x1, blocking collectives, on_device(): lax.all_to_all(grafted, fsdp, split_axis=0, concat_axis=0, tiled=True)  19.1 us
    ppermute x1, starting transfers between devices, on_device(): met = lax.ppermute(away, rep, partners(0))  15.1 us
    all_to_all x1, blocking collectives, on_device(): lax.all_to_all(pieces, along_x, split_axis=0, concat_axis=0, tiled=True)  13.6 us
    ppermute x1, waiting for transfers between devices, on_device(): met_last = lax.ppermute(away, rep, partners(2))  7.59 us
    ppermute x1, waiting for transfers between devices, on_device(): met_next = lax.ppermute(away, rep, partners(1))  6.63 us
    pallas_call x2, Pallas kernels, column_half(): pl.pallas_call(column_half_kernel, out_shape=jax.ShapeDtypeStruct((blocks...  2.53 us
  transfers between devices with their start and end apart: 5, of which 4 were waited for; matrix products, arithmetic and copies ran while one was open for 2% of the time, Pallas kernels for 4%

profile of v10, /device:TPU:2, one launch (start us, length us, event | category | flops | bytes accessed | tf_op | source)
XLA Modules:
  0.0 114.2 jit_solution(5778578646346900656)
XLA Ops:
  0.0 0.0 copy-start.1
  0.0 0.0 copy-start.2
  0.0 1.3 %column_half.2 = bf16[192,8,256]{2,1,0:T(8,128)(2,1)S(1)} custom-call(s32[1]{0:T(128)} %bitcast.1.side_ref, bf16[192,8,512]{2,1,0:T(8,128)(2,1)} %bitcast.15), custom_call_target="tpu_custom_call" | custom-call | tf_op jit(solution)/shard_map/column_half/pallas_call | solution.py:37
  1.3 1.9 %collective-permute-start = (bf16[192,8,256]{2,1,0:T(8,128)(2,1)S(1)}, bf16[192,8,256]{2,1,0:T(8,128)(2,1)S(1)}, u32[]{:S(2)}, u32[]{:S(2)}) collective-permute-start(bf16[192,8,256]{2,1,0:T(8,128)(2,1)S(1)} %column_half.2), channel_id=1, source_target_pairs={{0,64},{64,0},{1,65},{65,1},{2,66},{66,2},{3,67},{67,3},{4,68},{68... | collective-permute-start | bytes 2359304 | tf_op jit(solution)/shard_map/ppermute | solution.py:300
  3.2 1.3 %column_half.3.own_ref = bf16[192,8,256]{2,1,0:T(8,128)(2,1)S(1)} custom-call(s32[1]{0:T(128)} %bitcast.3.side_ref, bf16[192,8,512]{2,1,0:T(8,128)(2,1)} %bitcast.16), custom_call_target="tpu_custom_call" | custom-call | tf_op jit(solution)/shard_map/column_half/pallas_call | solution.py:37
  4.5 0.0 copy-done.1
  4.5 0.0 copy-done.2
  4.5 0.2 convert_reduce_fusion
  4.7 0.7 dynamic-slice_bitcast_fusion
  5.4 0.1 select_reduce_fusion.2
  5.5 0.1 select_reduce_fusion
  5.7 0.0 collective-permute-done.other_ref
  5.7 0.7 pair_sum.2
  6.3 15.1 %collective-permute-start.1 = (bf16[96,8,256]{2,1,0:T(8,128)(2,1)S(1)}, bf16[96,8,256]{2,1,0:T(8,128)(2,1)S(1)}, u32[]{:S(2)}, u32[]{:S(2)}) collective-permute-start(bf16[96,8,256]{2,1,0:T(8,128)(2,1)S(1)} %pair_sum.2), channel_id=1, source_target_pairs={{0,128},{64,960},{128,0},{192,320},{256,384},{320,192},{384,256},{... | collective-permute-start | bytes 1179656 | tf_op jit(solution)/shard_map/ppermute | solution.py:320
  21.4 0.7 fusion.1
  22.1 2.2 %fetch_roots.1 = (bf16[512,512]{1,0:T(8,128)(2,1)S(1)}, bf16[512,512]{1,0:T(8,128)(2,1)S(1)}) custom-call(s32[1]{0:T(128)} %bitcast.4.slot_ref, s32[1]{0:T(128)} %bitcast.5.core_ref, bf16[6,512,512]{2,1,0:T(8,128)(2,1)} %left_table.1, bf16[6,512,512]{2,1,0:T(8,128)(2,1)} %right_table.1), custom_call_target="tpu_custom_call" | custom-call | tf_op jit(solution)/shard_map/fetch_roots/pallas_call | solution.py:109
  24.3 0.7 pair_sum.3
  25.0 0.2 select_reduce_fusion.1.owner_ref
  25.2 2.0 %collective-permute-done.1 = bf16[96,8,256]{2,1,0:T(8,128)(2,1)S(1)} collective-permute-done((bf16[96,8,256]{2,1,0:T(8,128)(2,1)S(1)}, bf16[96,8,256]{2,1,0:T(8,128)(2,1)S(1)}, u32[]{:S(2)}, u32[]{:S(2)}) %collective-permute-start.1) | collective-permute-done | bytes 393248 | tf_op jit(solution)/shard_map/ppermute | solution.py:320
  27.2 1.9 %collective-permute-start.2 = (bf16[48,8,256]{2,1,0:T(8,128)(2,1)S(1)}, bf16[48,8,256]{2,1,0:T(8,128)(2,1)S(1)}, u32[]{:S(2)}, u32[]{:S(2)}) collective-permute-start(bf16[48,8,256]{2,1,0:T(8,128)(2,1)S(1)} %get-tuple-element.41), channel_id=1, source_target_pairs={{0,256},{64,832},{128,384},{192,448},{256,0},{320,576},{384,128},{... | collective-permute-start | bytes 589832 | tf_op jit(solution)/shard_map/ppermute | solution.py:334
  29.1 6.6 %collective-permute-done.2 = bf16[48,8,256]{2,1,0:T(8,128)(2,1)S(1)} collective-permute-done((bf16[48,8,256]{2,1,0:T(8,128)(2,1)S(1)}, bf16[48,8,256]{2,1,0:T(8,128)(2,1)S(1)}, u32[]{:S(2)}, u32[]{:S(2)}) %collective-permute-start.2) | collective-permute-done | bytes 196640 | tf_op jit(solution)/shard_map/ppermute | solution.py:334
  35.8 0.0 copy-start
  35.8 2.1 %collective-permute-start.3 = (bf16[24,8,256]{2,1,0:T(8,128)(2,1)S(1)}, bf16[24,8,256]{2,1,0:T(8,128)(2,1)S(1)}, u32[]{:S(2)}, u32[]{:S(2)}) collective-permute-start(bf16[24,8,256]{2,1,0:T(8,128)(2,1)S(1)} %get-tuple-element.43), channel_id=1, source_target_pairs={{0,896},{64,192},{128,768},{192,64},{256,640},{320,960},{384,512},... | collective-permute-start | bytes 294920 | tf_op jit(solution)/shard_map/ppermute | solution.py:337
  37.9 7.6 %collective-permute-done.3 = bf16[24,8,256]{2,1,0:T(8,128)(2,1)S(1)} collective-permute-done((bf16[24,8,256]{2,1,0:T(8,128)(2,1)S(1)}, bf16[24,8,256]{2,1,0:T(8,128)(2,1)S(1)}, u32[]{:S(2)}, u32[]{:S(2)}) %collective-permute-start.3) | collective-permute-done | bytes 98336 | tf_op jit(solution)/shard_map/ppermute | solution.py:337
  45.5 0.6 sum_to_owner.1
  46.1 29.3 %all_to_all.15.own_ref = bf16[64,8,256]{2,1,0:T(8,128)(2,1)S(1)} all-to-all(bf16[64,8,256]{2,1,0:T(8,128)(2,1)S(1)} %sum_to_owner.1), channel_id=1, replica_groups=mesh['xh'=4,'xl'=2,'core'=2,'y'=8,'z'=8] {'y','z'}, dimensions={0} | all-to-all | bytes 524288 | tf_op jit(solution)/shard_map/all_to_all | solution.py:341
  75.4 1.9 %collective-permute-start.4 = (bf16[64,8,256]{2,1,0:T(8,128)(2,1)S(1)}, bf16[64,8,256]{2,1,0:T(8,128)(2,1)S(1)}, u32[]{:S(2)}, u32[]{:S(2)}) collective-permute-start(bf16[64,8,256]{2,1,0:T(8,128)(2,1)S(1)} %all_to_all.15.own_ref), channel_id=1, source_target_pairs={{0,64},{64,0},{1,65},{65,1},{2,66},{66,2},{3,67},{67,3},{4,68},{68... | collective-permute-start | bytes 786440 | tf_op jit(solution)/shard_map/ppermute | solution.py:342
  77.3 0.3 own_product.1
  77.6 1.2 %collective-permute-done.4.other_ref = bf16[64,8,256]{2,1,0:T(8,128)(2,1)S(1)} collective-permute-done((bf16[64,8,256]{2,1,0:T(8,128)(2,1)S(1)}, bf16[64,8,256]{2,1,0:T(8,128)(2,1)S(1)}, u32[]{:S(2)}, u32[]{:S(2)}) %collective-permute-start.4) | collective-permute-done | bytes 262176 | tf_op jit(solution)/shard_map/ppermute | solution.py:342
  78.8 1.1 precondition.1
  79.9 19.1 %all_to_all.16.rows_ref = bf16[64,8,256]{2,1,0:T(8,128)(2,1)S(1)} all-to-all(bf16[64,8,256]{2,1,0:T(8,128)(2,1)S(1)} %precondition.1), channel_id=1, replica_groups=mesh['xh'=4,'xl'=2,'core'=2,'y'=8,'z'=8] {'y','z'}, dimensions={0} | all-to-all | bytes 524288 | tf_op jit(solution)/shard_map/all_to_all | solution.py:345
  98.9 0.7 split_columns.1
  99.6 13.6 %all_to_all.17.pieces_ref = bf16[8,6,8,128]{3,2,1,0:T(8,128)(2,1)S(1)} all-to-all(bf16[8,6,8,128]{3,2,1,0:T(8,128)(2,1)S(1)} %split_columns.1), channel_id=1, replica_groups=mesh['xh'=4,'xl'=2,'core'=2,'y'=8,'z'=8] {'xh','xl'}, dimensions={0} | all-to-all | bytes 196608 | tf_op jit(solution)/shard_map/all_to_all | solution.py:347
  113.2 0.0 copy-done
  113.2 1.1 update.1
  (9 shorter events, 0.1 us)
Async XLA Ops:
  0.0 4.5 %copy-start.1 = (s32[192]{0:T(256)S(1)}, s32[192]{0:T(256)}, u32[]{:S(2)}) copy-start(s32[192]{0:T(256)} %param.10) | copy-start | bytes 2308
  0.0 4.5 %copy-start.2 = (s32[192]{0:T(256)S(1)}, s32[192]{0:T(256)}, u32[]{:S(2)}) copy-start(s32[192]{0:T(256)} %param.11) | copy-start | bytes 2308
  1.3 4.4 %collective-permute-start = (bf16[192,8,256]{2,1,0:T(8,128)(2,1)S(1)}, bf16[192,8,256]{2,1,0:T(8,128)(2,1)S(1)}, u32[]{:S(2)}, u32[]{:S(2)}) collective-permute-start(bf16[192,8,256]{2,1,0:T(8,128)(2,1)S(1)} %column_half.2), channel_id=1, source_target_pairs={{0,64},{64,0},{1,65},{65,1},{2,66},{66,2},{3,67},{67,3},{4,68},{68... | collective-permute-start | bytes 2359304 | tf_op jit(solution)/shard_map/ppermute | solution.py:300
  6.3 20.8 %collective-permute-start.1 = (bf16[96,8,256]{2,1,0:T(8,128)(2,1)S(1)}, bf16[96,8,256]{2,1,0:T(8,128)(2,1)S(1)}, u32[]{:S(2)}, u32[]{:S(2)}) collective-permute-start(bf16[96,8,256]{2,1,0:T(8,128)(2,1)S(1)} %pair_sum.2), channel_id=1, source_target_pairs={{0,128},{64,960},{128,0},{192,320},{256,384},{320,192},{384,256},{... | collective-permute-start | bytes 1179656 | tf_op jit(solution)/shard_map/ppermute | solution.py:320
  27.2 8.6 %collective-permute-start.2 = (bf16[48,8,256]{2,1,0:T(8,128)(2,1)S(1)}, bf16[48,8,256]{2,1,0:T(8,128)(2,1)S(1)}, u32[]{:S(2)}, u32[]{:S(2)}) collective-permute-start(bf16[48,8,256]{2,1,0:T(8,128)(2,1)S(1)} %get-tuple-element.41), channel_id=1, source_target_pairs={{0,256},{64,832},{128,384},{192,448},{256,0},{320,576},{384,128},{... | collective-permute-start | bytes 589832 | tf_op jit(solution)/shard_map/ppermute | solution.py:334
  35.8 77.4 %copy-start = (f32[192,8,32]{0,2,1:T(8,128)S(1)}, f32[192,8,32]{0,2,1:T(8,128)}, u32[]{:S(2)}) copy-start(f32[192,8,32]{0,2,1:T(8,128)} %param.14) | copy-start | bytes 589828
  35.8 9.7 %collective-permute-start.3 = (bf16[24,8,256]{2,1,0:T(8,128)(2,1)S(1)}, bf16[24,8,256]{2,1,0:T(8,128)(2,1)S(1)}, u32[]{:S(2)}, u32[]{:S(2)}) collective-permute-start(bf16[24,8,256]{2,1,0:T(8,128)(2,1)S(1)} %get-tuple-element.43), channel_id=1, source_target_pairs={{0,896},{64,192},{128,768},{192,64},{256,640},{320,960},{384,512},... | collective-permute-start | bytes 294920 | tf_op jit(solution)/shard_map/ppermute | solution.py:337
  75.4 3.4 %collective-permute-start.4 = (bf16[64,8,256]{2,1,0:T(8,128)(2,1)S(1)}, bf16[64,8,256]{2,1,0:T(8,128)(2,1)S(1)}, u32[]{:S(2)}, u32[]{:S(2)}) collective-permute-start(bf16[64,8,256]{2,1,0:T(8,128)(2,1)S(1)} %all_to_all.15.own_ref), channel_id=1, source_target_pairs={{0,64},{64,0},{1,65},{65,1},{2,66},{66,2},{3,67},{67,3},{4,68},{68... | collective-permute-start | bytes 786440 | tf_op jit(solution)/shard_map/ppermute | solution.py:342

commit v11 on v9

--- a/solution.py
+++ b/solution.py
@@ -164,11 +164,20 @@
     product, squares = half_product(core_ref, other_ref, right_ref, True)
     right_prod = (product_ref[...] + product).astype(jnp.bfloat16)
     grad_squares = squares_ref[:, :1] + squares
-    precond = jnp.dot(left_ref[...], right_prod, preferred_element_type=jnp.float32)
-    precond_squares = jnp.sum(precond * precond, keepdims=True)
+    count = 128
+    precond_squares = jnp.zeros((1, 1), jnp.float32)
+    kept = []
+    for start in range(0, size, count):
+        precond = jnp.dot(
+            left_ref[start : start + count, :], right_prod, preferred_element_type=jnp.float32
+        )
+        precond_squares += jnp.sum(precond * precond, keepdims=True)
+        kept.append(precond[:, :half])
     scale = jnp.sqrt(grad_squares / area) / jnp.sqrt(precond_squares / area + 1e-06)
-    grafted = (precond[:, :half] * scale).astype(out_ref.dtype)
-    out_ref[...] = grafted.reshape(out_ref.shape)
+    rows = out_ref.shape[1]
+    for i, part in enumerate(kept):
+        grafted = (part * scale).astype(out_ref.dtype)
+        out_ref[i * count // rows : (i + 1) * count // rows] = grafted.reshape(-1, rows, half)
 
 
 def precondition(core, product, squares, other, left_root, right_root):

time: 111 us -> 111 us (level)
  no operation moved by 1% of the time
where the time goes in v11:
time: 111 us; the launch traced here: 109 us
  blocking collectives  69.7 us (63%)
  starting transfers between devices  23.4 us (21%)
  Pallas kernels  9.68 us (9%)
  waiting for transfers between devices  5.11 us (5%)
  other arithmetic  1.33 us (1%)
    all_to_all x1, blocking collectives, on_device(): lax.all_to_all(to_owner, fsdp, split_axis=0, concat_axis=0, tiled=True)  26.8 us
    all_to_all x1, blocking collectives, on_device(): lax.all_to_all(grafted, fsdp, split_axis=0, concat_axis=0, tiled=True)  17.2 us
    ppermute x1, starting transfers between devices, on_device(): other = lax.ppermute(away, 'core', swap)  16.1 us
    all_to_all x1, blocking collectives, on_device(): lax.all_to_all((keep + met).reshape(pairs, each, rows, half), 'xh', split...  15.1 us
    all_to_all x1, blocking collectives, on_device(): lax.all_to_all(pieces, along_x, split_axis=0, concat_axis=0, tiled=True)  10.5 us
    ppermute x1, starting transfers between devices, on_device(): other_half = lax.ppermute(grad_half, 'core', swap)  5.4 us
    ppermute x1, waiting for transfers between devices, on_device(): lax.ppermute(away, rep, [(i, neighbour(i)) for i in range(planes * cores)])  4.06 us
    pallas_call x2, Pallas kernels, column_half(): pl.pallas_call(column_half_kernel, out_shape=jax.ShapeDtypeStruct((blocks...  2.53 us
  transfers between devices with their start and end apart: 3, of which 3 were waited for; matrix products, arithmetic and copies ran while one was open for 1% of the time, Pallas kernels for 4%

profile of v11, /device:TPU:1, one launch (start us, length us, event | category | flops | bytes accessed | tf_op | source)
XLA Modules:
  0.0 109.4 jit_solution(5766671695456429239)
XLA Ops:
  0.0 0.0 copy-start.1
  0.0 0.0 copy-start.2
  0.0 1.3 %column_half.2 = bf16[192,8,256]{2,1,0:T(8,128)(2,1)S(1)} custom-call(s32[1]{0:T(128)} %bitcast.side_ref, bf16[192,8,512]{2,1,0:T(8,128)(2,1)} %bitcast.11), custom_call_target="tpu_custom_call" | custom-call | tf_op jit(solution)/shard_map/column_half/pallas_call | solution.py:37
  1.3 16.1 %collective-permute-start = (bf16[192,8,256]{2,1,0:T(8,128)(2,1)S(1)}, bf16[192,8,256]{2,1,0:T(8,128)(2,1)S(1)}, u32[]{:S(2)}, u32[]{:S(2)}) collective-permute-start(bf16[192,8,256]{2,1,0:T(8,128)(2,1)S(1)} %column_half.2), channel_id=1, source_target_pairs={{0,64},{64,0},{1,65},{65,1},{2,66},{66,2},{3,67},{67,3},{4,68},{68... | collective-permute-start | bytes 2359304 | tf_op jit(solution)/shard_map/ppermute | solution.py:296
  17.4 1.3 %column_half.3.own_ref = bf16[192,8,256]{2,1,0:T(8,128)(2,1)S(1)} custom-call(s32[1]{0:T(128)} %bitcast.2.side_ref, bf16[192,8,512]{2,1,0:T(8,128)(2,1)} %bitcast.12), custom_call_target="tpu_custom_call" | custom-call | tf_op jit(solution)/shard_map/column_half/pallas_call | solution.py:37
  18.6 0.0 copy-done.1
  18.6 0.0 copy-done.2
  18.7 0.2 convert_reduce_fusion
  18.9 0.1 select_reduce_fusion
  19.0 0.2 collective-permute-done.other_ref
  19.2 0.7 pair_sum.2
  19.9 1.9 %collective-permute-start.1 = (bf16[96,8,256]{2,1,0:T(8,128)(2,1)S(1)}, bf16[96,8,256]{2,1,0:T(8,128)(2,1)S(1)}, u32[]{:S(2)}, u32[]{:S(2)}) collective-permute-start(bf16[96,8,256]{2,1,0:T(8,128)(2,1)S(1)} %pair_sum.2), channel_id=1, source_target_pairs={{0,128},{64,960},{128,0},{192,320},{256,384},{320,192},{384,256},{... | collective-permute-start | bytes 1179656 | tf_op jit(solution)/shard_map/ppermute | solution.py:313
  21.8 0.7 fusion.3
  22.6 2.2 %fetch_roots.1 = (bf16[512,512]{1,0:T(8,128)(2,1)S(1)}, bf16[512,512]{1,0:T(8,128)(2,1)S(1)}) custom-call(s32[1]{0:T(128)} %bitcast.3.slot_ref, s32[1]{0:T(128)} %bitcast.4.core_ref, bf16[6,512,512]{2,1,0:T(8,128)(2,1)} %left_table.1, bf16[6,512,512]{2,1,0:T(8,128)(2,1)} %right_table.1), custom_call_target="tpu_custom_call" | custom-call | tf_op jit(solution)/shard_map/fetch_roots/pallas_call | solution.py:109
  24.7 0.7 pair_sum.3
  25.4 0.2 select_reduce_fusion.1.owner_ref
  25.6 4.1 %collective-permute-done.1 = bf16[96,8,256]{2,1,0:T(8,128)(2,1)S(1)} collective-permute-done((bf16[96,8,256]{2,1,0:T(8,128)(2,1)S(1)}, bf16[96,8,256]{2,1,0:T(8,128)(2,1)S(1)}, u32[]{:S(2)}, u32[]{:S(2)}) %collective-permute-start.1) | collective-permute-done | bytes 393248 | tf_op jit(solution)/shard_map/ppermute | solution.py:313
  29.6 0.1 add.46
  29.7 0.0 copy-start
  29.8 15.1 %all_to_all.20.parts_ref = bf16[4,24,8,256]{3,2,1,0:T(8,128)(2,1)S(1)} all-to-all(bf16[4,24,8,256]{3,2,1,0:T(8,128)(2,1)S(1)} %bitcast.13), channel_id=1, replica_groups=mesh['xh'=4,'xl'=2,'core'=2,'y'=8,'z'=8] {'xh'}, dimensions={0} | all-to-all | bytes 786432 | tf_op jit(solution)/shard_map/all_to_all | solution.py:325
  44.9 0.6 sum_to_owner.1
  45.5 26.8 %all_to_all.21.own_ref = bf16[64,8,256]{2,1,0:T(8,128)(2,1)S(1)} all-to-all(bf16[64,8,256]{2,1,0:T(8,128)(2,1)S(1)} %sum_to_owner.1), channel_id=1, replica_groups=mesh['xh'=4,'xl'=2,'core'=2,'y'=8,'z'=8] {'y','z'}, dimensions={0} | all-to-all | bytes 524288 | tf_op jit(solution)/shard_map/all_to_all | solution.py:329
  72.3 5.4 %collective-permute-start.2 = (bf16[64,8,256]{2,1,0:T(8,128)(2,1)S(1)}, bf16[64,8,256]{2,1,0:T(8,128)(2,1)S(1)}, u32[]{:S(2)}, u32[]{:S(2)}) collective-permute-start(bf16[64,8,256]{2,1,0:T(8,128)(2,1)S(1)} %all_to_all.21.own_ref), channel_id=1, source_target_pairs={{0,64},{64,0},{1,65},{65,1},{2,66},{66,2},{3,67},{67,3},{4,68},{68... | collective-permute-start | bytes 786440 | tf_op jit(solution)/shard_map/ppermute | solution.py:330
  77.7 0.3 own_product.1
  78.0 0.8 collective-permute-done.2.other_ref
  78.9 1.0 precondition.1
  79.9 17.2 %all_to_all.22.rows_ref = bf16[64,8,256]{2,1,0:T(8,128)(2,1)S(1)} all-to-all(bf16[64,8,256]{2,1,0:T(8,128)(2,1)S(1)} %precondition.1), channel_id=1, replica_groups=mesh['xh'=4,'xl'=2,'core'=2,'y'=8,'z'=8] {'y','z'}, dimensions={0} | all-to-all | bytes 524288 | tf_op jit(solution)/shard_map/all_to_all | solution.py:333
  97.1 0.7 split_columns.1
  97.8 10.5 %all_to_all.23.pieces_ref = bf16[8,6,8,128]{3,2,1,0:T(8,128)(2,1)S(1)} all-to-all(bf16[8,6,8,128]{3,2,1,0:T(8,128)(2,1)S(1)} %split_columns.1), channel_id=1, replica_groups=mesh['xh'=4,'xl'=2,'core'=2,'y'=8,'z'=8] {'xh','xl'}, dimensions={0} | all-to-all | bytes 196608 | tf_op jit(solution)/shard_map/all_to_all | solution.py:335
  108.3 0.0 copy-done
  108.3 1.1 update.1
  (5 shorter events, 0.0 us)
Async XLA Ops:
  0.0 18.6 %copy-start.1 = (s32[192]{0:T(256)S(1)}, s32[192]{0:T(256)}, u32[]{:S(2)}) copy-start(s32[192]{0:T(256)} %param.11) | copy-start | bytes 2308
  0.0 18.6 %copy-start.2 = (s32[192]{0:T(256)S(1)}, s32[192]{0:T(256)}, u32[]{:S(2)}) copy-start(s32[192]{0:T(256)} %param.12) | copy-start | bytes 2308
  1.3 18.0 %collective-permute-start = (bf16[192,8,256]{2,1,0:T(8,128)(2,1)S(1)}, bf16[192,8,256]{2,1,0:T(8,128)(2,1)S(1)}, u32[]{:S(2)}, u32[]{:S(2)}) collective-permute-start(bf16[192,8,256]{2,1,0:T(8,128)(2,1)S(1)} %column_half.2), channel_id=1, source_target_pairs={{0,64},{64,0},{1,65},{65,1},{2,66},{66,2},{3,67},{67,3},{4,68},{68... | collective-permute-start | bytes 2359304 | tf_op jit(solution)/shard_map/ppermute | solution.py:296
  19.9 9.7 %collective-permute-start.1 = (bf16[96,8,256]{2,1,0:T(8,128)(2,1)S(1)}, bf16[96,8,256]{2,1,0:T(8,128)(2,1)S(1)}, u32[]{:S(2)}, u32[]{:S(2)}) collective-permute-start(bf16[96,8,256]{2,1,0:T(8,128)(2,1)S(1)} %pair_sum.2), channel_id=1, source_target_pairs={{0,128},{64,960},{128,0},{192,320},{256,384},{320,192},{384,256},{... | collective-permute-start | bytes 1179656 | tf_op jit(solution)/shard_map/ppermute | solution.py:313
  29.7 78.6 %copy-start = (f32[192,8,32]{0,2,1:T(8,128)S(1)}, f32[192,8,32]{0,2,1:T(8,128)}, u32[]{:S(2)}) copy-start(f32[192,8,32]{0,2,1:T(8,128)} %param.15) | copy-start | bytes 589828
  72.3 6.6 %collective-permute-start.2 = (bf16[64,8,256]{2,1,0:T(8,128)(2,1)S(1)}, bf16[64,8,256]{2,1,0:T(8,128)(2,1)S(1)}, u32[]{:S(2)}, u32[]{:S(2)}) collective-permute-start(bf16[64,8,256]{2,1,0:T(8,128)(2,1)S(1)} %all_to_all.21.own_ref), channel_id=1, source_target_pairs={{0,64},{64,0},{1,65},{65,1},{2,66},{66,2},{3,67},{67,3},{4,68},{68... | collective-permute-start | bytes 786440 | tf_op jit(solution)/shard_map/ppermute | solution.py:330
